TPU v7x, 128 devices: a whole 4x4x4 slice. The times are simulated.
128 devices in a mesh: row: 8 (over x, z_lo), col: 16 (over y, z_hi, core).
Axes of the slice: x: 4, y: 4, z: 4 (z_hi: 2, z_lo: 2; z = z_hi * 2 + z_lo), core: 2. Of those that a mesh axis runs over, the one named last changes fastest.
Arguments:
- alignment_embedding: bfloat16 [64, 1536, 256], P('col', 'row'), may hold values from -6 to 6
- couplings_embedding: bfloat16 [1536, 1536, 128], P('row', 'col'), may hold values from -6 to 6
- alignment_availability: int32 [64, 1536], P('col', 'row'), may hold values 0 or 1
- amino_availability: int32 [1536], replicated, may hold values 0 or 1
- alignment_scaling_vector: float32 [256], replicated, may hold values from 0.3 to 3
- attention_joint_matrix: bfloat16 [256, 1024], replicated, may hold values from -0.375 to 0.375
- attention_final_matrix: bfloat16 [256, 256], replicated, may hold values from -0.375 to 0.375
- coupling_scaling_vector: float32 [128], replicated, may hold values from 0.3 to 3
- coupling_logit_matrix: bfloat16 [128, 8], replicated, may hold values from -8 to 8
- tensor_scaling_vector: float32 [256], replicated, may hold values from 0.3 to 3
- first_factor_matrix: bfloat16 [256, 32], replicated, may hold values from -0.375 to 0.375
- second_factor_matrix: bfloat16 [256, 32], replicated, may hold values from -0.375 to 0.375
- tensor_projection_matrix: bfloat16 [1024, 128], replicated, may hold values from -1.5 to 1.5
- tensor_offset_vector: float32 [128], replicated, may hold values from -3 to 3
Outputs:
- alignment_refreshed: bfloat16 [64, 1536, 256], P('col', 'row')
- couplings_refreshed: bfloat16 [1536, 1536, 128], P('row', 'col')
All inputs are finite; a program needn't handle non-finite values. No bound on the sum of `alignment_availability` on one device may be relied on, other than what follows from the above.
Results may differ from a plain program's by a relative error of at most 0.027.
The roundings to bfloat16 on the way count: a program that leaves them out, or rounds other values in their place, can miss the bound.
Values may be sent and summed in bfloat16 or wider, within the bound.
No kernel may reach another device: no remote copies, remote signals or barrier semaphores. Data moves between devices by JAX's collectives and lax.ppermute only.
A program may use at most 128 MiB of HBM per device.

v0:
```python
import math

import jax
import jax.numpy as jnp
from jax import lax
from jax.sharding import PartitionSpec as P


def standardize_lines(x, gain):
    x = x.astype(jnp.float32)
    mean = jnp.mean(x, axis=-1, keepdims=True)
    var = jnp.mean((x - mean) ** 2, axis=-1, keepdims=True)
    return (x - mean) * lax.rsqrt(var + 1e-05) * gain


def on_device(
    alignment_embedding,
    couplings_embedding,
    alignment_availability,
    amino_availability,
    alignment_scaling_vector,
    attention_joint_matrix,
    attention_final_matrix,
    coupling_scaling_vector,
    coupling_logit_matrix,
    tensor_scaling_vector,
    first_factor_matrix,
    second_factor_matrix,
    tensor_projection_matrix,
    tensor_offset_vector,
):
    aligned_lines, incoming_alignment, embedding_depth = alignment_embedding.shape
    col_block = couplings_embedding.shape[1]
    heads = coupling_logit_matrix.shape[1]
    head_dim = embedding_depth // heads
    outer_dim = first_factor_matrix.shape[1]
    alignment_standardized = standardize_lines(
        alignment_embedding, alignment_scaling_vector
    ).astype(jnp.bfloat16)
    availability_halfprec = alignment_availability.astype(jnp.bfloat16)
    joint_projected = jnp.dot(
        alignment_standardized, attention_joint_matrix, preferred_element_type=jnp.float32
    )
    front = joint_projected[:, :, :embedding_depth]
    sigmoid_switch = jax.nn.sigmoid(joint_projected[:, :, 3 * embedding_depth :])
    key_loc = joint_projected[:, :, embedding_depth : 2 * embedding_depth].astype(jnp.bfloat16)
    value_loc = joint_projected[:, :, 2 * embedding_depth : 3 * embedding_depth].astype(
        jnp.bfloat16
    )
    key_all, value_all, mask_all = (
        lax.all_gather(key_loc, "row", axis=1, tiled=True),
        lax.all_gather(value_loc, "row", axis=1, tiled=True),
        lax.all_gather(availability_halfprec, "row", axis=1, tiled=True),
    )
    asking_vectors = (front * head_dim ** (-0.5)).astype(jnp.bfloat16)
    znorm = standardize_lines(couplings_embedding, coupling_scaling_vector).astype(jnp.bfloat16)
    bias_tile = jnp.einsum(
        "ijc,ch->hij", znorm, coupling_logit_matrix, preferred_element_type=jnp.float32
    ).astype(jnp.bfloat16)
    bias_full = lax.all_gather(bias_tile, "col", axis=2, tiled=True).astype(jnp.float32)
    total_res = key_all.shape[1]

    def attend(items):
        q_seq, k_seq, content_vectors, m_seq = items
        q_seq = q_seq.reshape(incoming_alignment, heads, head_dim)
        k_seq = k_seq.reshape(total_res, heads, head_dim)
        content_vectors = content_vectors.reshape(total_res, heads, head_dim)
        scores = jnp.einsum("ihd,jhd->hij", q_seq, k_seq, preferred_element_type=jnp.float32)
        scores = (
            scores + bias_full + ((m_seq.astype(jnp.float32) - 1.0) * 1000000000.0)[None, None, :]
        )
        attention_probabilities = jax.nn.softmax(scores, axis=-1).astype(jnp.bfloat16)
        return jnp.einsum(
            "ktc,cko->tko",
            attention_probabilities,
            content_vectors,
            preferred_element_type=jnp.float32,
        ).reshape(incoming_alignment, embedding_depth)

    attended = lax.map(attend, (asking_vectors, key_all, value_all, mask_all))
    switched_attention = (sigmoid_switch * attended).astype(jnp.bfloat16)
    increment_tensor = jnp.dot(
        switched_attention, attention_final_matrix, preferred_element_type=jnp.float32
    )
    alignment_refreshed = (alignment_embedding.astype(jnp.float32) + increment_tensor).astype(
        jnp.bfloat16
    )
    tensor_standardized = standardize_lines(alignment_refreshed, tensor_scaling_vector).astype(
        jnp.bfloat16
    )
    availability_indicators = alignment_availability.astype(jnp.float32)[:, :, None]
    first_factor = (
        jnp.dot(tensor_standardized, first_factor_matrix, preferred_element_type=jnp.float32)
        * availability_indicators
    ).astype(jnp.bfloat16)
    second_factor = (
        jnp.dot(tensor_standardized, second_factor_matrix, preferred_element_type=jnp.float32)
        * availability_indicators
    ).astype(jnp.bfloat16)
    col_index = lax.axis_index("col")
    col_start = col_index * col_block
    right_wide = lax.all_gather(second_factor, "row", axis=1, tiled=True)
    left_all, right_all = (
        lax.all_gather(first_factor, "col", axis=0, tiled=True),
        lax.all_gather(right_wide, "col", axis=0, tiled=True),
    )
    right_mine = lax.dynamic_slice_in_dim(right_all, col_start, col_block, 1)
    seq_total = left_all.shape[0]
    block = math.gcd(incoming_alignment, 32)

    def outer_rows(index):
        left_block = lax.dynamic_slice_in_dim(left_all, index * block, block, 1)
        outer = (
            jnp.einsum("sia,sjb->ijab", left_block, right_mine, preferred_element_type=jnp.float32)
            / seq_total
        )
        outer = outer.astype(jnp.bfloat16).reshape(block, col_block, outer_dim * outer_dim)
        return (
            jnp.dot(outer, tensor_projection_matrix, preferred_element_type=jnp.float32)
            + tensor_offset_vector
        )

    pair_update = lax.map(outer_rows, jnp.arange(incoming_alignment // block)).reshape(
        incoming_alignment, col_block, -1
    )
    keep_rows = lax.dynamic_slice_in_dim(
        amino_availability, lax.axis_index("row") * incoming_alignment, incoming_alignment, 0
    ).astype(jnp.float32)
    keep_cols = lax.dynamic_slice_in_dim(amino_availability, col_start, col_block, 0).astype(
        jnp.float32
    )
    couplings_refreshed = (
        couplings_embedding.astype(jnp.float32)
        + pair_update * keep_rows[:, None, None] * keep_cols[None, :, None]
    )
    return (alignment_refreshed, couplings_refreshed.astype(jnp.bfloat16))


def solution(mesh):
    placed = (
        P("col", "row", None),
        P("row", "col", None),
        P("col", "row"),
        P(),
        P(),
        P(),
        P(),
        P(),
        P(),
        P(),
        P(),
        P(),
        P(),
        P(),
    )
    return jax.shard_map(
        on_device,
        mesh=mesh,
        in_specs=placed,
        out_specs=(P("col", "row", None), P("row", "col", None)),
        check_vma=False,
    )
```

profile of v0, /device:TPU:1, one launch (start us, length us, event | category | flops | bytes accessed | tf_op | source)
XLA Modules:
  0.0 615.0 jit_solution(2831379461477434238)
XLA Ops:
  11.6 7.7 %fusion.11 = f32[192,96]{1,0:T(8,128)S(1)} fusion(bf16[192,96,128]{2,1,0:T(8,128)(2,1)} %param.19, f32[192,96]{1,0:T(8,128)S(1)} %broadcast_multiply_fusion), kind=kLoop, calls=%fused_computation.24 | loop fusion | flops 9418752 | bytes 4866048 | tf_op jit(solution)/shard_map/reduce_sum | solution.py:12
  19.3 7.9 %fusion.22 = bf16[8,192,96]{2,0,1:T(8,128)(2,1)S(1)} fusion(bf16[192,96,128]{2,1,0:T(8,128)(2,1)S(1)} %copy-done.3, f32[128]{0:T(128)S(1)} %copy-done.15, f32[192,96]{1,0:T(8,128)S(1)} %add_rsqrt_fusion, f32[192,96]{1,0:T(8,128)S(1)} %broadcast_multiply_fusion, bf16[128,8]{0,1:T(8,128)(2,1)S(1)} %copy-done.13), kind=kOutput, calls=%fused_computation.34 | convolution fusion | flops 49692672 | bytes 5163520 | tf_op jit(solution)/shard_map/ijc,ch->hij/dot_general | solution.py:57
  33.2 21.1 %all-gather = bf16[8,192,4]{1,2,0:T(4,128)(2,1)S(1)} all-gather(bf16[1,192,4]{1,2,0:T(4,128)(2,1)S(1)} %get-tuple-element.219), channel_id=1, replica_groups=mesh['row'=8,'col'=16] {'row'}, dimensions={0}, use_global_device_ids=true | all-gather | bytes 13824 | tf_op jit(solution)/shard_map/all_gather | solution.py:53
  56.4 40.2 %all-gather.10.cloned.1.call-done = bf16[8,192,1536]{1,0,2:T(8,128)(2,1)} async-done(((bf16[8,192,96]{1,0,2:T(8,128)(2,1)}), bf16[8,192,1536]{1,0,2:T(8,128)(2,1)}) %all-gather.10.cloned.1.call-update) | async-done | bytes 4718608 | tf_op jit(solution)/shard_map/all_gather | solution.py:60
  96.6 10.0 %copy.51 = f32[8,192,1536]{2,1,0:T(8,128)} copy(bf16[8,192,1536]{1,0,2:T(8,128)(2,1)} %all-gather.10.cloned.1.call-done) | data formatting | bytes 14155776 | tf_op jit(solution)/shard_map/while | solution.py:80
  106.6 59.5 %all-gather.6.cloned.1.call-done = bf16[4,1536,256]{2,1,0:T(8,128)(2,1)} async-done(((bf16[4,192,256]{2,1,0:T(8,128)(2,1)}), bf16[4,1536,256]{2,1,0:T(8,128)(2,1)}) %all-gather.6.cloned.1.call-update) | async-done | bytes 3145744 | tf_op jit(solution)/shard_map/all_gather | solution.py:52
  166.2 73.5 %all-gather.8.cloned.1.call-done = bf16[4,1536,256]{2,1,0:T(8,128)(2,1)} async-done(((bf16[4,192,256]{2,1,0:T(8,128)(2,1)}), bf16[4,1536,256]{2,1,0:T(8,128)(2,1)}) %all-gather.8.cloned.1.call-update) | async-done | bytes 3145744 | tf_op jit(solution)/shard_map/all_gather | solution.py:51
  239.7 96.8 %while.22 = (s32[]{:T(128)}, f32[4,192,256]{2,1,0:T(8,128)}, bf16[4,1536,256]{2,1,0:T(8,128)(2,1)}, bf16[4,192,256]{2,1,0:T(8,128)(2,1)}, bf16[4,1536,256]{2,1,0...) while((s32[]{:T(128)}, f32[4,192,256]{2,1,0:T(8,128)}, ...), condition=%wide.region_7.8_spmd, body=%wide.region_4.7_spmd.sunk | while | flops 318514176 | bytes 84864632 | solution.py:80
  253.3 9.8 %fusion.85 = f32[8,32,192]{2,1,0:T(8,128)S(1)} fusion(bf16[1536,8,32]{0,2,1:T(8,128)(2,1)S(1)} %bitcast.99, f32[8,192]{1,0:T(8,128)S(1)} %fusion.84, f32[8,192,1536]{2,1,0:T(8,128)} %copy-done.2), kind=kOutput, calls=%fused_computation.12.clone.1 | convolution fusion | flops 158075904 | bytes 10426368 | tf_op jit(solution)/shard_map/while/body/eval_jaxpr/ktc,cko->tko/dot_general | solution.py:73
  277.5 9.8 %fusion.85 = f32[8,32,192]{2,1,0:T(8,128)S(1)} fusion(bf16[1536,8,32]{0,2,1:T(8,128)(2,1)S(1)} %bitcast.99, f32[8,192]{1,0:T(8,128)S(1)} %fusion.84, f32[8,192,1536]{2,1,0:T(8,128)} %copy-done.2), kind=kOutput, calls=%fused_computation.12.clone.1 | convolution fusion | flops 158075904 | bytes 10426368 | tf_op jit(solution)/shard_map/while/body/eval_jaxpr/ktc,cko->tko/dot_general | solution.py:73
  301.7 9.8 %fusion.85 = f32[8,32,192]{2,1,0:T(8,128)S(1)} fusion(bf16[1536,8,32]{0,2,1:T(8,128)(2,1)S(1)} %bitcast.99, f32[8,192]{1,0:T(8,128)S(1)} %fusion.84, f32[8,192,1536]{2,1,0:T(8,128)} %copy-done.2), kind=kOutput, calls=%fused_computation.12.clone.1 | convolution fusion | flops 158075904 | bytes 10426368 | tf_op jit(solution)/shard_map/while/body/eval_jaxpr/ktc,cko->tko/dot_general | solution.py:73
  325.9 9.8 %fusion.85 = f32[8,32,192]{2,1,0:T(8,128)S(1)} fusion(bf16[1536,8,32]{0,2,1:T(8,128)(2,1)S(1)} %bitcast.99, f32[8,192]{1,0:T(8,128)S(1)} %fusion.84, f32[8,192,1536]{2,1,0:T(8,128)} %copy-done.2), kind=kOutput, calls=%fused_computation.12.clone.1 | convolution fusion | flops 158075904 | bytes 10426368 | tf_op jit(solution)/shard_map/while/body/eval_jaxpr/ktc,cko->tko/dot_general | solution.py:73
  339.4 33.1 %all_gather.26 = bf16[4,1536,32]{2,0,1:T(4,128)(2,1)S(1)} all-gather(bf16[4,192,32]{2,0,1:T(4,128)(2,1)S(1)} %copy.53), channel_id=1, replica_groups=mesh['row'=8,'col'=16] {'row'}, dimensions={1}, use_global_device_ids=true | all-gather | bytes 442368 | tf_op jit(solution)/shard_map/all_gather | solution.py:102
  376.4 33.2 %all_gather.25 = bf16[64,192,32]{1,2,0:T(8,128)(2,1)S(1)} all-gather(bf16[4,192,32]{1,2,0:T(8,128)(2,1)S(1)} %fusion.25), channel_id=1, replica_groups=mesh['row'=8,'col'=16] {'col'}, dimensions={0}, use_global_device_ids=true | all-gather | bytes 835584 | tf_op jit(solution)/shard_map/all_gather | solution.py:104
  411.9 34.0 %all-gather.12.cloned.1.call-done = bf16[64,1536,32]{1,2,0:T(8,128)(2,1)} async-done(((bf16[4,1536,32]{1,2,0:T(8,128)(2,1)}), bf16[64,1536,32]{1,2,0:T(8,128)(2,1)}) %all-gather.12.cloned.1.call-update) | async-done | bytes 6291472 | tf_op jit(solution)/shard_map/all_gather | solution.py:105
  447.5 146.2 %while.23 = (s32[]{:T(128)}, f32[6,32,96,128]{3,2,1,0:T(8,128)}, s32[6]{0:T(128)S(1)}, bf16[64,192,32]{0,2,1:T(8,128)(2,1)S(1)}, bf16[64,96,32]{1,0,2:T(8,128)(2...) while((s32[]{:T(128)}, f32[6,32,96,128]{3,2,1,0:T(8,128)}, ...), condition=%wide.region_11.12_spmd, body=%wide.region_10.11_spmd.sunk | while | flops 1214644224 | bytes 29885612 | solution.py:123
  454.4 10.6 %copy.79 = bf16[32,96,32,32]{1,3,2,0:T(8,128)(2,1)} copy(bf16[32,96,32,32]{1,2,3,0:T(8,128)(2,1)} %fusion.90) | data formatting | bytes 12582912 | tf_op jit(solution)/shard_map/while/body/eval_jaxpr/convert_element_type | solution.py:117
  465.0 6.9 %bitcast_dynamic-update-slice_fusion.2 = f32[6,32,96,128]{3,2,1,0:T(8,128)} fusion(f32[6,32,96,128]{3,2,1,0:T(8,128)} %get-tuple-element.350, s32[]{:T(128)} %get-tuple-element.349, bf16[32,96,1024]{1,2,0:T(8,128)(2,1)} %bitcast.97, f32[128]{0:T(128)S(1)} %get-tuple-element.366, bf16[1024,128]{1,0:T(8,128)(2,1)S(1)} %get-tuple-element.365), kind=kOutput, calls=%fused_computation.2.clone.1 | convolution fusion | flops 805699584 | bytes 10224640 | tf_op jit(solution)/shard_map/while/body/eval_jaxpr/dot_general | solution.py:119
  473.2 5.6 fusion.90
  478.8 10.6 %copy.79 = bf16[32,96,32,32]{1,3,2,0:T(8,128)(2,1)} copy(bf16[32,96,32,32]{1,2,3,0:T(8,128)(2,1)} %fusion.90) | data formatting | bytes 12582912 | tf_op jit(solution)/shard_map/while/body/eval_jaxpr/convert_element_type | solution.py:117
  489.4 6.9 %bitcast_dynamic-update-slice_fusion.2 = f32[6,32,96,128]{3,2,1,0:T(8,128)} fusion(f32[6,32,96,128]{3,2,1,0:T(8,128)} %get-tuple-element.350, s32[]{:T(128)} %get-tuple-element.349, bf16[32,96,1024]{1,2,0:T(8,128)(2,1)} %bitcast.97, f32[128]{0:T(128)S(1)} %get-tuple-element.366, bf16[1024,128]{1,0:T(8,128)(2,1)S(1)} %get-tuple-element.365), kind=kOutput, calls=%fused_computation.2.clone.1 | convolution fusion | flops 805699584 | bytes 10224640 | tf_op jit(solution)/shard_map/while/body/eval_jaxpr/dot_general | solution.py:119
  497.5 5.6 fusion.90
  503.1 10.6 %copy.79 = bf16[32,96,32,32]{1,3,2,0:T(8,128)(2,1)} copy(bf16[32,96,32,32]{1,2,3,0:T(8,128)(2,1)} %fusion.90) | data formatting | bytes 12582912 | tf_op jit(solution)/shard_map/while/body/eval_jaxpr/convert_element_type | solution.py:117
  513.7 6.9 %bitcast_dynamic-update-slice_fusion.2 = f32[6,32,96,128]{3,2,1,0:T(8,128)} fusion(f32[6,32,96,128]{3,2,1,0:T(8,128)} %get-tuple-element.350, s32[]{:T(128)} %get-tuple-element.349, bf16[32,96,1024]{1,2,0:T(8,128)(2,1)} %bitcast.97, f32[128]{0:T(128)S(1)} %get-tuple-element.366, bf16[1024,128]{1,0:T(8,128)(2,1)S(1)} %get-tuple-element.365), kind=kOutput, calls=%fused_computation.2.clone.1 | convolution fusion | flops 805699584 | bytes 10224640 | tf_op jit(solution)/shard_map/while/body/eval_jaxpr/dot_general | solution.py:119
  527.5 10.6 %copy.79 = bf16[32,96,32,32]{1,3,2,0:T(8,128)(2,1)} copy(bf16[32,96,32,32]{1,2,3,0:T(8,128)(2,1)} %fusion.90) | data formatting | bytes 12582912 | tf_op jit(solution)/shard_map/while/body/eval_jaxpr/convert_element_type | solution.py:117
  538.1 6.9 %bitcast_dynamic-update-slice_fusion.2 = f32[6,32,96,128]{3,2,1,0:T(8,128)} fusion(f32[6,32,96,128]{3,2,1,0:T(8,128)} %get-tuple-element.350, s32[]{:T(128)} %get-tuple-element.349, bf16[32,96,1024]{1,2,0:T(8,128)(2,1)} %bitcast.97, f32[128]{0:T(128)S(1)} %get-tuple-element.366, bf16[1024,128]{1,0:T(8,128)(2,1)S(1)} %get-tuple-element.365), kind=kOutput, calls=%fused_computation.2.clone.1 | convolution fusion | flops 805699584 | bytes 10224640 | tf_op jit(solution)/shard_map/while/body/eval_jaxpr/dot_general | solution.py:119
  551.8 10.6 %copy.79 = bf16[32,96,32,32]{1,3,2,0:T(8,128)(2,1)} copy(bf16[32,96,32,32]{1,2,3,0:T(8,128)(2,1)} %fusion.90) | data formatting | bytes 12582912 | tf_op jit(solution)/shard_map/while/body/eval_jaxpr/convert_element_type | solution.py:117
  562.4 6.9 %bitcast_dynamic-update-slice_fusion.2 = f32[6,32,96,128]{3,2,1,0:T(8,128)} fusion(f32[6,32,96,128]{3,2,1,0:T(8,128)} %get-tuple-element.350, s32[]{:T(128)} %get-tuple-element.349, bf16[32,96,1024]{1,2,0:T(8,128)(2,1)} %bitcast.97, f32[128]{0:T(128)S(1)} %get-tuple-element.366, bf16[1024,128]{1,0:T(8,128)(2,1)S(1)} %get-tuple-element.365), kind=kOutput, calls=%fused_computation.2.clone.1 | convolution fusion | flops 805699584 | bytes 10224640 | tf_op jit(solution)/shard_map/while/body/eval_jaxpr/dot_general | solution.py:119
  570.6 5.6 fusion.90
  576.2 10.6 %copy.79 = bf16[32,96,32,32]{1,3,2,0:T(8,128)(2,1)} copy(bf16[32,96,32,32]{1,2,3,0:T(8,128)(2,1)} %fusion.90) | data formatting | bytes 12582912 | tf_op jit(solution)/shard_map/while/body/eval_jaxpr/convert_element_type | solution.py:117
  586.8 7.0 %bitcast_dynamic-update-slice_fusion.2 = f32[6,32,96,128]{3,2,1,0:T(8,128)} fusion(f32[6,32,96,128]{3,2,1,0:T(8,128)} %get-tuple-element.350, s32[]{:T(128)} %get-tuple-element.349, bf16[32,96,1024]{1,2,0:T(8,128)(2,1)} %bitcast.97, f32[128]{0:T(128)S(1)} %get-tuple-element.366, bf16[1024,128]{1,0:T(8,128)(2,1)S(1)} %get-tuple-element.365), kind=kOutput, calls=%fused_computation.2.clone.1 | convolution fusion | flops 805699584 | bytes 10224640 | tf_op jit(solution)/shard_map/while/body/eval_jaxpr/dot_general | solution.py:119
  593.7 14.8 %fusion.14 = bf16[192,96,128]{2,1,0:T(8,128)(2,1)} fusion(bf16[192,96,128]{2,1,0:T(8,128)(2,1)} %param.19, f32[6,32,96,128]{3,2,1,0:T(8,128)} %get-tuple-element.129, f32[96]{0:T(128)S(1)} %dynamic-slice_convert_fusion.1, f32[192]{0:T(256)S(1)} %dynamic-slice_convert_fusion), kind=kLoop, calls=%fused_computation.27 | loop fusion | flops 11796480 | bytes 18875520 | tf_op jit(solution)/shard_map/convert_element_type | solution.py:136
  (125 shorter events, 100.7 us)
Async XLA Ops:
  7.2 22.0 %copy-start = (bf16[256,1024]{1,0:T(8,128)(2,1)S(1)}, bf16[256,1024]{1,0:T(8,128)(2,1)}, u32[]{:S(2)}) copy-start(bf16[256,1024]{1,0:T(8,128)(2,1)} %param.23) | copy-start | bytes 1572868
  7.2 12.1 %copy-start.15 = (f32[128]{0:T(128)S(1)}, f32[128]{0:T(128)}, u32[]{:S(2)}) copy-start(f32[128]{0:T(128)} %param.25) | copy-start | bytes 1540
  7.2 12.1 %copy-start.13 = (bf16[128,8]{0,1:T(8,128)(2,1)S(1)}, bf16[128,8]{0,1:T(8,128)(2,1)}, u32[]{:S(2)}) copy-start(bf16[128,8]{0,1:T(8,128)(2,1)} %param.26) | copy-start | bytes 6148
  7.2 89.4 %all-gather.10.cloned.1.call-start = ((), (), s32[]{:S(2)}) async-start(), calls=%async_computation.2 | async-start | bytes 6684672 | tf_op jit(solution)/shard_map/all_gather | solution.py:60
  7.2 12.0 %copy-start.3 = (bf16[192,96,128]{2,1,0:T(8,128)(2,1)S(1)}, bf16[192,96,128]{2,1,0:T(8,128)(2,1)}, u32[]{:S(2)}) copy-start(bf16[192,96,128]{2,1,0:T(8,128)(2,1)} %param.19) | copy-start | bytes 14155780
  11.5 17.0 %copy-start.5 = (bf16[4,192,256]{2,1,0:T(8,128)(2,1)S(1)}, bf16[4,192,256]{2,1,0:T(8,128)(2,1)}, u32[]{:S(2)}) copy-start(bf16[4,192,256]{2,1,0:T(8,128)(2,1)} %param.18) | copy-start | bytes 1179652
  11.5 17.6 %copy-start.9 = (f32[256]{0:T(256)S(1)}, f32[256]{0:T(256)}, u32[]{:S(2)}) copy-start(f32[256]{0:T(256)} %param.22) | copy-start | bytes 3076
  19.3 13.9 %copy-start.8 = (s32[4,192]{1,0:T(4,128)S(1)}, s32[4,192]{1,0:T(4,128)}, u32[]{:S(2)}) copy-start(s32[4,192]{1,0:T(4,128)} %param.20) | copy-start | bytes 9220
  28.5 137.7 %all-gather.6.cloned.1.call-start = ((), (), s32[]{:S(2)}) async-start(), calls=%async_computation | async-start | bytes 3538944 | tf_op jit(solution)/shard_map/all_gather | solution.py:52
  32.4 207.3 %all-gather.8.cloned.1.call-start = ((), (), s32[]{:S(2)}) async-start(), calls=%async_computation.1 | async-start | bytes 3538944 | tf_op jit(solution)/shard_map/all_gather | solution.py:51
  33.1 412.7 %all-gather.12.cloned.1.call-start = ((), (), s32[]{:S(2)}) async-start(), calls=%async_computation.3 | async-start | bytes 6684672 | tf_op jit(solution)/shard_map/all_gather | solution.py:105
  239.7 96.8 %copy-start.10 = (bf16[256,256]{1,0:T(8,128)(2,1)S(1)}, bf16[256,256]{1,0:T(8,128)(2,1)}, u32[]{:S(2)}) copy-start(bf16[256,256]{1,0:T(8,128)(2,1)} %param.24) | copy-start | bytes 393220
  239.7 99.1 %copy-start.11 = (bf16[256,32]{0,1:T(8,128)(2,1)S(1)}, bf16[256,32]{0,1:T(8,128)(2,1)}, u32[]{:S(2)}) copy-start(bf16[256,32]{0,1:T(8,128)(2,1)} %param.29) | copy-start | bytes 49156
  239.7 99.1 %copy-start.14 = (f32[256]{0:T(256)S(1)}, f32[256]{0:T(256)}, u32[]{:S(2)}) copy-start(f32[256]{0:T(256)} %param.27) | copy-start | bytes 3076
  247.6 3.6 copy-start.2
  271.8 3.6 copy-start.2
  296.0 3.6 copy-start.2
  320.2 3.6 copy-start.2
  336.5 39.5 %copy-start.12 = (bf16[256,32]{0,1:T(8,128)(2,1)S(1)}, bf16[256,32]{0,1:T(8,128)(2,1)}, u32[]{:S(2)}) copy-start(bf16[256,32]{0,1:T(8,128)(2,1)} %param.28) | copy-start | bytes 49156
  336.5 111.0 %copy-start.4 = (bf16[1024,128]{1,0:T(8,128)(2,1)S(1)}, bf16[1024,128]{1,0:T(8,128)(2,1)}, u32[]{:S(2)}) copy-start(bf16[1024,128]{1,0:T(8,128)(2,1)} %param.30) | copy-start | bytes 786436
  336.5 111.0 %copy-start.7 = (f32[128]{0:T(128)S(1)}, f32[128]{0:T(128)}, u32[]{:S(2)}) copy-start(f32[128]{0:T(128)} %param.31) | copy-start | bytes 1540
  338.4 37.6 %copy-start.6 = (bf16[4,192,256]{2,1,0:T(8,128)(2,1)}, bf16[4,192,256]{2,1,0:T(8,128)(2,1)S(1)}, u32[]{:S(2)}) copy-start(bf16[4,192,256]{2,1,0:T(8,128)(2,1)S(1)} %get-tuple-element.223) | copy-start | bytes 1179652
  593.7 14.8 %copy-start.1 = (bf16[256,1024]{1,0:T(8,128)(2,1)S(1)}, bf16[256,1024]{1,0:T(8,128)(2,1)}, u32[]{:S(2)}) copy-start(bf16[256,1024]{1,0:T(8,128)(2,1)} %param.23) | copy-start | bytes 1572868
Sparse Core Ops, SparseCore 0:
  28.6 67.9 all-gather.9
  98.2 67.8 all-gather.5
  168.4 71.2 all-gather.7
  374.6 71.2 all-gather.11
where the time goes:
time: 617 us; the launch traced here: 615 us
  waiting for transfers between devices  208 us (34%)
  matrix products  148 us (24%)
  local copies, waits for them, and re-layouts  115 us (19%)
  blocking collectives  87.5 us (14%)
  other arithmetic  38.4 us (6%)
  between operations  14.1 us (2%)
    all_gather x1, waiting for transfers between devices, on_device(): lax.all_gather(key_loc, 'row', axis=1, tiled=True)  73.5 us
    convert_element_type x6, local copies, waits for them, and re-layouts, outer_rows(): outer.astype(jnp.bfloat16).reshape(block, col_block, outer_dim * outer_dim)  63.5 us
    all_gather x1, waiting for transfers between devices, on_device(): lax.all_gather(value_loc, 'row', axis=1, tiled=True)  59.5 us
    dot_general x6, matrix products, outer_rows(): jnp.dot(outer, tensor_projection_matrix, preferred_element_type=jnp.float32)  41.5 us
    all_gather x1, waiting for transfers between devices, on_device(): lax.all_gather(bias_tile, 'col', axis=2, tiled=True).astype(jnp.float32)  40.2 us
    dot_general x4, matrix products, attend(): jnp.einsum('ktc,cko->tko', attention_probabilities, content_vectors, pref...  39.1 us
    all_gather x1, waiting for transfers between devices, on_device(): lax.all_gather(right_wide, 'col', axis=0, tiled=True)  34 us
    dot_general x6, matrix products, outer_rows(): jnp.einsum('sia,sjb->ijab', left_block, right_mine, preferred_element_typ...  33.8 us
  transfers between devices with their start and end apart: 4, of which 4 were waited for; matrix products, arithmetic and copies ran while one was open for 3% of the time, Pallas kernels for 0%

commit v1 on v0

v1 whole, which is shorter than its diff:
```python
import jax
import jax.numpy as jnp
import numpy as np
from jax import lax
from jax.experimental import pallas as pl
from jax.experimental.pallas import tpu as pltpu
from jax.sharding import PartitionSpec as P

F32 = jnp.float32
BF16 = jnp.bfloat16
HEADS = 8
HEAD = 32
SEQS = 4
ROWS = 192
QUADS = 48
COLS = 96
EMB = 256
PAIR = 128
PEERS_ROW = 8
PEERS_COL = 16
TOTAL = 1536
VMEM_LIMIT = 56 * 1024 * 1024


def mm(a, b):
    return jnp.dot(a, b, preferred_element_type=F32)


def mm_nt(a, b):
    return lax.dot_general(a, b, (((1,), (1,)), ((), ())), preferred_element_type=F32)


def mm_tn(a, b):
    return lax.dot_general(a, b, (((0,), (0,)), ((), ())), preferred_element_type=F32)


def normalised(x, gain):
    mean = jnp.mean(x, axis=-1, keepdims=True)
    d = x - mean
    var = jnp.mean(d * d, axis=-1, keepdims=True)
    return (d * lax.rsqrt(var + 1e-05) * gain).astype(BF16)


def slot_of(shape):
    return (lax.broadcasted_iota(jnp.int32, shape, len(shape) - 1) // HEAD) % 4


def params(**kw):
    return pltpu.CompilerParams(vmem_limit_bytes=VMEM_LIMIT, **kw)


def project_kernel(x_ref, g_ref, w_ref, e_ref, p_ref, qkv_ref, gate_ref):
    slot = slot_of((ROWS, 4 * 128))
    plain = [normalised(x_ref[s].astype(F32), g_ref[...]) for s in range(SEQS)]
    moved = [mm(p_ref[...], n).astype(BF16) for n in plain]
    for part in range(4):
        rows = moved if part in (0, 3) else plain
        for m in range(2):
            w = mm(w_ref[:, part * EMB + m * 128 : part * EMB + (m + 1) * 128], e_ref[...]).astype(BF16)
            acc = mm(rows[0], w)
            for s in range(1, SEQS):
                acc = jnp.where(slot == s, mm(rows[s], w), acc)
            for u in range(4):
                t = acc[:, u * 128 : (u + 1) * 128]
                h = 4 * m + u
                if part == 0:
                    qkv_ref[h, 0] = (t * HEAD ** (-0.5)).astype(BF16)
                elif part == 3:
                    gate_ref[h] = jax.nn.sigmoid(t)
                else:
                    qkv_ref[h, part] = t.astype(BF16)


def project(x, gain, w, expand, perm):
    return pl.pallas_call(
        project_kernel,
        out_shape=(
            jax.ShapeDtypeStruct((HEADS, 3, ROWS, 128), BF16),
            jax.ShapeDtypeStruct((HEADS, ROWS, 128), F32),
        ),
        compiler_params=params(),
        name="project",
    )(x, gain, w, expand, perm)


def bias_kernel(z_ref, g_ref, a_ref, o_ref):
    acc = jnp.zeros((128, 4 * COLS), F32)
    for k in range(8):
        n = normalised(z_ref[768 * k : 768 * (k + 1)].astype(F32), g_ref[...])
        both = jnp.concatenate([n[:384], n[384:]], axis=1)
        acc += mm_nt(a_ref[:, 256 * k : 256 * (k + 1)], both)
    o_ref[...] = acc.astype(BF16).reshape(HEADS, 16, 4 * COLS)


def pair_bias(z, gain, a):
    return pl.pallas_call(
        bias_kernel,
        out_shape=jax.ShapeDtypeStruct((HEADS, QUADS, 4 * COLS), BF16),
        grid=(3,),
        in_specs=[
            pl.BlockSpec((6144, PAIR), lambda t: (t, 0)),
            pl.BlockSpec((1, PAIR), lambda t: (0, 0)),
            pl.BlockSpec((128, 2048), lambda t: (0, 0)),
        ],
        out_specs=pl.BlockSpec((HEADS, 16, 4 * COLS), lambda t: (0, t, 0)),
        compiler_params=params(),
        name="pair_bias",
    )(z, gain, a)


def attend_kernel(qkv_ref, b_ref, m_ref, o_ref, k_ext, v_ext, bias):
    step = pl.program_id(0)
    block = 2 * ROWS

    @pl.when(step == 0)
    def _():
        slot = slot_of((ROWS, 128))
        eye = (
            lax.broadcasted_iota(jnp.int32, (8, 128), 0) == lax.broadcasted_iota(jnp.int32, (8, 128), 1)
        ).astype(BF16)
        absent = ((m_ref[...].astype(F32) - 1.0) * 1000000000.0).astype(BF16)
        k_ext[:, 128:] = mm_tn(absent, eye).astype(BF16)
        for r in range(PEERS_ROW):
            rows = slice(r * ROWS, (r + 1) * ROWS)
            k_ext[rows, :128] = qkv_ref[r, 1]
            v = qkv_ref[r, 2].astype(F32)
            for s in range(SEQS):
                v_ext[s, rows, :128] = jnp.where(slot == s, v, 0.0).astype(BF16)
                v_ext[s, rows, 128:] = jnp.where(slot == s, 1.0, 0.0).astype(BF16)

    for a in range(2):
        for quad in range(4):
            got = [b_ref[4 * quad + k, a].astype(F32) for k in range(4)]
            for u in range(4):
                line = jnp.concatenate([g[:, COLS * u : COLS * (u + 1)] for g in got], axis=1)
                bias[a * ROWS + u * QUADS : a * ROWS + (u + 1) * QUADS, 384 * quad : 384 * (quad + 1)] = line

    q = jnp.concatenate([qkv_ref[2 * step, 0], qkv_ref[2 * step + 1, 0]], axis=0).astype(F32)
    slot = slot_of((block, 128))
    lane = lax.broadcasted_iota(jnp.int32, (block, 128), 1)

    def one(s, total):
        lhs = jnp.concatenate(
            [jnp.where(slot == s, q, 0.0).astype(BF16), jnp.where(lane == s, 1.0, 0.0).astype(BF16)],
            axis=1,
        )
        scores = mm_nt(lhs, k_ext[...]) + bias[...]
        top = jnp.max(scores, axis=1, keepdims=True)
        e = jnp.exp(scores - top).astype(BF16)
        return total + mm(e, v_ext[s])

    total = lax.fori_loop(0, SEQS, one, jnp.zeros((block, 256), F32))
    o_ref[...] = (total[:, :128] / total[:, 128:]).astype(BF16).reshape(2, ROWS, 128)


def attend(qkv, bias, present):
    return pl.pallas_call(
        attend_kernel,
        out_shape=jax.ShapeDtypeStruct((PEERS_ROW, ROWS, 128), BF16),
        grid=(PEERS_ROW // 2,),
        in_specs=[
            pl.BlockSpec((PEERS_ROW, 3, ROWS, 128), lambda t: (0, 0, 0, 0)),
            pl.BlockSpec((PEERS_COL, 2, QUADS, 4 * COLS), lambda t: (0, t, 0, 0)),
            pl.BlockSpec((8, TOTAL), lambda t: (0, 0)),
        ],
        out_specs=pl.BlockSpec((2, ROWS, 128), lambda t: (t, 0, 0)),
        scratch_shapes=[
            pltpu.VMEM((TOTAL, 256), BF16),
            pltpu.VMEM((SEQS, TOTAL, 256), BF16),
            pltpu.VMEM((2 * ROWS, TOTAL), F32),
        ],
        compiler_params=params(),
        name="attend",
    )(qkv, bias, present)


def finish_kernel(
    att_ref, gate_ref, x_ref, wf_ref, pinv_ref, g_ref, wl_ref, wr_ref, ac_ref, ar_ref, new_ref, left_ref, right_ref
):
    gated = jnp.concatenate(
        [(gate_ref[h] * att_ref[h].astype(F32)).astype(BF16) for h in range(HEADS)], axis=1
    )
    gated = mm(pinv_ref[...], gated)
    w = jnp.concatenate([wf_ref[HEAD * (k // 4) : HEAD * (k // 4 + 1)] for k in range(4 * HEADS)], axis=0)
    slot = slot_of((ROWS, 4 * EMB))
    slot_one = slot_of((ROWS, 128))
    left = jnp.zeros((ROWS, 128), F32)
    for s in range(SEQS):
        inc = mm(jnp.where(slot == s, gated, 0.0).astype(BF16), w)
        new = (x_ref[s].astype(F32) + inc).astype(BF16)
        new_ref[s] = new
        n = normalised(new.astype(F32), g_ref[...])
        left = jnp.where(slot_one == s, mm(n, wl_ref[...]), left)
        right = mm_nt(wr_ref[...], n) * ar_ref[s : s + 1]
        right_ref[0, HEAD * s : HEAD * (s + 1)] = right[:, :COLS].astype(BF16)
        right_ref[1, HEAD * s : HEAD * (s + 1)] = right[:, COLS:].astype(BF16)
    left_ref[...] = (left * ac_ref[...]).astype(BF16)


def finish(*args):
    return pl.pallas_call(
        finish_kernel,
        out_shape=(
            jax.ShapeDtypeStruct((SEQS, ROWS, EMB), BF16),
            jax.ShapeDtypeStruct((ROWS, 128), BF16),
            jax.ShapeDtypeStruct((2, 128, COLS), BF16),
        ),
        compiler_params=params(),
        name="finish",
    )(*args)


STEP = 8


def outer_kernel(l_ref, r_ref, w_ref, off_ref, ki_ref, kj_ref, z_ref, o_ref, l_all, r_all, rhs_r, obf):
    step = pl.program_id(0)

    @pl.when(step == 0)
    def _():
        for c in range(PEERS_COL):
            l_all[ROWS * c : ROWS * (c + 1)] = l_ref[c].astype(F32)
            r_all[128 * c : 128 * (c + 1), :COLS] = r_ref[c].astype(F32)
        r_all[:, COLS:] = jnp.zeros((PEERS_COL * 128, 128 - COLS), F32)
        for q in range(8):
            lines = [
                r_all[pl.ds(HEAD * s + 4 * q + b, PEERS_COL, stride=128), :] for b in range(4) for s in range(SEQS)
            ]
            turned = jnp.transpose(jnp.concatenate(lines, axis=0))
            rhs_r[COLS * q : COLS * (q + 1)] = turned[:COLS].astype(BF16)

    slot = slot_of((PEERS_COL, 128))
    tiles = []
    for k in range(STEP):
        m = l_all[pl.ds(step * STEP + k, PEERS_COL, stride=ROWS), :]
        rolled = [m] + [pltpu.roll(m, HEAD * d, 1) for d in range(1, 4)]
        tiles.append(
            jnp.concatenate(
                [
                    jnp.where(slot == b, rolled[(b - s) % 4], 0.0).astype(BF16)
                    for b in range(4)
                    for s in range(SEQS)
                ],
                axis=0,
            )
        )
    for k in range(0, STEP, 2):
        outer = mm(rhs_r[...], jnp.concatenate(tiles[k : k + 2], axis=1)).astype(BF16)
        for e in range(2):
            for q in range(8):
                obf[COLS * (k + e) : COLS * (k + e + 1), 128 * q : 128 * (q + 1)] = outer[
                    COLS * q : COLS * (q + 1), 128 * e : 128 * (e + 1)
                ]
    update = mm(obf[...], w_ref[...]) + off_ref[...]
    for k in range(STEP):
        keep = kj_ref[...] * ki_ref[step * STEP + k]
        o_ref[k] = (z_ref[k].astype(F32) + update[COLS * k : COLS * (k + 1)] * keep).astype(BF16)


def outer_update(left, right, w, offset, keep_i, keep_j, z):
    return pl.pallas_call(
        outer_kernel,
        out_shape=jax.ShapeDtypeStruct((ROWS, COLS, PAIR), BF16),
        grid=(ROWS // STEP,),
        in_specs=[
            pl.BlockSpec((PEERS_COL, ROWS, 128), lambda t: (0, 0, 0)),
            pl.BlockSpec((PEERS_COL, 128, COLS), lambda t: (0, 0, 0)),
            pl.BlockSpec((1024, PAIR), lambda t: (0, 0)),
            pl.BlockSpec((1, PAIR), lambda t: (0, 0)),
            pl.BlockSpec(memory_space=pltpu.SMEM),
            pl.BlockSpec((COLS, PAIR), lambda t: (0, 0)),
            pl.BlockSpec((STEP, COLS, PAIR), lambda t: (t, 0, 0)),
        ],
        out_specs=pl.BlockSpec((STEP, COLS, PAIR), lambda t: (t, 0, 0)),
        scratch_shapes=[
            pltpu.VMEM((PEERS_COL * ROWS, 128), F32),
            pltpu.VMEM((PEERS_COL * 128, 128), F32),
            pltpu.VMEM((8 * COLS, 256), BF16),
            pltpu.VMEM((STEP * COLS, 1024), BF16),
        ],
        compiler_params=params(),
        name="outer_update",
    )(left, right, w, offset, keep_i, keep_j, z)


def tables():
    expand = np.zeros((128, 4, 4, HEAD), np.float32)
    for u in range(4):
        for d in range(HEAD):
            expand[u * HEAD + d, u, :, d] = 1
    perm = np.zeros((ROWS, ROWS), np.float32)
    for i in range(ROWS):
        perm[(i % 4) * QUADS + i // 4, i] = 1
    return expand.reshape(128, 512), perm


def on_device(
    alignment_embedding,
    couplings_embedding,
    alignment_availability,
    amino_availability,
    alignment_scaling_vector,
    attention_joint_matrix,
    attention_final_matrix,
    coupling_scaling_vector,
    coupling_logit_matrix,
    tensor_scaling_vector,
    first_factor_matrix,
    second_factor_matrix,
    tensor_projection_matrix,
    tensor_offset_vector,
):
    expand, perm = tables()
    qkv, gate = project(
        alignment_embedding,
        alignment_scaling_vector[None],
        attention_joint_matrix,
        jnp.asarray(expand, BF16),
        jnp.asarray(perm, BF16),
    )
    qkv = lax.all_to_all(qkv, "row", 0, 0, tiled=True)
    spread = (
        jnp.eye(16, dtype=BF16)[None, :, :, None] * coupling_logit_matrix.T[:, None, None, :]
    ).reshape(HEADS * 16, 16 * PAIR)
    bias = pair_bias(
        couplings_embedding.reshape(ROWS * COLS, PAIR), coupling_scaling_vector[None], spread
    )
    bias = lax.all_to_all(bias, "row", 0, 0, tiled=True)
    bias = lax.all_gather(bias, "col", axis=0)
    present = jnp.pad(alignment_availability.astype(BF16), ((0, 4), (0, 0)))
    present_all = lax.all_gather(present, "row", axis=1, tiled=True)
    attended = attend(qkv, bias, present_all)
    attended = lax.all_to_all(attended, "row", 0, 0, tiled=True)
    present = alignment_availability.astype(F32)
    alignment_refreshed, left, right = finish(
        attended,
        gate,
        alignment_embedding,
        attention_final_matrix,
        jnp.asarray(perm.T, BF16),
        tensor_scaling_vector[None],
        jnp.tile(first_factor_matrix, (1, 4)),
        second_factor_matrix.T,
        jnp.repeat(present.T, HEAD, axis=1),
        present,
    )
    left = lax.all_gather(left, "col", axis=0)
    right = lax.all_gather(right, "row", axis=0, tiled=True)
    right = lax.all_to_all(right, "col", 0, 0, tiled=True)
    keep = amino_availability.astype(F32)
    keep_i = lax.dynamic_slice_in_dim(keep, lax.axis_index("row") * ROWS, ROWS)
    keep_j = lax.dynamic_slice_in_dim(keep, lax.axis_index("col") * COLS, COLS)
    projection = (tensor_projection_matrix.astype(F32) / 64).astype(BF16)
    projection = projection.reshape(HEAD, 8, 4, PAIR).transpose(1, 2, 0, 3).reshape(1024, PAIR)
    couplings_refreshed = outer_update(
        left,
        right,
        projection,
        tensor_offset_vector[None],
        keep_i,
        jnp.broadcast_to(keep_j[:, None], (COLS, PAIR)),
        couplings_embedding,
    )
    return alignment_refreshed, couplings_refreshed


def solution(mesh):
    placed = (P("col", "row", None), P("row", "col", None), P("col", "row")) + (P(),) * 11
    return jax.shard_map(
        on_device,
        mesh=mesh,
        in_specs=placed,
        out_specs=(P("col", "row", None), P("row", "col", None)),
        check_vma=False,
    )
```

time: 617 us -> 269 us (0.44)
  waiting for transfers between devices: 208 us -> 31.2 us
  matrix products: 148 us -> 0 us
  local copies, waits for them, and re-layouts: 115 us -> 8.07 us
  Pallas kernels: 0 us -> 95 us
  other arithmetic: 38.4 us -> 1.45 us
  starting transfers between devices: 0.16 us -> 19.9 us
  blocking collectives: 87.5 us -> 98.7 us
    all_gather x4 -> x1, waiting for transfers between devices: 207 us -> 26.4 us  [on_device(): bias = lax.all_gather(bias, 'col', axis=0)]
    dot_general x25 -> x0, matrix products: 148 us -> none  [the longest x6 41.5 us: outer_rows(): jnp.dot(outer, tensor_projection_matrix, preferred_element_type=jnp.float32)]
    pallas_call x0 -> x5, Pallas kernels: none -> 95 us  [the longest x1 44.5 us: outer_update(): pl.pallas_call(outer_kernel, out_shape=jax.ShapeDtypeStruct((ROWS, COLS,...]
    convert_element_type x8 -> x0, local copies, waits for them, and re-layouts: 64.8 us -> none  [the longest x6 63.5 us: outer_rows(): outer.astype(jnp.bfloat16).reshape(block, col_block, outer_dim * outer_dim)]
    while x11 -> x0, local copies, waits for them, and re-layouts: 27 us -> none
    all_to_all x0 -> x3, starting transfers between devices: none -> 19.9 us  [the longest x1 12.1 us: on_device(): right = lax.all_to_all(right, 'col', 0, 0, tiled=True)]
    convert_element_type x5 -> x4, other arithmetic: 18.3 us -> 0.66 us  [the longest x1 0.6 us: on_device(): present = alignment_availability.astype(F32)]
    dynamic_slice x27 -> x2, local copies, waits for them, and re-layouts: 17.1 us -> 0.71 us  [the longest x1 0.64 us: on_device(): keep_i = lax.dynamic_slice_in_dim(keep, lax.axis_index('row') * ROWS, ROWS)]
  transfers between devices with their start and end apart: 4 -> 4, of which waited for: 4 -> 2; matrix products, arithmetic and copies ran while one was open for 3% -> 2% of each run, Pallas kernels for 0% -> 2%
where the time goes in v1:
time: 269 us; the launch traced here: 268 us
  blocking collectives  98.7 us (37%)
  Pallas kernels  95 us (35%)
  waiting for transfers between devices  31.2 us (12%)
  starting transfers between devices  19.9 us (7%)
  between operations  14.1 us (5%)
  local copies, waits for them, and re-layouts  8.07 us (3%)
    pallas_call x1, Pallas kernels, outer_update(): pl.pallas_call(outer_kernel, out_shape=jax.ShapeDtypeStruct((ROWS, COLS,...  44.5 us
    all_gather x1, blocking collectives, on_device(): present_all = lax.all_gather(present, 'row', axis=1, tiled=True)  32.8 us
    pallas_call x1, Pallas kernels, attend(): pl.pallas_call(attend_kernel, out_shape=jax.ShapeDtypeStruct((PEERS_ROW,...  31.7 us
    all_gather x1, blocking collectives, on_device(): left = lax.all_gather(left, 'col', axis=0)  28.4 us
    all_gather x1, waiting for transfers between devices, on_device(): bias = lax.all_gather(bias, 'col', axis=0)  26.4 us
    all_gather x1, blocking collectives, on_device(): right = lax.all_gather(right, 'row', axis=0, tiled=True)  24.6 us
    all_to_all x1, blocking collectives, on_device(): bias = lax.all_to_all(bias, 'row', 0, 0, tiled=True)  12.8 us
    all_to_all x1, starting transfers between devices, on_device(): right = lax.all_to_all(right, 'col', 0, 0, tiled=True)  12.1 us
  transfers between devices with their start and end apart: 4, of which 2 were waited for; matrix products, arithmetic and copies ran while one was open for 2% of the time, Pallas kernels for 2%

profile of v1, /device:TPU:1, one launch (start us, length us, event | category | flops | bytes accessed | tf_op | source)
XLA Modules:
  0.0 268.5 jit_solution(7772505048725435319)
XLA Ops:
  7.2 0.0 all-gather.5.cloned.1.call-start
  7.2 0.8 broadcast_multiply_fusion
  8.0 0.9 copy.35
  9.0 8.2 %pair_bias.1 = bf16[8,48,384]{2,1,0:T(8,128)(2,1)} custom-call(bf16[18432,128]{1,0:T(8,128)(2,1)} %bitcast.29, f32[1,128]{1,0:T(1,128)} %bitcast.43, bf16[128,2048]{1,0:T(8,128)(2,1)} %bitcast.32), custom_call_target="tpu_custom_call" | custom-call | tf_op jit(solution)/shard_map/pair_bias/pallas_call | solution.py:96
  17.2 12.8 %all_to_all.20 = bf16[8,48,384]{2,1,0:T(8,128)(2,1)} all-to-all(bf16[8,48,384]{2,1,0:T(8,128)(2,1)} %pair_bias.1), channel_id=1, replica_groups=mesh['row'=8,'col'=16] {'row'}, dimensions={0} | all-to-all | bytes 589824 | tf_op jit(solution)/shard_map/all_to_all | solution.py:328
  30.0 0.0 all-gather.5.cloned.1.call-update
  30.0 6.0 %project.1 = (bf16[8,3,192,128]{3,2,1,0:T(8,128)(2,1)}, f32[8,192,128]{2,1,0:T(8,128)}) custom-call(bf16[4,192,256]{2,1,0:T(8,128)(2,1)} %x_ref.3, f32[1,256]{1,0:T(1,128)} %bitcast.42, bf16[256,1024]{1,0:T(8,128)(2,1)} %w_ref.1, bf16[128,512]{1,0:T(8,128)(2,1)} %constant.28.clone.e_ref, bf16[192,192]{1,0:T(8,128)(2,1)} %constant.29.clone.p_ref), custom_call_target="tpu_custom_call" | custom-call | tf_op jit(solution)/shard_map/project/pallas_call | solution.py:75
  36.0 3.7 %all-to-all-start = ((bf16[8,3,192,128]{3,2,1,0:T(8,128)(2,1)}), bf16[8,3,192,128]{3,2,1,0:T(8,128)(2,1)S(1)}, u32[]{:S(2)}, u32[]{:S(2)}) async-start(bf16[8,3,192,128]{3,2,1,0:T(8,128)(2,1)} %get-tuple-element.7), calls=%async_computation | async-start | bytes 2359296 | tf_op jit(solution)/shard_map/all_to_all | solution.py:321
  39.7 0.6 fusion.1
  40.3 32.8 %all-gather.2 = bf16[8,192,8]{1,2,0:T(8,128)(2,1)S(1)} all-gather(bf16[1,192,8]{1,2,0:T(8,128)(2,1)S(1)} %pad_bitcast_fusion), channel_id=1, replica_groups=mesh['row'=8,'col'=16] {'row'}, dimensions={0}, use_global_device_ids=true | all-gather | bytes 27648 | tf_op jit(solution)/shard_map/all_gather | solution.py:331
  73.2 0.7 reshape.41
  73.9 0.0 all-to-all-done.qkv_ref
  73.9 26.4 %all-gather.5.cloned.1.call-done = bf16[128,48,384]{2,1,0:T(8,128)(2,1)} async-done(((bf16[8,48,384]{2,1,0:T(8,128)(2,1)}), bf16[128,48,384]{2,1,0:T(8,128)(2,1)}) %all-gather.5.cloned.1.call-update) | async-done | bytes 4718608 | tf_op jit(solution)/shard_map/all_gather | solution.py:329
  100.2 31.7 %attend.1 = bf16[8,192,128]{2,1,0:T(8,128)(2,1)} custom-call(bf16[8,3,192,128]{3,2,1,0:T(8,128)(2,1)} %copy-done, bf16[16,8,48,384]{3,2,1,0:T(8,128)(2,1)} %bitcast.30, bf16[8,1536]{1,0:T(8,128)(2,1)} %bitcast.38), custom_call_target="tpu_custom_call" | custom-call | tf_op jit(solution)/shard_map/attend/pallas_call | solution.py:157
  131.9 4.0 %all-to-all-start.2 = ((bf16[8,192,128]{2,1,0:T(8,128)(2,1)}), bf16[8,192,128]{2,1,0:T(8,128)(2,1)S(1)}, u32[]{:S(2)}, u32[]{:S(2)}) async-start(bf16[8,192,128]{2,1,0:T(8,128)(2,1)} %attend.1), calls=%async_computation.2 | async-start | bytes 786432 | tf_op jit(solution)/shard_map/all_to_all | solution.py:333
  136.0 0.7 copy.29.ac_ref
  136.7 0.7 copy.28.wl_ref
  137.5 0.1 dynamic_slice.7
  137.5 0.6 dynamic_slice.6.ki_ref
  138.2 0.1 multiply_convert_fusion
  138.2 0.8 copy.31
  139.0 4.9 %all-to-all-done.2.att_ref = bf16[8,192,128]{2,1,0:T(8,128)(2,1)S(1)} async-done(((bf16[8,192,128]{2,1,0:T(8,128)(2,1)}), bf16[8,192,128]{2,1,0:T(8,128)(2,1)S(1)}, u32[]{:S(2)}, u32[]{:S(2)}) %all-to-all-start.2) | async-done | bytes 393248 | tf_op jit(solution)/shard_map/all_to_all | solution.py:333
  143.9 0.7 copy-done.1
  144.6 4.6 %finish.1 = (bf16[4,192,256]{2,1,0:T(8,128)(2,1)}, bf16[192,128]{1,0:T(8,128)(2,1)}, bf16[2,128,96]{2,1,0:T(8,128)(2,1)}) custom-call(bf16[8,192,128]{2,1,0:T(8,128)(2,1)} %copy-done.1, f32[8,192,128]{2,1,0:T(8,128)} %get-tuple-element.8.gate_ref, bf16[4,192,256]{2,1,0:T(8,128)(2,1)} %x_ref.3, bf16[256,256]{1,0:T(8,128)(2,1)} %wf_ref.1, ...), custom_call_target="tpu_custom_call" | custom-call | tf_op jit(solution)/shard_map/finish/pallas_call | solution.py:201
  149.3 0.9 copy.30
  150.2 24.6 %all_gather.23 = bf16[16,128,96]{1,2,0:T(8,128)(2,1)} all-gather(bf16[2,128,96]{1,2,0:T(8,128)(2,1)S(1)} %copy.30), channel_id=1, replica_groups=mesh['row'=8,'col'=16] {'row'}, dimensions={0}, use_global_device_ids=true | all-gather | bytes 442368 | tf_op jit(solution)/shard_map/all_gather | solution.py:348
  174.9 12.1 %all-to-all-start.3 = ((bf16[16,128,96]{1,2,0:T(8,128)(2,1)}), bf16[16,128,96]{1,2,0:T(8,128)(2,1)S(1)}, u32[]{:S(2)}, u32[]{:S(2)}) async-start(bf16[16,128,96]{1,2,0:T(8,128)(2,1)} %all_gather.23), calls=%async_computation.3 | async-start | bytes 786432 | tf_op jit(solution)/shard_map/all_to_all | solution.py:349
  187.0 28.4 %all-gather.1 = bf16[3072,128]{1,0:T(8,128)(2,1)} all-gather(bf16[192,128]{1,0:T(8,128)(2,1)} %get-tuple-element.10), channel_id=3, replica_groups=mesh['row'=8,'col'=16] {'col'}, dimensions={0}, use_global_device_ids=true | all-gather | bytes 835584 | tf_op jit(solution)/shard_map/all_gather | solution.py:347
  215.4 0.0 all-to-all-done.3
  215.4 1.0 copy.32.r_ref
  216.4 0.7 broadcast_in_dim.28.kj_ref
  217.1 44.5 %outer_update.1 = bf16[192,96,128]{2,1,0:T(8,128)(2,1)} custom-call(bf16[16,192,128]{2,1,0:T(8,128)(2,1)} %bitcast.31, bf16[16,128,96]{2,1,0:T(8,128)(2,1)} %copy.32.r_ref, bf16[1024,128]{1,0:T(8,128)(2,1)} %bitcast.34, f32[1,128]{1,0:T(1,128)} %bitcast.44, f32[192]{0:T(256)} %dynamic_slice.6.ki_ref, f32[96,128]{1,0:T(8,128)} %broadcast_in_dim.28.kj_ref, ...), custom_call_target="tpu_custom_call" | custom-call | tf_op jit(solution)/shard_map/outer_update/pallas_call | solution.py:261
  (17 shorter events, 0.1 us)
Async XLA Ops:
  7.2 93.0 %all-gather.5.cloned.1.call-start = ((), (), s32[]{:S(2)}) async-start(), calls=%async_computation.4 | async-start | bytes 5013504 | tf_op jit(solution)/shard_map/all_gather | solution.py:329
  9.0 30.7 %copy-start.5 = (s32[4,192]{1,0:T(4,128)S(1)}, s32[4,192]{1,0:T(4,128)}, u32[]{:S(2)}) copy-start(s32[4,192]{1,0:T(4,128)} %param.19) | copy-start | bytes 9220
  36.0 100.8 %copy-start.3 = (bf16[256,32]{0,1:T(8,128)(2,1)S(1)}, bf16[256,32]{0,1:T(8,128)(2,1)}, u32[]{:S(2)}) copy-start(bf16[256,32]{0,1:T(8,128)(2,1)} %param.27) | copy-start | bytes 49156
  36.0 101.5 %copy-start.4 = (s32[1536]{0:T(1024)S(1)}, s32[1536]{0:T(1024)}, u32[]{:S(2)}) copy-start(s32[1536]{0:T(1024)} %param.20) | copy-start | bytes 18436
  36.0 102.2 %copy-start.2 = (bf16[1024,128]{1,0:T(8,128)(2,1)S(1)}, bf16[1024,128]{1,0:T(8,128)(2,1)}, u32[]{:S(2)}) copy-start(bf16[1024,128]{1,0:T(8,128)(2,1)} %param.29) | copy-start | bytes 786436
  36.0 37.9 %all-to-all-start = ((bf16[8,3,192,128]{3,2,1,0:T(8,128)(2,1)}), bf16[8,3,192,128]{3,2,1,0:T(8,128)(2,1)S(1)}, u32[]{:S(2)}, u32[]{:S(2)}) async-start(bf16[8,3,192,128]{3,2,1,0:T(8,128)(2,1)} %get-tuple-element.7), calls=%async_computation | async-start | bytes 2359296 | tf_op jit(solution)/shard_map/all_to_all | solution.py:321
  73.9 26.4 %copy-start = (bf16[8,3,192,128]{3,2,1,0:T(8,128)(2,1)}, bf16[8,3,192,128]{3,2,1,0:T(8,128)(2,1)S(1)}, u32[]{:S(2)}) copy-start(bf16[8,3,192,128]{3,2,1,0:T(8,128)(2,1)S(1)} %all-to-all-done.qkv_ref) | copy-start | bytes 3538948
  131.9 12.0 %all-to-all-start.2 = ((bf16[8,192,128]{2,1,0:T(8,128)(2,1)}), bf16[8,192,128]{2,1,0:T(8,128)(2,1)S(1)}, u32[]{:S(2)}, u32[]{:S(2)}) async-start(bf16[8,192,128]{2,1,0:T(8,128)(2,1)} %attend.1), calls=%async_computation.2 | async-start | bytes 786432 | tf_op jit(solution)/shard_map/all_to_all | solution.py:333
  143.9 0.7 copy-start.1
  174.9 40.5 %all-to-all-start.3 = ((bf16[16,128,96]{1,2,0:T(8,128)(2,1)}), bf16[16,128,96]{1,2,0:T(8,128)(2,1)S(1)}, u32[]{:S(2)}, u32[]{:S(2)}) async-start(bf16[16,128,96]{1,2,0:T(8,128)(2,1)} %all_gather.23), calls=%async_computation.3 | async-start | bytes 786432 | tf_op jit(solution)/shard_map/all_to_all | solution.py:349
Sparse Core Ops, SparseCore 0:
  30.1 70.0 all-gather.4

commit v2 on v1

v2 whole, which is shorter than its diff:
```python
import jax
import jax.numpy as jnp
import numpy as np
from jax import lax
from jax.experimental import pallas as pl
from jax.experimental.pallas import tpu as pltpu
from jax.sharding import Mesh, PartitionSpec as P

F32 = jnp.float32
BF16 = jnp.bfloat16
HEADS = 8
HEAD = 32
SEQS = 4
ROWS = 192
HALF = 96
QUADS = 24
COLS = 96
EMB = 256
PAIR = 128
PEERS_COL = 16
TOTAL = 1536
CHUNK = 4
Q_ROWS, K_ROWS, V_ROWS, M_ROWS = 0, 192, 384, 576
SENT_ROWS = 592
LOG2E = 1.4426950408889634
ROW = ("x", "zl")
COL = ("y", "zh", "core")
VMEM_LIMIT = 56 * 1024 * 1024


def mm(a, b):
    return jnp.dot(a, b, preferred_element_type=F32)


def mm_nt(a, b):
    return lax.dot_general(a, b, (((1,), (1,)), ((), ())), preferred_element_type=F32)


def normalised(x, gain):
    mean = jnp.mean(x, axis=-1, keepdims=True)
    d = x - mean
    var = jnp.mean(d * d, axis=-1, keepdims=True)
    return (d * lax.rsqrt(var + 1e-05) * gain).astype(BF16)


def slot_of(shape):
    return (lax.broadcasted_iota(jnp.int32, shape, len(shape) - 1) // HEAD) % 4


def params():
    return pltpu.CompilerParams(vmem_limit_bytes=VMEM_LIMIT)


def vmem():
    return pl.BlockSpec(memory_space=pltpu.VMEM)


def smem():
    return pl.BlockSpec(memory_space=pltpu.SMEM)


def project_kernel(x_ref, g_ref, w_ref, e_ref, p_ref, m_ref, qkv_ref, gate_ref):
    slot = slot_of((ROWS, 4 * 128))
    plain = [normalised(x_ref[s].astype(F32), g_ref[...]) for s in range(SEQS)]
    moved = [mm(p_ref[...], n).astype(BF16) for n in plain]
    for part in range(4):
        rows = moved if part in (0, 3) else plain
        for m in range(2):
            w = mm(w_ref[:, part * EMB + m * 128 : part * EMB + (m + 1) * 128], e_ref[...]).astype(BF16)
            acc = mm(rows[0], w)
            for s in range(1, SEQS):
                acc = jnp.where(slot == s, mm(rows[s], w), acc)
            for u in range(4):
                t = acc[:, u * 128 : (u + 1) * 128]
                h = 4 * m + u
                if part == 0:
                    qkv_ref[h, Q_ROWS:K_ROWS] = (t * HEAD ** (-0.5)).astype(BF16)
                elif part == 1:
                    qkv_ref[h, K_ROWS:V_ROWS] = t.astype(BF16)
                elif part == 2:
                    qkv_ref[h, V_ROWS:M_ROWS] = t.astype(BF16)
                else:
                    gate_ref[h] = jax.nn.sigmoid(t)
    for h in range(HEADS):
        qkv_ref[h, M_ROWS:] = m_ref[...]


def project(x, gain, w, expand, perm, present):
    return pl.pallas_call(
        project_kernel,
        out_shape=(
            jax.ShapeDtypeStruct((HEADS, SENT_ROWS, 128), BF16),
            jax.ShapeDtypeStruct((HEADS, ROWS, 128), F32),
        ),
        compiler_params=params(),
        name="project",
    )(x, gain, w, expand, perm, present)


def bias_kernel(z_ref, g_ref, a_ref, o_ref):
    acc = jnp.zeros((128, 4 * COLS), F32)
    for k in range(8):
        n = normalised(z_ref[768 * k : 768 * (k + 1)].astype(F32), g_ref[...])
        both = jnp.concatenate([n[:384], n[384:]], axis=1)
        acc += mm_nt(a_ref[:, 256 * k : 256 * (k + 1)], both)
    o_ref[...] = acc.astype(BF16).reshape(HEADS, 16, 4 * COLS)


def pair_bias(z, gain, a):
    return pl.pallas_call(
        bias_kernel,
        out_shape=jax.ShapeDtypeStruct((HEADS, 2 * QUADS, 4 * COLS), BF16),
        grid=(3,),
        in_specs=[
            pl.BlockSpec((6144, PAIR), lambda t: (t, 0)),
            pl.BlockSpec((1, PAIR), lambda t: (0, 0)),
            pl.BlockSpec((128, 2048), lambda t: (0, 0)),
        ],
        out_specs=pl.BlockSpec((HEADS, 16, 4 * COLS), lambda t: (0, t, 0)),
        compiler_params=params(),
        name="pair_bias",
    )(z, gain, a)


OFFSETS = (0, 3, 1, 2)


def prepare_kernel(at_ref, own_ref, par_ref, k_ref, v_ref, q_ref):
    y = at_ref[0]
    core = at_ref[1]
    for side, ref in enumerate((own_ref, par_ref)):
        for d in range(4):
            first = 2 * lax.rem(y + OFFSETS[d], 4)
            span = slice(384 * d, 384 * (d + 1))
            keys = jnp.concatenate([ref[first + e, K_ROWS:V_ROWS] for e in range(2)], axis=0)
            k_ref[side, :128, span] = jnp.transpose(keys.astype(F32)).astype(BF16)
            for e in range(2):
                v_ref[side, 384 * d + ROWS * e : 384 * d + ROWS * (e + 1), :128] = ref[first + e, V_ROWS:M_ROWS]
            masks = [ref[first + e, M_ROWS:].astype(F32) for e in range(2)]
            line = jnp.concatenate([masks[0][:8], masks[0][8:, :64], masks[1][:8], masks[1][8:, :64]], axis=1)
            absent = (line - 1.0) * 1000000000.0
            k_ref[side, 128:, span] = jnp.concatenate([absent, jnp.zeros((120, 384), F32)], axis=0).astype(BF16)
        v_ref[side, :, 128:] = jnp.ones((TOTAL, 128), BF16)
        for r in range(8):
            q_ref[side, r] = ref[r, pl.ds(pl.multiple_of(core * HALF, HALF), HALF)]


def prepare(at, own, par):
    return pl.pallas_call(
        prepare_kernel,
        out_shape=(
            jax.ShapeDtypeStruct((2, EMB, TOTAL), BF16),
            jax.ShapeDtypeStruct((2, TOTAL, EMB), BF16),
            jax.ShapeDtypeStruct((2, 8, HALF, 128), BF16),
        ),
        in_specs=[smem(), vmem(), vmem()],
        out_specs=(vmem(), vmem(), vmem()),
        compiler_params=params(),
        name="prepare",
    )(at, own, par)


def attend_kernel(at_ref, k_ref, v_ref, q_ref, b0, bp, bm, f1, f2, o_ref, bias, even, odd):
    core = at_ref[1]
    count = CHUNK * HALF
    for d, ref in enumerate((b0, bp, bm, (f1, f2))):
        for r in range(CHUNK):
            got = ref[r] if d < 3 else ref[r // 2][r % 2]
            got = [got[k].astype(F32) * LOG2E for k in range(4)]
            for u in range(4):
                line = jnp.concatenate([g[:, COLS * u : COLS * (u + 1)] for g in got], axis=1)
                top = r * HALF + u * QUADS
                bias[top : top + QUADS, 384 * d : 384 * (d + 1)] = line
    slot = slot_of((count, 128))
    wide = slot_of((count, 256))
    lane = lax.broadcasted_iota(jnp.int32, (count, 128), 1)

    def scores(out, side, s):
        q = jnp.concatenate([q_ref[side, r] for r in range(CHUNK)], axis=0).astype(F32)
        lhs = jnp.concatenate(
            [jnp.where(slot == s, q, 0.0).astype(BF16), jnp.where(lane == s, 1.0, 0.0).astype(BF16)], axis=1
        )
        top = None
        for t in range(6):
            span = slice(256 * t, 256 * (t + 1))
            c = mm(lhs, k_ref[side, :, span]) * LOG2E + bias[:, span]
            out[:, span] = c
            both = jnp.maximum(c[:, :128], c[:, 128:])
            top = both if top is None else jnp.maximum(top, both)
        return jnp.max(top, axis=1, keepdims=True)

    def values(buf, top, side):
        acc = None
        for t in range(6):
            span = slice(256 * t, 256 * (t + 1))
            e = jnp.exp2(buf[:, span] - top).astype(BF16)
            p = mm(e, v_ref[side, span])
            acc = p if acc is None else acc + p
        return acc

    for side in range(2):
        top = scores(even, side, 0)
        total = jnp.zeros((count, 256), F32)
        for s in range(SEQS):
            now, later = (even, odd) if s % 2 == 0 else (odd, even)
            if s < SEQS - 1:
                following = scores(later, side, s + 1)
            total = jnp.where(wide == s, values(now, top, side), total)
            if s < SEQS - 1:
                top = following
        out = (total[:, :128] / total[:, 128:]).astype(BF16)
        quad = core if side == 0 else 1 - core
        for r in range(CHUNK):
            o_ref[r, quad] = out[HALF * r : HALF * (r + 1)]


def attend(at, k, v, q, pieces, chunk):
    return pl.pallas_call(
        attend_kernel,
        out_shape=jax.ShapeDtypeStruct((CHUNK, 2, HALF, 128), BF16),
        grid=(1,),
        in_specs=[
            smem(),
            pl.BlockSpec((2, EMB, TOTAL), lambda t: (0, 0, 0)),
            pl.BlockSpec((2, TOTAL, EMB), lambda t: (0, 0, 0)),
            pl.BlockSpec((2, CHUNK, HALF, 128), lambda t: (0, chunk, 0, 0)),
        ]
        + [vmem()] * 5,
        out_specs=pl.BlockSpec((CHUNK, 2, HALF, 128), lambda t: (0, 0, 0, 0)),
        scratch_shapes=[pltpu.VMEM((CHUNK * HALF, TOTAL), F32) for _ in range(3)],
        compiler_params=params(),
        name=f"attend_{chunk}",
    )(at, k, v, q, *pieces)


def finish_kernel(
    att_ref, gate_ref, x_ref, wf_ref, pinv_ref, g_ref, wl_ref, wr_ref, ac_ref, ar_ref, new_ref, left_ref, right_ref
):
    gated = jnp.concatenate(
        [(gate_ref[h] * att_ref[h].astype(F32)).astype(BF16) for h in range(HEADS)], axis=1
    )
    gated = mm(pinv_ref[...], gated)
    w = jnp.concatenate([wf_ref[HEAD * (k // 4) : HEAD * (k // 4 + 1)] for k in range(4 * HEADS)], axis=0)
    slot = slot_of((ROWS, 4 * EMB))
    slot_one = slot_of((ROWS, 128))
    left = jnp.zeros((ROWS, 128), F32)
    for s in range(SEQS):
        inc = mm(jnp.where(slot == s, gated, 0.0).astype(BF16), w)
        new = (x_ref[s].astype(F32) + inc).astype(BF16)
        new_ref[s] = new
        n = normalised(new.astype(F32), g_ref[...])
        left = jnp.where(slot_one == s, mm(n, wl_ref[...]), left)
        right = mm_nt(wr_ref[...], n) * ar_ref[s : s + 1]
        rows = slice(HEAD * s, HEAD * (s + 1))
        right_ref[0, rows] = right[:, :128].astype(BF16)
        right_ref[1, rows] = jnp.concatenate([right[:, COLS:], right[:, :32]], axis=1).astype(BF16)
    left_ref[...] = (left * ac_ref[...]).astype(BF16)


def finish(*args):
    return pl.pallas_call(
        finish_kernel,
        out_shape=(
            jax.ShapeDtypeStruct((SEQS, ROWS, EMB), BF16),
            jax.ShapeDtypeStruct((ROWS, 128), BF16),
            jax.ShapeDtypeStruct((2, 128, 128), BF16),
        ),
        compiler_params=params(),
        name="finish",
    )(*args)


STEP = 48


def outer_kernel(at_ref, lo_ref, lp_ref, r_ref, w_ref, off_ref, ki_ref, kj_ref, z_ref, o_ref, l_all, r_all, lhs, rhs, obf):
    step = pl.program_id(0)

    @pl.when(step == 0)
    def _():
        core = at_ref[1]
        for p in range(PEERS_COL // 2):
            for side, ref in enumerate((lo_ref, lp_ref)):
                c = 2 * p + (core if side == 0 else 1 - core)
                l_all[pl.ds(pl.multiple_of(c * ROWS, ROWS), ROWS)] = ref[p].astype(F32)
        for c in range(PEERS_COL):
            r_all[128 * c : 128 * (c + 1)] = r_ref[c].astype(F32)
        for q in range(8):
            lines = [
                r_all[pl.ds(HEAD * s + 4 * q + b, PEERS_COL, stride=128), :] for b in range(4) for s in range(SEQS)
            ]
            turned = jnp.transpose(jnp.concatenate(lines, axis=0))
            lhs[COLS * q : COLS * (q + 1)] = turned[:COLS].astype(BF16)

    slot = slot_of((PEERS_COL, 128))
    for k in range(STEP):
        m = l_all[pl.ds(step * STEP + k, PEERS_COL, stride=ROWS), :]
        rolled = [m] + [pltpu.roll(m, HEAD * d, 1) for d in range(1, 4)]
        for b in range(4):
            for s in range(SEQS):
                at = 64 * b + 16 * s
                rhs[at : at + 16, 128 * k : 128 * (k + 1)] = jnp.where(slot == b, rolled[(b - s) % 4], 0.0).astype(BF16)
    for k in range(0, STEP, 2):
        outer = mm(lhs[...], rhs[:, 128 * k : 128 * (k + 2)]).astype(BF16)
        for e in range(2):
            for q in range(8):
                obf[COLS * (k + e) : COLS * (k + e + 1), 128 * q : 128 * (q + 1)] = outer[
                    COLS * q : COLS * (q + 1), 128 * e : 128 * (e + 1)
                ]
    update = mm(obf[...], w_ref[...]) + off_ref[...]
    for k in range(STEP):
        keep = kj_ref[...] * ki_ref[step * STEP + k]
        o_ref[k] = (z_ref[k].astype(F32) + update[COLS * k : COLS * (k + 1)] * keep).astype(BF16)


def outer_update(at, left_own, left_par, right, w, offset, keep_i, keep_j, z):
    return pl.pallas_call(
        outer_kernel,
        out_shape=jax.ShapeDtypeStruct((ROWS, COLS, PAIR), BF16),
        grid=(ROWS // STEP,),
        in_specs=[
            smem(),
            pl.BlockSpec((PEERS_COL // 2, ROWS, 128), lambda t: (0, 0, 0)),
            pl.BlockSpec((PEERS_COL // 2, ROWS, 128), lambda t: (0, 0, 0)),
            pl.BlockSpec((PEERS_COL, 128, 128), lambda t: (0, 0, 0)),
            pl.BlockSpec((1024, PAIR), lambda t: (0, 0)),
            pl.BlockSpec((1, PAIR), lambda t: (0, 0)),
            smem(),
            pl.BlockSpec((COLS, PAIR), lambda t: (0, 0)),
            pl.BlockSpec((STEP, COLS, PAIR), lambda t: (t, 0, 0)),
        ],
        out_specs=pl.BlockSpec((STEP, COLS, PAIR), lambda t: (t, 0, 0)),
        scratch_shapes=[
            pltpu.VMEM((PEERS_COL * ROWS, 128), F32),
            pltpu.VMEM((PEERS_COL * 128, 128), F32),
            pltpu.VMEM((8 * COLS, 256), BF16),
            pltpu.VMEM((256, 128 * STEP), BF16),
            pltpu.VMEM((STEP * COLS, 1024), BF16),
        ],
        compiler_params=params(),
        name="outer_update",
    )(at, left_own, left_par, right, w, offset, keep_i, keep_j, z)


def tables():
    expand = np.zeros((128, 4, 4, HEAD), np.float32)
    for u in range(4):
        for d in range(HEAD):
            expand[u * HEAD + d, u, :, d] = 1
    perm = np.zeros((ROWS, ROWS), np.float32)
    for i in range(ROWS):
        half, rest = divmod(i, HALF)
        perm[half * HALF + (rest % 4) * QUADS + rest // 4, i] = 1
    return expand.reshape(128, 512), perm


def swap_cores(x):
    return lax.ppermute(x, "core", [(0, 1), (1, 0)])


def along_y(x, d):
    return lax.ppermute(x, "y", [(a, (a + d) % 4) for a in range(4)])


def to_all(x, axes, n):
    return lax.all_to_all(jnp.broadcast_to(x[None], (n,) + x.shape), axes, 0, 0, tiled=True)


def turn_grid(x):
    def index(a, b, c, d):
        return ((a * 2 + b) * 4 + c) * 2 + d

    moves = [
        (index(a, b, c, d), index(c, d, a, b)) for a in range(4) for b in range(2) for c in range(4) for d in range(2)
    ]
    return lax.ppermute(x, ("x", "zl", "y", "zh"), moves)


def ring_pieces(block):
    up, down = along_y(block, 1), along_y(block, 3)
    return block, up, down, along_y(up[: CHUNK // 2], 1), along_y(down[CHUNK // 2 :], 3)


def on_device(
    alignment_embedding,
    couplings_embedding,
    alignment_availability,
    amino_availability,
    alignment_scaling_vector,
    attention_joint_matrix,
    attention_final_matrix,
    coupling_scaling_vector,
    coupling_logit_matrix,
    tensor_scaling_vector,
    first_factor_matrix,
    second_factor_matrix,
    tensor_projection_matrix,
    tensor_offset_vector,
):
    core = lax.axis_index("core")
    at = jnp.stack([lax.axis_index("y"), core]).astype(jnp.int32)
    expand, perm = tables()

    spread = (
        jnp.eye(16, dtype=BF16)[None, :, :, None] * coupling_logit_matrix.T[:, None, None, :]
    ).reshape(HEADS * 16, 16 * PAIR)
    bias = pair_bias(
        couplings_embedding.reshape(ROWS * COLS, PAIR), coupling_scaling_vector[None], spread
    ).reshape(HEADS, 1, 2, QUADS, 4 * COLS)
    bias = jnp.broadcast_to(bias, (HEADS, 2, 2, QUADS, 4 * COLS)).reshape(4 * HEADS, QUADS, 4 * COLS)
    bias = lax.all_to_all(bias, ROW + ("zh", "core"), 0, 0, tiled=True).reshape(8, 4, QUADS, 4 * COLS)

    present = alignment_availability.astype(BF16)
    sent_mask = jnp.pad(
        jnp.stack([present[:, :128], jnp.pad(present[:, 128:], ((0, 0), (0, 64)))]), ((0, 0), (0, 4), (0, 0))
    ).reshape(16, 128)
    own, gate = project(
        alignment_embedding,
        alignment_scaling_vector[None],
        attention_joint_matrix,
        jnp.asarray(expand, BF16),
        jnp.asarray(perm, BF16),
        sent_mask,
    )
    own = lax.all_to_all(own, ROW, 0, 0, tiled=True)
    k, v, q = prepare(at, own, swap_cores(own))

    attended = jnp.concatenate(
        [attend(at, k, v, q, ring_pieces(bias[CHUNK * c : CHUNK * (c + 1)]), c) for c in range(2)], axis=0
    ).reshape(16, HALF, 128)
    attended = lax.all_to_all(attended, ROW + ("core",), 0, 0, tiled=True).reshape(HEADS, ROWS, 128)

    present = alignment_availability.astype(F32)
    alignment_refreshed, left, right = finish(
        attended,
        gate,
        alignment_embedding,
        attention_final_matrix,
        jnp.asarray(perm.T, BF16),
        tensor_scaling_vector[None],
        jnp.tile(first_factor_matrix, (1, 4)),
        second_factor_matrix.T,
        jnp.repeat(present.T, HEAD, axis=1),
        present,
    )
    mine = lax.dynamic_index_in_dim(right, core, 0, False)
    theirs = swap_cores(lax.dynamic_index_in_dim(right, 1 - core, 0, False))
    right = jnp.where(core == 0, jnp.stack([mine, theirs]), jnp.stack([theirs, mine]))
    right = to_all(turn_grid(right), ROW, 8).reshape(PEERS_COL, 128, 128)
    left = to_all(left, ("y", "zh"), 8)

    keep = amino_availability.astype(F32)
    keep_i = lax.dynamic_slice_in_dim(keep, lax.axis_index(ROW) * ROWS, ROWS)
    keep_j = lax.dynamic_slice_in_dim(keep, lax.axis_index(COL) * COLS, COLS)
    projection = (tensor_projection_matrix.astype(F32) / 64).astype(BF16)
    projection = projection.reshape(HEAD, 8, 4, PAIR).transpose(1, 2, 0, 3).reshape(1024, PAIR)
    couplings_refreshed = outer_update(
        at,
        left,
        swap_cores(left),
        right,
        projection,
        tensor_offset_vector[None],
        keep_i,
        jnp.broadcast_to(keep_j[:, None], (COLS, PAIR)),
        couplings_embedding,
    )
    return alignment_refreshed, couplings_refreshed


def solution(mesh):
    mesh = Mesh(mesh.devices.reshape(4, 2, 4, 2, 2), ROW + COL)
    placed = (P(COL, ROW, None), P(ROW, COL, None), P(COL, ROW)) + (P(),) * 11
    return jax.shard_map(
        on_device,
        mesh=mesh,
        in_specs=placed,
        out_specs=(P(COL, ROW, None), P(ROW, COL, None)),
        check_vma=False,
    )
```

time: 269 us -> 182 us (0.68)
  blocking collectives: 98.7 us -> 0 us
  Pallas kernels: 95 us -> 70.4 us
  starting transfers between devices: 19.9 us -> 42.7 us
  waiting for transfers between devices: 31.2 us -> 46.4 us
  between operations: 14.1 us -> 0.82 us
  local copies, waits for them, and re-layouts: 8.07 us -> 15.8 us
  other arithmetic: 1.45 us -> 4.48 us
    all_gather x3 -> x0, blocking collectives: 85.9 us -> none  [the longest x1 32.8 us: on_device(): present_all = lax.all_gather(present, 'row', axis=1, tiled=True)]
    all_to_all x3 -> x5, waiting for transfers between devices: 4.87 us -> 39.1 us  [the longest x2 11.8 us: to_all(): lax.all_to_all(jnp.broadcast_to(x[None], (n,) + x.shape), axes, 0, 0, til...]
    all_gather x1 -> x0, waiting for transfers between devices: 26.4 us -> none  [on_device(): bias = lax.all_gather(bias, 'col', axis=0)]
    pallas_call x1, Pallas kernels: 44.5 us -> 26.8 us  [outer_update(): pl.pallas_call(outer_kernel, out_shape=jax.ShapeDtypeStruct((ROWS, COLS,...]
    ppermute x0 -> x12, starting transfers between devices: none -> 13.8 us  [the longest x8 10.9 us: along_y(): return lax.ppermute(x, 'y', [(a, (a + d) % 4) for a in range(4)])]
    all_to_all x1 -> x0, blocking collectives: 12.8 us -> none  [on_device(): bias = lax.all_to_all(bias, 'row', 0, 0, tiled=True)]
    all_to_all x3 -> x5, starting transfers between devices: 19.9 us -> 28.9 us  [the longest x2 10.7 us: to_all(): lax.all_to_all(jnp.broadcast_to(x[None], (n,) + x.shape), axes, 0, 0, til...]
    ppermute x0 -> x12, waiting for transfers between devices: none -> 7.32 us  [the longest x8 6.45 us: along_y(): return lax.ppermute(x, 'y', [(a, (a + d) % 4) for a in range(4)])]
  transfers between devices with their start and end apart: 4 -> 17, of which waited for: 2 -> 8; matrix products, arithmetic and copies ran while one was open for 2% -> 5% of each run, Pallas kernels for 2% -> 12%
where the time goes in v2:
time: 182 us; the launch traced here: 181 us
  Pallas kernels  70.4 us (39%)
  waiting for transfers between devices  46.4 us (25%)
  starting transfers between devices  42.7 us (23%)
  local copies, waits for them, and re-layouts  15.8 us (9%)
  other arithmetic  4.48 us (2%)
    pallas_call x1, Pallas kernels, outer_update(): pl.pallas_call(outer_kernel, out_shape=jax.ShapeDtypeStruct((ROWS, COLS,...  26.8 us
    pallas_call x2, Pallas kernels, attend(): pl.pallas_call(attend_kernel, out_shape=jax.ShapeDtypeStruct((CHUNK, 2, H...  20.6 us
    all_to_all x2, waiting for transfers between devices, to_all(): lax.all_to_all(jnp.broadcast_to(x[None], (n,) + x.shape), axes, 0, 0, til...  11.8 us
    all_to_all x1, waiting for transfers between devices, on_device(): lax.all_to_all(bias, ROW + ('zh', 'core'), 0, 0, tiled=True)  11.6 us
    ppermute x8, starting transfers between devices, along_y(): return lax.ppermute(x, 'y', [(a, (a + d) % 4) for a in range(4)])  10.9 us
    all_to_all x2, starting transfers between devices, to_all(): lax.all_to_all(jnp.broadcast_to(x[None], (n,) + x.shape), axes, 0, 0, til...  10.7 us
    all_to_all x1, waiting for transfers between devices, on_device(): own = lax.all_to_all(own, ROW, 0, 0, tiled=True)  8.48 us
    pallas_call x1, Pallas kernels, pair_bias(): pl.pallas_call(bias_kernel, out_shape=jax.ShapeDtypeStruct((HEADS, 2 * QU...  8.19 us
  transfers between devices with their start and end apart: 17, of which 8 were waited for; matrix products, arithmetic and copies ran while one was open for 5% of the time, Pallas kernels for 12%

profile of v2, /device:TPU:1, one launch (start us, length us, event | category | flops | bytes accessed | tf_op | source)
XLA Modules:
  0.0 180.6 jit_solution(3163196551369961043)
XLA Ops:
  0.6 1.3 fusion.6
  2.6 6.3 %project.1 = (bf16[8,592,128]{2,1,0:T(8,128)(2,1)}, f32[8,192,128]{2,1,0:T(8,128)}) custom-call(bf16[4,192,256]{2,1,0:T(8,128)(2,1)} %x_ref.3, f32[1,256]{1,0:T(1,128)} %bitcast.58, bf16[256,1024]{1,0:T(8,128)(2,1)} %w_ref.1, bf16[128,512]{1,0:T(8,128)(2,1)} %constant.52.clone.e_ref, bf16[192,192]{1,0:T(8,128)(2,1)} %constant.53.clone.p_ref, ...), custom_call_target="tpu_custom_call" | custom-call | tf_op jit(solution)/shard_map/project/pallas_call | solution.py:89
  8.9 6.2 %all-to-all-start = ((bf16[8,592,128]{2,1,0:T(8,128)(2,1)}), bf16[8,592,128]{2,1,0:T(8,128)(2,1)S(1)}, u32[]{:S(2)}, u32[]{:S(2)}) async-start(bf16[8,592,128]{2,1,0:T(8,128)(2,1)} %get-tuple-element.10), calls=%async_computation | async-start | bytes 2424832 | tf_op jit(solution)/shard_map/all_to_all | solution.py:425
  15.2 0.9 copy.27
  16.1 8.2 %pair_bias.1 = bf16[8,48,384]{2,1,0:T(8,128)(2,1)} custom-call(bf16[18432,128]{1,0:T(8,128)(2,1)} %bitcast.38, f32[1,128]{1,0:T(1,128)} %bitcast.59, bf16[128,2048]{1,0:T(8,128)(2,1)} %bitcast.40), custom_call_target="tpu_custom_call" | custom-call | tf_op jit(solution)/shard_map/pair_bias/pallas_call | solution.py:110
  24.3 8.5 %all-to-all-done.own_ref = bf16[8,592,128]{2,1,0:T(8,128)(2,1)S(1)} async-done(((bf16[8,592,128]{2,1,0:T(8,128)(2,1)}), bf16[8,592,128]{2,1,0:T(8,128)(2,1)S(1)}, u32[]{:S(2)}, u32[]{:S(2)}) %all-to-all-start) | async-done | bytes 1212448 | tf_op jit(solution)/shard_map/all_to_all | solution.py:425
  32.8 2.0 %broadcast_in_dim.45 = bf16[8,2,2,24,384]{4,3,2,1,0:T(8,128)(2,1)} broadcast(bf16[8,2,24,384]{3,2,1,0:T(8,128)(2,1)} %bitcast.43), dimensions={0,2,3,4} | broadcast | bytes 884736 | tf_op jit(solution)/shard_map/broadcast_in_dim | solution.py:410
  34.8 6.6 %all-to-all-start.1 = ((bf16[32,24,384]{2,1,0:T(8,128)(2,1)}), bf16[32,24,384]{2,1,0:T(8,128)(2,1)S(1)}, u32[]{:S(2)}, u32[]{:S(2)}) async-start(bf16[32,24,384]{2,1,0:T(8,128)(2,1)} %bitcast.10), calls=%async_computation.1 | async-start | bytes 1179648 | tf_op jit(solution)/shard_map/all_to_all | solution.py:411
  41.8 11.6 %all-to-all-done.1 = bf16[32,24,384]{2,1,0:T(8,128)(2,1)S(1)} async-done(((bf16[32,24,384]{2,1,0:T(8,128)(2,1)}), bf16[32,24,384]{2,1,0:T(8,128)(2,1)S(1)}, u32[]{:S(2)}, u32[]{:S(2)}) %all-to-all-start.1) | async-done | bytes 589856 | tf_op jit(solution)/shard_map/all_to_all | solution.py:411
  53.5 1.4 collective-permute-start.1
  54.9 1.5 collective-permute-start.2
  56.4 2.7 %collective-permute-start.6 = (bf16[4,4,24,384]{3,2,1,0:T(8,128)(2,1)S(1)}, bf16[4,4,24,384]{3,2,1,0:T(8,128)(2,1)S(1)}, u32[]{:S(2)}, u32[]{:S(2)}) collective-permute-start(bf16[4,4,24,384]{3,2,1,0:T(8,128)(2,1)S(1)} %bitcast.45), channel_id=1, source_target_pairs={{0,12},{4,0},{8,4},{12,8},{1,13},{5,1},{9,5},{13,9},{2,14},{6,2},{... | collective-permute-start | bytes 884744 | tf_op jit(solution)/shard_map/ppermute | solution.py:362
  59.1 4.3 %collective-permute-done.1.bp = bf16[4,4,24,384]{3,2,1,0:T(8,128)(2,1)S(1)} collective-permute-done((bf16[4,4,24,384]{3,2,1,0:T(8,128)(2,1)S(1)}, bf16[4,4,24,384]{3,2,1,0:T(8,128)(2,1)S(1)}, u32[]{:S(2)}, u32[]{:S(2)}) %collective-permute-start.1) | collective-permute-done | bytes 294944 | tf_op jit(solution)/shard_map/ppermute | solution.py:362
  64.8 2.7 %collective-permute-start.4 = (bf16[2,4,24,384]{3,2,1,0:T(8,128)(2,1)}, bf16[2,4,24,384]{3,2,1,0:T(8,128)(2,1)}, u32[]{:S(2)}, u32[]{:S(2)}) collective-permute-start(bf16[2,4,24,384]{3,2,1,0:T(8,128)(2,1)} %slice.44), channel_id=1, source_target_pairs={{0,12},{4,0},{8,4},{12,8},{1,13},{5,1},{9,5},{13,9},{2,14},{6,2},{... | collective-permute-start | bytes 442376 | tf_op jit(solution)/shard_map/ppermute | solution.py:362
  67.5 2.2 %collective-permute-done.5.bp = bf16[4,4,24,384]{3,2,1,0:T(8,128)(2,1)S(1)} collective-permute-done((bf16[4,4,24,384]{3,2,1,0:T(8,128)(2,1)S(1)}, bf16[4,4,24,384]{3,2,1,0:T(8,128)(2,1)S(1)}, u32[]{:S(2)}, u32[]{:S(2)}) %collective-permute-start.5) | collective-permute-done | bytes 294944 | tf_op jit(solution)/shard_map/ppermute | solution.py:362
  71.2 2.7 %collective-permute-start.8 = (bf16[2,4,24,384]{3,2,1,0:T(8,128)(2,1)}, bf16[2,4,24,384]{3,2,1,0:T(8,128)(2,1)}, u32[]{:S(2)}, u32[]{:S(2)}) collective-permute-start(bf16[2,4,24,384]{3,2,1,0:T(8,128)(2,1)} %slice.47), channel_id=1, source_target_pairs={{0,12},{4,0},{8,4},{12,8},{1,13},{5,1},{9,5},{13,9},{2,14},{6,2},{... | collective-permute-start | bytes 442376 | tf_op jit(solution)/shard_map/ppermute | solution.py:362
  74.5 1.0 copy-done.4
  75.5 3.9 %prepare.1 = (bf16[2,256,1536]{2,1,0:T(8,128)(2,1)}, bf16[2,1536,256]{2,1,0:T(8,128)(2,1)}, bf16[2,8,96,128]{3,2,1,0:T(8,128)(2,1)}) custom-call(s32[2]{0:T(128)} %pad_add_fusion.at_ref, bf16[8,592,128]{2,1,0:T(8,128)(2,1)} %copy-done, bf16[8,592,128]{2,1,0:T(8,128)(2,1)} %copy-done.4), custom_call_target="tpu_custom_call" | custom-call | tf_op jit(solution)/shard_map/prepare/pallas_call | solution.py:149
  80.1 10.1 %attend_0.1 = bf16[4,2,96,128]{3,2,1,0:T(8,128)(2,1)} custom-call(s32[2]{0:T(128)} %pad_add_fusion.at_ref, bf16[2,256,1536]{2,1,0:T(8,128)(2,1)} %get-tuple-element.11.k_ref, bf16[2,1536,256]{2,1,0:T(8,128)(2,1)} %get-tuple-element.12.v_ref, bf16[2,8,96,128]{3,2,1,0:T(8,128)(2,1)} %get-tuple-element.13.q_ref, bf16[4,4,24,384]{3,2,1,0:T(8,128)(2,1)} %bitcast.49, ...), custom_call_target="tpu_custom_call" | custom-call | tf_op jit(solution)/shard_map/attend_0/pallas_call | solution.py:218
  90.3 10.5 %attend_1.1 = bf16[4,2,96,128]{3,2,1,0:T(8,128)(2,1)} custom-call(s32[2]{0:T(128)} %pad_add_fusion.at_ref, bf16[2,256,1536]{2,1,0:T(8,128)(2,1)} %get-tuple-element.11.k_ref, bf16[2,1536,256]{2,1,0:T(8,128)(2,1)} %get-tuple-element.12.v_ref, bf16[2,8,96,128]{3,2,1,0:T(8,128)(2,1)} %get-tuple-element.13.q_ref, bf16[4,4,24,384]{3,2,1,0:T(8,128)(2,1)} %bitcast.46, ...), custom_call_target="tpu_custom_call" | custom-call | tf_op jit(solution)/shard_map/attend_1/pallas_call | solution.py:218
  100.7 1.7 pad_maximum_fusion
  102.4 5.4 %all-to-all-start.2 = ((bf16[16,96,128]{2,1,0:T(8,128)(2,1)}), bf16[16,96,128]{2,1,0:T(8,128)(2,1)S(1)}, u32[]{:S(2)}, u32[]{:S(2)}) async-start(bf16[16,96,128]{2,1,0:T(8,128)(2,1)} %bitcast.13), calls=%async_computation.2 | async-start | bytes 786432 | tf_op jit(solution)/shard_map/all_to_all | solution.py:431
  109.3 7.1 %all-to-all-done.2 = bf16[16,96,128]{2,1,0:T(8,128)(2,1)S(1)} async-done(((bf16[16,96,128]{2,1,0:T(8,128)(2,1)}), bf16[16,96,128]{2,1,0:T(8,128)(2,1)S(1)}, u32[]{:S(2)}, u32[]{:S(2)}) %all-to-all-start.2) | async-done | bytes 393248 | tf_op jit(solution)/shard_map/all_to_all | solution.py:431
  117.2 4.6 %finish.1 = (bf16[4,192,256]{2,1,0:T(8,128)(2,1)}, bf16[192,128]{1,0:T(8,128)(2,1)}, bf16[2,128,128]{2,1,0:T(8,128)(2,1)}) custom-call(bf16[8,192,128]{2,1,0:T(8,128)(2,1)} %bitcast.42, f32[8,192,128]{2,1,0:T(8,128)} %get-tuple-element.14.gate_ref, bf16[4,192,256]{2,1,0:T(8,128)(2,1)} %x_ref.3, bf16[256,256]{1,0:T(8,128)(2,1)} %wf_ref.1, ...), custom_call_target="tpu_custom_call" | custom-call | tf_op jit(solution)/shard_map/finish/pallas_call | solution.py:261
  121.9 1.6 broadcast_in_dim.48
  123.5 3.5 %all-to-all-start.3 = ((bf16[8,192,128]{2,1,0:T(8,128)(2,1)}), bf16[8,192,128]{2,1,0:T(8,128)(2,1)S(1)}, u32[]{:S(2)}, u32[]{:S(2)}) async-start(bf16[8,192,128]{2,1,0:T(8,128)(2,1)} %broadcast_in_dim.48), calls=%async_computation.3 | async-start | bytes 786432 | tf_op jit(solution)/shard_map/all_to_all | solution.py:366
  130.1 5.9 %all-to-all-done.3.lo_ref = bf16[8,192,128]{2,1,0:T(8,128)(2,1)S(1)} async-done(((bf16[8,192,128]{2,1,0:T(8,128)(2,1)}), bf16[8,192,128]{2,1,0:T(8,128)(2,1)S(1)}, u32[]{:S(2)}, u32[]{:S(2)}) %all-to-all-start.3) | async-done | bytes 393248 | tf_op jit(solution)/shard_map/all_to_all | solution.py:366
  136.0 0.9 broadcast_in_dim.49
  137.0 7.2 %all-to-all-start.4 = ((bf16[8,2,128,128]{3,2,1,0:T(8,128)(2,1)}), bf16[8,2,128,128]{3,2,1,0:T(8,128)(2,1)S(1)}, u32[]{:S(2)}, u32[]{:S(2)}) async-start(bf16[8,2,128,128]{3,2,1,0:T(8,128)(2,1)} %broadcast_in_dim.49), calls=%async_computation.4 | async-start | bytes 1048576 | tf_op jit(solution)/shard_map/all_to_all | solution.py:366
  144.2 1.1 collective-permute-start.9
  147.0 5.9 %all-to-all-done.4 = bf16[8,2,128,128]{3,2,1,0:T(8,128)(2,1)S(1)} async-done(((bf16[8,2,128,128]{3,2,1,0:T(8,128)(2,1)}), bf16[8,2,128,128]{3,2,1,0:T(8,128)(2,1)S(1)}, u32[]{:S(2)}, u32[]{:S(2)}) %all-to-all-start.4) | async-done | bytes 524320 | tf_op jit(solution)/shard_map/all_to_all | solution.py:366
  153.8 26.8 %outer_update.1 = bf16[192,96,128]{2,1,0:T(8,128)(2,1)} custom-call(s32[2]{0:T(128)} %pad_add_fusion.at_ref, bf16[8,192,128]{2,1,0:T(8,128)(2,1)} %copy-done.2, bf16[8,192,128]{2,1,0:T(8,128)(2,1)} %copy-done.12, bf16[16,128,128]{2,1,0:T(8,128)(2,1)} %bitcast.39, bf16[1024,128]{1,0:T(8,128)(2,1)} %bitcast.50, f32[1,128]{1,0:T(1,128)} %bitcast.60, ...), custom_call_target="tpu_custom_call" | custom-call | tf_op jit(solution)/shard_map/outer_update/pallas_call | solution.py:317
  (74 shorter events, 13.3 us)
Async XLA Ops:
  2.6 12.5 %copy-start.17 = (bf16[128,8]{0,1:T(8,128)(2,1)S(1)}, bf16[128,8]{0,1:T(8,128)(2,1)}, u32[]{:S(2)}) copy-start(bf16[128,8]{0,1:T(8,128)(2,1)} %param.25) | copy-start | bytes 6148
  8.9 23.9 %all-to-all-start = ((bf16[8,592,128]{2,1,0:T(8,128)(2,1)}), bf16[8,592,128]{2,1,0:T(8,128)(2,1)S(1)}, u32[]{:S(2)}, u32[]{:S(2)}) async-start(bf16[8,592,128]{2,1,0:T(8,128)(2,1)} %get-tuple-element.10), calls=%async_computation | async-start | bytes 2424832 | tf_op jit(solution)/shard_map/all_to_all | solution.py:425
  32.8 20.7 %copy-start = (bf16[8,592,128]{2,1,0:T(8,128)(2,1)}, bf16[8,592,128]{2,1,0:T(8,128)(2,1)S(1)}, u32[]{:S(2)}) copy-start(bf16[8,592,128]{2,1,0:T(8,128)(2,1)S(1)} %all-to-all-done.own_ref) | copy-start | bytes 3637252
  34.8 18.6 %all-to-all-start.1 = ((bf16[32,24,384]{2,1,0:T(8,128)(2,1)}), bf16[32,24,384]{2,1,0:T(8,128)(2,1)S(1)}, u32[]{:S(2)}, u32[]{:S(2)}) async-start(bf16[32,24,384]{2,1,0:T(8,128)(2,1)} %bitcast.10), calls=%async_computation.1 | async-start | bytes 1179648 | tf_op jit(solution)/shard_map/all_to_all | solution.py:411
  41.5 33.0 %collective-permute-start = (bf16[8,592,128]{2,1,0:T(8,128)(2,1)S(1)}, bf16[8,592,128]{2,1,0:T(8,128)(2,1)S(1)}, u32[]{:S(2)}, u32[]{:S(2)}) collective-permute-start(bf16[8,592,128]{2,1,0:T(8,128)(2,1)S(1)} %all-to-all-done.own_ref), channel_id=1, source_target_pairs={{0,1},{1,0},{2,3},{3,2},{4,5},{5,4},{6,7},{7,6},{8,9},{9,8},{10,11... | collective-permute-start | bytes 3637256 | tf_op jit(solution)/shard_map/ppermute | solution.py:358
  53.5 16.9 %copy-start.6 = (bf16[16,24,384]{2,1,0:T(8,128)(2,1)}, bf16[16,24,384]{2,1,0:T(8,128)(2,1)S(1)}, u32[]{:S(2)}) copy-start(bf16[16,24,384]{2,1,0:T(8,128)(2,1)S(1)} %get-tuple-element.18) | copy-start | bytes 884740
  53.5 25.9 %copy-start.5 = (bf16[16,24,384]{2,1,0:T(8,128)(2,1)}, bf16[16,24,384]{2,1,0:T(8,128)(2,1)S(1)}, u32[]{:S(2)}) copy-start(bf16[16,24,384]{2,1,0:T(8,128)(2,1)S(1)} %get-tuple-element.19) | copy-start | bytes 884740
  53.5 9.8 %collective-permute-start.1 = (bf16[4,4,24,384]{3,2,1,0:T(8,128)(2,1)S(1)}, bf16[4,4,24,384]{3,2,1,0:T(8,128)(2,1)S(1)}, u32[]{:S(2)}, u32[]{:S(2)}) collective-permute-start(bf16[4,4,24,384]{3,2,1,0:T(8,128)(2,1)S(1)} %bitcast.47), channel_id=1, source_target_pairs={{0,4},{4,8},{8,12},{12,0},{1,5},{5,9},{9,13},{13,1},{2,6},{6,10},{... | collective-permute-start | bytes 884744 | tf_op jit(solution)/shard_map/ppermute | solution.py:362
  54.9 9.2 %collective-permute-start.2 = (bf16[4,4,24,384]{3,2,1,0:T(8,128)(2,1)S(1)}, bf16[4,4,24,384]{3,2,1,0:T(8,128)(2,1)S(1)}, u32[]{:S(2)}, u32[]{:S(2)}) collective-permute-start(bf16[4,4,24,384]{3,2,1,0:T(8,128)(2,1)S(1)} %bitcast.48), channel_id=1, source_target_pairs={{0,12},{4,0},{8,4},{12,8},{1,13},{5,1},{9,5},{13,9},{2,14},{6,2},{... | collective-permute-start | bytes 884744 | tf_op jit(solution)/shard_map/ppermute | solution.py:362
  56.4 13.3 %collective-permute-start.5 = (bf16[4,4,24,384]{3,2,1,0:T(8,128)(2,1)S(1)}, bf16[4,4,24,384]{3,2,1,0:T(8,128)(2,1)S(1)}, u32[]{:S(2)}, u32[]{:S(2)}) collective-permute-start(bf16[4,4,24,384]{3,2,1,0:T(8,128)(2,1)S(1)} %bitcast.44), channel_id=1, source_target_pairs={{0,4},{4,8},{8,12},{12,0},{1,5},{5,9},{9,13},{13,1},{2,6},{6,10},{... | collective-permute-start | bytes 884744 | tf_op jit(solution)/shard_map/ppermute | solution.py:362
  56.4 14.0 %collective-permute-start.6 = (bf16[4,4,24,384]{3,2,1,0:T(8,128)(2,1)S(1)}, bf16[4,4,24,384]{3,2,1,0:T(8,128)(2,1)S(1)}, u32[]{:S(2)}, u32[]{:S(2)}) collective-permute-start(bf16[4,4,24,384]{3,2,1,0:T(8,128)(2,1)S(1)} %bitcast.45), channel_id=1, source_target_pairs={{0,12},{4,0},{8,4},{12,8},{1,13},{5,1},{9,5},{13,9},{2,14},{6,2},{... | collective-permute-start | bytes 884744 | tf_op jit(solution)/shard_map/ppermute | solution.py:362
  63.4 7.8 %copy-start.10 = (bf16[4,4,24,384]{3,2,1,0:T(8,128)(2,1)}, bf16[4,4,24,384]{3,2,1,0:T(8,128)(2,1)S(1)}, u32[]{:S(2)}) copy-start(bf16[4,4,24,384]{3,2,1,0:T(8,128)(2,1)S(1)} %collective-permute-done.1.bp) | copy-start | bytes 884740
  64.1 15.3 %collective-permute-start.3 = (bf16[2,4,24,384]{3,2,1,0:T(8,128)(2,1)}, bf16[2,4,24,384]{3,2,1,0:T(8,128)(2,1)S(1)}, u32[]{:S(2)}, u32[]{:S(2)}) collective-permute-start(bf16[2,4,24,384]{3,2,1,0:T(8,128)(2,1)} %slice.43), channel_id=1, source_target_pairs={{0,4},{4,8},{8,12},{12,0},{1,5},{5,9},{9,13},{13,1},{2,6},{6,10},{... | collective-permute-start | bytes 442376 | tf_op jit(solution)/shard_map/ppermute | solution.py:362
  64.1 9.7 %copy-start.11 = (bf16[4,4,24,384]{3,2,1,0:T(8,128)(2,1)}, bf16[4,4,24,384]{3,2,1,0:T(8,128)(2,1)S(1)}, u32[]{:S(2)}) copy-start(bf16[4,4,24,384]{3,2,1,0:T(8,128)(2,1)S(1)} %collective-permute-done.2.bm) | copy-start | bytes 884740
  64.8 14.6 %collective-permute-start.4 = (bf16[2,4,24,384]{3,2,1,0:T(8,128)(2,1)}, bf16[2,4,24,384]{3,2,1,0:T(8,128)(2,1)}, u32[]{:S(2)}, u32[]{:S(2)}) collective-permute-start(bf16[2,4,24,384]{3,2,1,0:T(8,128)(2,1)} %slice.44), channel_id=1, source_target_pairs={{0,12},{4,0},{8,4},{12,8},{1,13},{5,1},{9,5},{13,9},{2,14},{6,2},{... | collective-permute-start | bytes 442376 | tf_op jit(solution)/shard_map/ppermute | solution.py:362
  69.7 20.5 %copy-start.8 = (bf16[4,4,24,384]{3,2,1,0:T(8,128)(2,1)}, bf16[4,4,24,384]{3,2,1,0:T(8,128)(2,1)S(1)}, u32[]{:S(2)}) copy-start(bf16[4,4,24,384]{3,2,1,0:T(8,128)(2,1)S(1)} %collective-permute-done.5.bp) | copy-start | bytes 884740
  70.4 19.8 %collective-permute-start.7 = (bf16[2,4,24,384]{3,2,1,0:T(8,128)(2,1)}, bf16[2,4,24,384]{3,2,1,0:T(8,128)(2,1)}, u32[]{:S(2)}, u32[]{:S(2)}) collective-permute-start(bf16[2,4,24,384]{3,2,1,0:T(8,128)(2,1)} %slice.46), channel_id=1, source_target_pairs={{0,4},{4,8},{8,12},{12,0},{1,5},{5,9},{9,13},{13,1},{2,6},{6,10},{... | collective-permute-start | bytes 442376 | tf_op jit(solution)/shard_map/ppermute | solution.py:362
  70.4 19.8 %copy-start.9 = (bf16[4,4,24,384]{3,2,1,0:T(8,128)(2,1)}, bf16[4,4,24,384]{3,2,1,0:T(8,128)(2,1)S(1)}, u32[]{:S(2)}) copy-start(bf16[4,4,24,384]{3,2,1,0:T(8,128)(2,1)S(1)} %collective-permute-done.6.bm) | copy-start | bytes 884740
  71.2 19.1 %collective-permute-start.8 = (bf16[2,4,24,384]{3,2,1,0:T(8,128)(2,1)}, bf16[2,4,24,384]{3,2,1,0:T(8,128)(2,1)}, u32[]{:S(2)}, u32[]{:S(2)}) collective-permute-start(bf16[2,4,24,384]{3,2,1,0:T(8,128)(2,1)} %slice.47), channel_id=1, source_target_pairs={{0,12},{4,0},{8,4},{12,8},{1,13},{5,1},{9,5},{13,9},{2,14},{6,2},{... | collective-permute-start | bytes 442376 | tf_op jit(solution)/shard_map/ppermute | solution.py:362
  74.5 1.0 copy-start.4
  90.2 10.5 %copy-start.7 = (bf16[4,2,96,128]{3,2,1,0:T(8,128)(2,1)S(1)}, bf16[4,2,96,128]{3,2,1,0:T(8,128)(2,1)}, u32[]{:S(2)}) copy-start(bf16[4,2,96,128]{3,2,1,0:T(8,128)(2,1)} %attend_0.1) | copy-start | bytes 589828
  100.7 7.9 %copy-start.15 = (bf16[256,32]{0,1:T(8,128)(2,1)S(1)}, bf16[256,32]{0,1:T(8,128)(2,1)}, u32[]{:S(2)}) copy-start(bf16[256,32]{0,1:T(8,128)(2,1)} %param.27) | copy-start | bytes 49156
  102.4 14.0 %all-to-all-start.2 = ((bf16[16,96,128]{2,1,0:T(8,128)(2,1)}), bf16[16,96,128]{2,1,0:T(8,128)(2,1)S(1)}, u32[]{:S(2)}, u32[]{:S(2)}) async-start(bf16[16,96,128]{2,1,0:T(8,128)(2,1)} %bitcast.13), calls=%async_computation.2 | async-start | bytes 786432 | tf_op jit(solution)/shard_map/all_to_all | solution.py:431
  121.9 23.5 %copy-start.16 = (s32[1536]{0:T(1024)S(1)}, s32[1536]{0:T(1024)}, u32[]{:S(2)}) copy-start(s32[1536]{0:T(1024)} %param.20) | copy-start | bytes 18436
  121.9 24.2 %copy-start.13 = (bf16[1024,128]{1,0:T(8,128)(2,1)S(1)}, bf16[1024,128]{1,0:T(8,128)(2,1)}, u32[]{:S(2)}) copy-start(bf16[1024,128]{1,0:T(8,128)(2,1)} %param.29) | copy-start | bytes 786436
  123.5 12.5 %all-to-all-start.3 = ((bf16[8,192,128]{2,1,0:T(8,128)(2,1)}), bf16[8,192,128]{2,1,0:T(8,128)(2,1)S(1)}, u32[]{:S(2)}, u32[]{:S(2)}) async-start(bf16[8,192,128]{2,1,0:T(8,128)(2,1)} %broadcast_in_dim.48), calls=%async_computation.3 | async-start | bytes 786432 | tf_op jit(solution)/shard_map/all_to_all | solution.py:366
  127.8 1.6 collective-permute-start.10
  129.4 0.7 collective-permute-start.11
  136.0 17.6 %copy-start.2 = (bf16[8,192,128]{2,1,0:T(8,128)(2,1)}, bf16[8,192,128]{2,1,0:T(8,128)(2,1)S(1)}, u32[]{:S(2)}) copy-start(bf16[8,192,128]{2,1,0:T(8,128)(2,1)S(1)} %all-to-all-done.3.lo_ref) | copy-start | bytes 1179652
  137.0 15.9 %all-to-all-start.4 = ((bf16[8,2,128,128]{3,2,1,0:T(8,128)(2,1)}), bf16[8,2,128,128]{3,2,1,0:T(8,128)(2,1)S(1)}, u32[]{:S(2)}, u32[]{:S(2)}) async-start(bf16[8,2,128,128]{3,2,1,0:T(8,128)(2,1)} %broadcast_in_dim.49), calls=%async_computation.4 | async-start | bytes 1048576 | tf_op jit(solution)/shard_map/all_to_all | solution.py:366
  144.2 8.6 %collective-permute-start.9 = (bf16[8,192,128]{2,1,0:T(8,128)(2,1)S(1)}, bf16[8,192,128]{2,1,0:T(8,128)(2,1)S(1)}, u32[]{:S(2)}, u32[]{:S(2)}) collective-permute-start(bf16[8,192,128]{2,1,0:T(8,128)(2,1)S(1)} %all-to-all-done.3.lo_ref), channel_id=1, source_target_pairs={{0,1},{1,0},{2,3},{3,2},{4,5},{5,4},{6,7},{7,6},{8,9},{9,8},{10,11... | collective-permute-start | bytes 1179656 | tf_op jit(solution)/shard_map/ppermute | solution.py:358
  152.8 1.0 copy-start.12
  (3 other events, 2.2 us)

commit v3 on v2

--- a/solution.py
+++ b/solution.py
@@ -97,29 +97,34 @@
     )(x, gain, w, expand, perm, present)
 
 
-def bias_kernel(z_ref, g_ref, a_ref, o_ref):
+def bias_kernel(z_ref, g_ref, w_ref, o_ref):
     acc = jnp.zeros((128, 4 * COLS), F32)
+    group = lax.broadcasted_iota(jnp.int32, (128, PAIR), 0) % 16
+    w = w_ref[...].astype(F32)
     for k in range(8):
         n = normalised(z_ref[768 * k : 768 * (k + 1)].astype(F32), g_ref[...])
         both = jnp.concatenate([n[:384], n[384:]], axis=1)
-        acc += mm_nt(a_ref[:, 256 * k : 256 * (k + 1)], both)
-    o_ref[...] = acc.astype(BF16).reshape(HEADS, 16, 4 * COLS)
-
-
-def pair_bias(z, gain, a):
+        spread = [jnp.where(group == 2 * k + e, w, 0.0).astype(BF16) for e in range(2)]
+        acc += mm_nt(jnp.concatenate(spread, axis=1), both)
+    out = acc.astype(BF16).reshape(HEADS, 16, 4 * COLS)
+    for copy in range(2):
+        o_ref[:, copy] = out
+
+
+def pair_bias(z, gain, w):
     return pl.pallas_call(
         bias_kernel,
-        out_shape=jax.ShapeDtypeStruct((HEADS, 2 * QUADS, 4 * COLS), BF16),
+        out_shape=jax.ShapeDtypeStruct((HEADS, 2, 2 * QUADS, 4 * COLS), BF16),
         grid=(3,),
         in_specs=[
             pl.BlockSpec((6144, PAIR), lambda t: (t, 0)),
             pl.BlockSpec((1, PAIR), lambda t: (0, 0)),
-            pl.BlockSpec((128, 2048), lambda t: (0, 0)),
+            pl.BlockSpec((128, PAIR), lambda t: (0, 0)),
         ],
-        out_specs=pl.BlockSpec((HEADS, 16, 4 * COLS), lambda t: (0, t, 0)),
+        out_specs=pl.BlockSpec((HEADS, 2, 16, 4 * COLS), lambda t: (0, 0, t, 0)),
         compiler_params=params(),
         name="pair_bias",
-    )(z, gain, a)
+    )(z, gain, w)
 
 
 OFFSETS = (0, 3, 1, 2)
@@ -163,10 +168,9 @@
 def attend_kernel(at_ref, k_ref, v_ref, q_ref, b0, bp, bm, f1, f2, o_ref, bias, even, odd):
     core = at_ref[1]
     count = CHUNK * HALF
-    for d, ref in enumerate((b0, bp, bm, (f1, f2))):
+    for d, refs in enumerate(((b0,), (bp,), (bm,), (f1, f2))):
         for r in range(CHUNK):
-            got = ref[r] if d < 3 else ref[r // 2][r % 2]
-            got = [got[k].astype(F32) * LOG2E for k in range(4)]
+            got = [ref[r, k].astype(F32) * LOG2E for ref in refs for k in range(4 // len(refs))]
             for u in range(4):
                 line = jnp.concatenate([g[:, COLS * u : COLS * (u + 1)] for g in got], axis=1)
                 top = r * HALF + u * QUADS
@@ -198,43 +202,51 @@
             acc = p if acc is None else acc + p
         return acc
 
-    for side in range(2):
-        top = scores(even, side, 0)
-        total = jnp.zeros((count, 256), F32)
-        for s in range(SEQS):
-            now, later = (even, odd) if s % 2 == 0 else (odd, even)
-            if s < SEQS - 1:
-                following = scores(later, side, s + 1)
-            total = jnp.where(wide == s, values(now, top, side), total)
-            if s < SEQS - 1:
-                top = following
-        out = (total[:, :128] / total[:, 128:]).astype(BF16)
-        quad = core if side == 0 else 1 - core
-        for r in range(CHUNK):
-            o_ref[r, quad] = out[HALF * r : HALF * (r + 1)]
-
-
-def attend(at, k, v, q, pieces, chunk):
+    top = scores(even, 0, 0)
+    for n in range(2 * SEQS):
+        side, s = divmod(n, SEQS)
+        now, later = (even, odd) if n % 2 == 0 else (odd, even)
+        if n < 2 * SEQS - 1:
+            following = scores(later, *divmod(n + 1, SEQS))
+        got = values(now, top, side)
+        total = got if s == 0 else jnp.where(wide == s, got, total)
+        if n < 2 * SEQS - 1:
+            top = following
+        if s == SEQS - 1:
+            out = (total[:, :128] / total[:, 128:]).astype(BF16)
+            quad = core if side == 0 else 1 - core
+            for r in range(CHUNK):
+                o_ref[r, quad] = out[HALF * r : HALF * (r + 1)]
+
+
+def attend(at, k, v, q, pieces):
+    def piece(parts):
+        return pl.BlockSpec((CHUNK, parts, QUADS, 4 * COLS), lambda t: (t, 0, 0, 0))
+
     return pl.pallas_call(
         attend_kernel,
-        out_shape=jax.ShapeDtypeStruct((CHUNK, 2, HALF, 128), BF16),
-        grid=(1,),
+        out_shape=jax.ShapeDtypeStruct((8, 2, HALF, 128), BF16),
+        grid=(8 // CHUNK,),
         in_specs=[
             smem(),
             pl.BlockSpec((2, EMB, TOTAL), lambda t: (0, 0, 0)),
             pl.BlockSpec((2, TOTAL, EMB), lambda t: (0, 0, 0)),
-            pl.BlockSpec((2, CHUNK, HALF, 128), lambda t: (0, chunk, 0, 0)),
-        ]
-        + [vmem()] * 5,
-        out_specs=pl.BlockSpec((CHUNK, 2, HALF, 128), lambda t: (0, 0, 0, 0)),
+            pl.BlockSpec((2, CHUNK, HALF, 128), lambda t: (0, t, 0, 0)),
+            piece(4),
+            piece(4),
+            piece(4),
+            piece(2),
+            piece(2),
+        ],
+        out_specs=pl.BlockSpec((CHUNK, 2, HALF, 128), lambda t: (t, 0, 0, 0)),
         scratch_shapes=[pltpu.VMEM((CHUNK * HALF, TOTAL), F32) for _ in range(3)],
         compiler_params=params(),
-        name=f"attend_{chunk}",
+        name="attend",
     )(at, k, v, q, *pieces)
 
 
 def finish_kernel(
-    att_ref, gate_ref, x_ref, wf_ref, pinv_ref, g_ref, wl_ref, wr_ref, ac_ref, ar_ref, new_ref, left_ref, right_ref
+    at_ref, att_ref, gate_ref, x_ref, wf_ref, pinv_ref, g_ref, wl_ref, wr_ref, ac_ref, ar_ref, new_ref, left_ref, near_ref, far_ref
 ):
     gated = jnp.concatenate(
         [(gate_ref[h] * att_ref[h].astype(F32)).astype(BF16) for h in range(HEADS)], axis=1
@@ -252,9 +264,13 @@
         left = jnp.where(slot_one == s, mm(n, wl_ref[...]), left)
         right = mm_nt(wr_ref[...], n) * ar_ref[s : s + 1]
         rows = slice(HEAD * s, HEAD * (s + 1))
-        right_ref[0, rows] = right[:, :128].astype(BF16)
-        right_ref[1, rows] = jnp.concatenate([right[:, COLS:], right[:, :32]], axis=1).astype(BF16)
-    left_ref[...] = (left * ac_ref[...]).astype(BF16)
+        halves = [right[:, :128], jnp.concatenate([right[:, COLS:], right[:, :32]], axis=1)]
+        first = at_ref[1] == 0
+        near_ref[rows] = jnp.where(first, halves[0], halves[1]).astype(BF16)
+        far_ref[rows] = jnp.where(first, halves[1], halves[0]).astype(BF16)
+    left = (left * ac_ref[...]).astype(BF16)
+    for copy in range(PEERS_COL // 2):
+        left_ref[copy] = left
 
 
 def finish(*args):
@@ -262,9 +278,11 @@
         finish_kernel,
         out_shape=(
             jax.ShapeDtypeStruct((SEQS, ROWS, EMB), BF16),
-            jax.ShapeDtypeStruct((ROWS, 128), BF16),
-            jax.ShapeDtypeStruct((2, 128, 128), BF16),
+            jax.ShapeDtypeStruct((PEERS_COL // 2, ROWS, 128), BF16),
+            jax.ShapeDtypeStruct((128, 128), BF16),
+            jax.ShapeDtypeStruct((128, 128), BF16),
         ),
+        in_specs=[smem()] + [vmem()] * 10,
         compiler_params=params(),
         name="finish",
     )(*args)
@@ -273,7 +291,7 @@
 STEP = 48
 
 
-def outer_kernel(at_ref, lo_ref, lp_ref, r_ref, w_ref, off_ref, ki_ref, kj_ref, z_ref, o_ref, l_all, r_all, lhs, rhs, obf):
+def outer_kernel(at_ref, lo_ref, lp_ref, r0, rp, rm, rt, w_ref, off_ref, ki_ref, kj_ref, z_ref, o_ref, l_all, r_all, lhs, rhs, obf):
     step = pl.program_id(0)
 
     @pl.when(step == 0)
@@ -283,8 +301,13 @@
             for side, ref in enumerate((lo_ref, lp_ref)):
                 c = 2 * p + (core if side == 0 else 1 - core)
                 l_all[pl.ds(pl.multiple_of(c * ROWS, ROWS), ROWS)] = ref[p].astype(F32)
-        for c in range(PEERS_COL):
-            r_all[128 * c : 128 * (c + 1)] = r_ref[c].astype(F32)
+        for d, ref in enumerate((r0, rp, rm, rt)):
+            y = lax.rem(at_ref[2] + OFFSETS[d], 4)
+            for e in range(2):
+                zh = at_ref[3] if e == 0 else 1 - at_ref[3]
+                for side in range(2):
+                    c = 4 * y + 2 * zh + (core if side == 0 else 1 - core)
+                    r_all[pl.ds(pl.multiple_of(c * 128, 128), 128)] = ref[e, side].astype(F32)
         for q in range(8):
             lines = [
                 r_all[pl.ds(HEAD * s + 4 * q + b, PEERS_COL, stride=128), :] for b in range(4) for s in range(SEQS)
@@ -313,7 +336,7 @@
         o_ref[k] = (z_ref[k].astype(F32) + update[COLS * k : COLS * (k + 1)] * keep).astype(BF16)
 
 
-def outer_update(at, left_own, left_par, right, w, offset, keep_i, keep_j, z):
+def outer_update(at, left_own, left_par, rights, w, offset, keep_i, keep_j, z):
     return pl.pallas_call(
         outer_kernel,
         out_shape=jax.ShapeDtypeStruct((ROWS, COLS, PAIR), BF16),
@@ -322,7 +345,9 @@
             smem(),
             pl.BlockSpec((PEERS_COL // 2, ROWS, 128), lambda t: (0, 0, 0)),
             pl.BlockSpec((PEERS_COL // 2, ROWS, 128), lambda t: (0, 0, 0)),
-            pl.BlockSpec((PEERS_COL, 128, 128), lambda t: (0, 0, 0)),
+        ]
+        + [pl.BlockSpec((2, 2, 128, 128), lambda t: (0, 0, 0, 0))] * 4
+        + [
             pl.BlockSpec((1024, PAIR), lambda t: (0, 0)),
             pl.BlockSpec((1, PAIR), lambda t: (0, 0)),
             smem(),
@@ -339,7 +364,7 @@
         ],
         compiler_params=params(),
         name="outer_update",
-    )(at, left_own, left_par, right, w, offset, keep_i, keep_j, z)
+    )(at, left_own, left_par, *rights, w, offset, keep_i, keep_j, z)
 
 
 def tables():
@@ -362,23 +387,32 @@
     return lax.ppermute(x, "y", [(a, (a + d) % 4) for a in range(4)])
 
 
-def to_all(x, axes, n):
-    return lax.all_to_all(jnp.broadcast_to(x[None], (n,) + x.shape), axes, 0, 0, tiled=True)
-
-
-def turn_grid(x):
-    def index(a, b, c, d):
-        return ((a * 2 + b) * 4 + c) * 2 + d
+def along_x(x, d):
+    return lax.ppermute(x, "x", [(a, (a + d) % 4) for a in range(4)])
+
+
+def swap_z(x):
+    return lax.ppermute(x, "zl", [(0, 1), (1, 0)])
+
+
+def turn_grid(x, cross):
+    def index(a, b, c, d, k):
+        return (((a * 2 + b) * 4 + c) * 2 + d) * 2 + k
 
     moves = [
-        (index(a, b, c, d), index(c, d, a, b)) for a in range(4) for b in range(2) for c in range(4) for d in range(2)
+        (index(a, b, c, d, k), index(c, d, a, b, k ^ cross))
+        for a in range(4)
+        for b in range(2)
+        for c in range(4)
+        for d in range(2)
+        for k in range(2)
     ]
-    return lax.ppermute(x, ("x", "zl", "y", "zh"), moves)
+    return lax.ppermute(x, ROW + COL, moves)
 
 
 def ring_pieces(block):
     up, down = along_y(block, 1), along_y(block, 3)
-    return block, up, down, along_y(up[: CHUNK // 2], 1), along_y(down[CHUNK // 2 :], 3)
+    return block, up, down, along_y(up[:, :2], 1), along_y(down[:, 2:], 3)
 
 
 def on_device(
@@ -398,16 +432,14 @@
     tensor_offset_vector,
 ):
     core = lax.axis_index("core")
-    at = jnp.stack([lax.axis_index("y"), core]).astype(jnp.int32)
+    at = jnp.stack([lax.axis_index(name) for name in ("y", "core", "x", "zl")]).astype(jnp.int32)
     expand, perm = tables()
 
-    spread = (
-        jnp.eye(16, dtype=BF16)[None, :, :, None] * coupling_logit_matrix.T[:, None, None, :]
-    ).reshape(HEADS * 16, 16 * PAIR)
     bias = pair_bias(
-        couplings_embedding.reshape(ROWS * COLS, PAIR), coupling_scaling_vector[None], spread
-    ).reshape(HEADS, 1, 2, QUADS, 4 * COLS)
-    bias = jnp.broadcast_to(bias, (HEADS, 2, 2, QUADS, 4 * COLS)).reshape(4 * HEADS, QUADS, 4 * COLS)
+        couplings_embedding.reshape(ROWS * COLS, PAIR),
+        coupling_scaling_vector[None],
+        jnp.repeat(coupling_logit_matrix.T, 16, axis=0),
+    ).reshape(4 * HEADS, QUADS, 4 * COLS)
     bias = lax.all_to_all(bias, ROW + ("zh", "core"), 0, 0, tiled=True).reshape(8, 4, QUADS, 4 * COLS)
 
     present = alignment_availability.astype(BF16)
@@ -422,16 +454,16 @@
         jnp.asarray(perm, BF16),
         sent_mask,
     )
+    own, bias = lax.optimization_barrier((own, bias))
     own = lax.all_to_all(own, ROW, 0, 0, tiled=True)
+    pieces = ring_pieces(bias)
     k, v, q = prepare(at, own, swap_cores(own))
-
-    attended = jnp.concatenate(
-        [attend(at, k, v, q, ring_pieces(bias[CHUNK * c : CHUNK * (c + 1)]), c) for c in range(2)], axis=0
-    ).reshape(16, HALF, 128)
+    attended = attend(at, k, v, q, pieces).reshape(16, HALF, 128)
     attended = lax.all_to_all(attended, ROW + ("core",), 0, 0, tiled=True).reshape(HEADS, ROWS, 128)
 
     present = alignment_availability.astype(F32)
-    alignment_refreshed, left, right = finish(
+    alignment_refreshed, left, near, far = finish(
+        at,
         attended,
         gate,
         alignment_embedding,
@@ -443,11 +475,10 @@
         jnp.repeat(present.T, HEAD, axis=1),
         present,
     )
-    mine = lax.dynamic_index_in_dim(right, core, 0, False)
-    theirs = swap_cores(lax.dynamic_index_in_dim(right, 1 - core, 0, False))
-    right = jnp.where(core == 0, jnp.stack([mine, theirs]), jnp.stack([theirs, mine]))
-    right = to_all(turn_grid(right), ROW, 8).reshape(PEERS_COL, 128, 128)
-    left = to_all(left, ("y", "zh"), 8)
+    left = lax.all_to_all(left, ("y", "zh"), 0, 0, tiled=True)
+    right = jnp.stack([turn_grid(near, 0), turn_grid(far, 1)])
+    right = jnp.stack([right, swap_z(right)])
+    rights = [right] + [along_x(right, d) for d in (1, 3, 2)]
 
     keep = amino_availability.astype(F32)
     keep_i = lax.dynamic_slice_in_dim(keep, lax.axis_index(ROW) * ROWS, ROWS)
@@ -458,7 +489,7 @@
         at,
         left,
         swap_cores(left),
-        right,
+        rights,
         projection,
         tensor_offset_vector[None],
         keep_i,

time: 182 us -> 179 us (0.984)
  blocking collectives: 0 us -> 20 us
  waiting for transfers between devices: 46.4 us -> 33.4 us
  local copies, waits for them, and re-layouts: 15.8 us -> 8.2 us
  Pallas kernels: 70.4 us -> 67.6 us
  starting transfers between devices: 42.7 us -> 45.4 us
  other arithmetic: 4.48 us -> 1.89 us
    all_to_all x3 -> x1, waiting for transfers between devices: 20.3 us -> 0.01 us  [on_device(): left = lax.all_to_all(left, ('y', 'zh'), 0, 0, tiled=True)]
    all_to_all x0 -> x1, blocking collectives: none -> 20 us  [on_device(): own = lax.all_to_all(own, ROW, 0, 0, tiled=True)]
    ppermute x1 -> x6, starting transfers between devices: 0.66 us -> 18.5 us  [the longest x3 8.55 us: along_x(): return lax.ppermute(x, 'x', [(a, (a + d) % 4) for a in range(4)])]
    all_to_all x3 -> x1, starting transfers between devices: 16.9 us -> 4.82 us  [on_device(): left = lax.all_to_all(left, ('y', 'zh'), 0, 0, tiled=True)]
    ppermute x8 -> x4, waiting for transfers between devices: 6.45 us -> 14.8 us  [along_y(): return lax.ppermute(x, 'y', [(a, (a + d) % 4) for a in range(4)])]
    all_to_all x1, waiting for transfers between devices: 11.6 us -> 4.46 us  [on_device(): lax.all_to_all(bias, ROW + ('zh', 'core'), 0, 0, tiled=True)]
    ppermute x1 -> x6, waiting for transfers between devices: 0.01 us -> 7.03 us  [the longest x3 5.25 us: along_x(): return lax.ppermute(x, 'x', [(a, (a + d) % 4) for a in range(4)])]
    ppermute x8 -> x4, starting transfers between devices: 10.9 us -> 5.42 us  [along_y(): return lax.ppermute(x, 'y', [(a, (a + d) % 4) for a in range(4)])]
  transfers between devices with their start and end apart: 17 -> 15, of which waited for: 8 -> 8; matrix products, arithmetic and copies ran while one was open for 5% -> 4% of each run, Pallas kernels for 12% -> 6%
where the time goes in v3:
time: 179 us; the launch traced here: 177 us
  Pallas kernels  67.6 us (38%)
  starting transfers between devices  45.4 us (25%)
  waiting for transfers between devices  33.4 us (19%)
  blocking collectives  20 us (11%)
  local copies, waits for them, and re-layouts  8.2 us (5%)
  other arithmetic  1.89 us (1%)
    pallas_call x1, Pallas kernels, outer_update(): pl.pallas_call(outer_kernel, out_shape=jax.ShapeDtypeStruct((ROWS, COLS,...  27 us
    all_to_all x1, blocking collectives, on_device(): own = lax.all_to_all(own, ROW, 0, 0, tiled=True)  20 us
    pallas_call x1, Pallas kernels, attend(): pl.pallas_call(attend_kernel, out_shape=jax.ShapeDtypeStruct((8, 2, HALF,...  17.6 us
    ppermute x4, waiting for transfers between devices, along_y(): return lax.ppermute(x, 'y', [(a, (a + d) % 4) for a in range(4)])  14.8 us
    all_to_all x1, starting transfers between devices, on_device(): lax.all_to_all(bias, ROW + ('zh', 'core'), 0, 0, tiled=True)  9.43 us
    ppermute x3, starting transfers between devices, along_x(): return lax.ppermute(x, 'x', [(a, (a + d) % 4) for a in range(4)])  8.55 us
    pallas_call x1, Pallas kernels, pair_bias(): pl.pallas_call(bias_kernel, out_shape=jax.ShapeDtypeStruct((HEADS, 2, 2 *...  8.14 us
    ppermute x1, starting transfers between devices, swap_z(): return lax.ppermute(x, 'zl', [(0, 1), (1, 0)])  7.52 us
  transfers between devices with their start and end apart: 15, of which 8 were waited for; matrix products, arithmetic and copies ran while one was open for 4% of the time, Pallas kernels for 6%

profile of v3, /device:TPU:1, one launch (start us, length us, event | category | flops | bytes accessed | tf_op | source)
XLA Modules:
  0.0 177.4 jit_solution(12082249988466030631)
XLA Ops:
  0.6 1.3 broadcast_in_dim.26
  1.9 8.1 %pair_bias.1 = bf16[8,2,48,384]{3,2,1,0:T(8,128)(2,1)} custom-call(bf16[18432,128]{1,0:T(8,128)(2,1)} %bitcast.35, f32[1,128]{1,0:T(1,128)} %bitcast.54, bf16[128,128]{1,0:T(8,128)(2,1)} %bitcast.46), custom_call_target="tpu_custom_call" | custom-call | tf_op jit(solution)/shard_map/pair_bias/pallas_call | solution.py:115
  10.1 9.4 %all-to-all-start = ((bf16[32,24,384]{2,1,0:T(8,128)(2,1)}), bf16[32,24,384]{2,1,0:T(8,128)(2,1)S(1)}, u32[]{:S(2)}, u32[]{:S(2)}) async-start(bf16[32,24,384]{2,1,0:T(8,128)(2,1)} %bitcast.39), calls=%async_computation | async-start | bytes 1179648 | tf_op jit(solution)/shard_map/all_to_all | solution.py:443
  20.7 6.3 %project.1 = (bf16[8,592,128]{2,1,0:T(8,128)(2,1)}, f32[8,192,128]{2,1,0:T(8,128)}) custom-call(bf16[4,192,256]{2,1,0:T(8,128)(2,1)} %x_ref.3, f32[1,256]{1,0:T(1,128)} %bitcast.53, bf16[256,1024]{1,0:T(8,128)(2,1)} %w_ref.1, bf16[128,512]{1,0:T(8,128)(2,1)} %constant.42.clone.e_ref, bf16[192,192]{1,0:T(8,128)(2,1)} %constant.43.clone.p_ref, ...), custom_call_target="tpu_custom_call" | custom-call | tf_op jit(solution)/shard_map/project/pallas_call | solution.py:89
  27.0 4.5 %all-to-all-done = bf16[32,24,384]{2,1,0:T(8,128)(2,1)S(1)} async-done(((bf16[32,24,384]{2,1,0:T(8,128)(2,1)}), bf16[32,24,384]{2,1,0:T(8,128)(2,1)S(1)}, u32[]{:S(2)}, u32[]{:S(2)}) %all-to-all-start) | async-done | bytes 589856 | tf_op jit(solution)/shard_map/all_to_all | solution.py:443
  31.5 20.0 %all_to_all.20.own_ref = bf16[8,592,128]{2,1,0:T(8,128)(2,1)S(1)} all-to-all(bf16[8,592,128]{2,1,0:T(8,128)(2,1)} %get-tuple-element.14), channel_id=1, replica_groups=mesh['x'=4,'zl'=2,'y'=4,'zh'=2,'core'=2] {'x','zl'}, dimensions={0} | all-to-all | bytes 2424832 | tf_op jit(solution)/shard_map/all_to_all | solution.py:458
  51.5 1.6 collective-permute-start
  53.1 1.3 collective-permute-start.1
  54.4 1.4 collective-permute-start.2
  55.9 13.6 %collective-permute-done.1.bp = bf16[8,4,24,384]{3,2,1,0:T(8,128)(2,1)S(1)} collective-permute-done((bf16[8,4,24,384]{3,2,1,0:T(8,128)(2,1)S(1)}, bf16[8,4,24,384]{3,2,1,0:T(8,128)(2,1)S(1)}, u32[]{:S(2)}, u32[]{:S(2)}) %collective-permute-start.1) | collective-permute-done | bytes 589856 | tf_op jit(solution)/shard_map/ppermute | solution.py:387
  69.4 0.8 slice.18
  70.2 0.8 slice.19
  71.0 2.7 %collective-permute-start.4 = (bf16[8,2,24,384]{3,2,1,0:T(8,128)(2,1)}, bf16[8,2,24,384]{3,2,1,0:T(8,128)(2,1)}, u32[]{:S(2)}, u32[]{:S(2)}) collective-permute-start(bf16[8,2,24,384]{3,2,1,0:T(8,128)(2,1)} %slice.19), channel_id=1, source_target_pairs={{0,12},{4,0},{8,4},{12,8},{1,13},{5,1},{9,5},{13,9},{2,14},{6,2},{... | collective-permute-start | bytes 884744 | tf_op jit(solution)/shard_map/ppermute | solution.py:387
  74.3 3.9 %prepare.1 = (bf16[2,256,1536]{2,1,0:T(8,128)(2,1)}, bf16[2,1536,256]{2,1,0:T(8,128)(2,1)}, bf16[2,8,96,128]{3,2,1,0:T(8,128)(2,1)}) custom-call(s32[4]{0:T(128)} %pad_add_fusion.at_ref, bf16[8,592,128]{2,1,0:T(8,128)(2,1)} %copy-done, bf16[8,592,128]{2,1,0:T(8,128)(2,1)} %collective-permute-done.par_ref), custom_call_target="tpu_custom_call" | custom-call | tf_op jit(solution)/shard_map/prepare/pallas_call | solution.py:154
  78.3 1.2 collective-permute-done.3.f1
  80.2 17.6 %attend.1 = bf16[8,2,96,128]{3,2,1,0:T(8,128)(2,1)} custom-call(s32[4]{0:T(128)} %pad_add_fusion.at_ref, bf16[2,256,1536]{2,1,0:T(8,128)(2,1)} %get-tuple-element.15.k_ref, bf16[2,1536,256]{2,1,0:T(8,128)(2,1)} %get-tuple-element.16.v_ref, bf16[2,8,96,128]{3,2,1,0:T(8,128)(2,1)} %get-tuple-element.17.q_ref, bf16[8,4,24,384]{3,2,1,0:T(8,128)(2,1)} %bitcast.38, ...), custom_call_target="tpu_custom_call" | custom-call | tf_op jit(solution)/shard_map/attend/pallas_call | solution.py:226
  97.8 4.9 %all-to-all-start.2 = ((bf16[16,96,128]{2,1,0:T(8,128)(2,1)}), bf16[16,96,128]{2,1,0:T(8,128)(2,1)S(1)}, u32[]{:S(2)}, u32[]{:S(2)}) async-start(bf16[16,96,128]{2,1,0:T(8,128)(2,1)} %bitcast.40), calls=%async_computation.2 | async-start | bytes 786432 | tf_op jit(solution)/shard_map/all_to_all | solution.py:462
  104.2 7.1 %all-to-all-done.2 = bf16[16,96,128]{2,1,0:T(8,128)(2,1)S(1)} async-done(((bf16[16,96,128]{2,1,0:T(8,128)(2,1)}), bf16[16,96,128]{2,1,0:T(8,128)(2,1)S(1)}, u32[]{:S(2)}, u32[]{:S(2)}) %all-to-all-start.2) | async-done | bytes 393248 | tf_op jit(solution)/shard_map/all_to_all | solution.py:462
  112.1 4.7 %finish.1 = (bf16[4,192,256]{2,1,0:T(8,128)(2,1)}, bf16[8,192,128]{2,1,0:T(8,128)(2,1)}, bf16[128,128]{1,0:T(8,128)(2,1)}, bf16[128,128]{1,0:T(8,128)(2,1)}) custom-call(s32[4]{0:T(128)} %pad_add_fusion.at_ref, bf16[8,192,128]{2,1,0:T(8,128)(2,1)} %bitcast.41, f32[8,192,128]{2,1,0:T(8,128)} %get-tuple-element.19.gate_ref, bf16[4,192,256]{2,1,0:T(8,128)(2,1)} %x_ref.3, ...), custom_call_target="tpu_custom_call" | custom-call | tf_op jit(solution)/shard_map/finish/pallas_call | solution.py:277
  116.8 4.8 %all-to-all-start.3 = ((bf16[8,192,128]{2,1,0:T(8,128)(2,1)}), bf16[8,192,128]{2,1,0:T(8,128)(2,1)S(1)}, u32[]{:S(2)}, u32[]{:S(2)}) async-start(bf16[8,192,128]{2,1,0:T(8,128)(2,1)} %get-tuple-element.21), calls=%async_computation.3 | async-start | bytes 786432 | tf_op jit(solution)/shard_map/all_to_all | solution.py:478
  121.7 1.4 collective-permute-start.6
  123.1 1.1 collective-permute-start.7
  124.1 1.1 collective-permute-done.7
  125.2 7.5 %collective-permute-start.8 = (bf16[2,128,128]{2,1,0:T(8,128)(2,1)S(1)}, bf16[2,128,128]{2,1,0:T(8,128)(2,1)S(1)}, u32[]{:S(2)}, u32[]{:S(2)}) collective-permute-start(bf16[2,128,128]{2,1,0:T(8,128)(2,1)S(1)} %get-tuple-element.25), channel_id=1, source_target_pairs={{0,16},{16,0},{1,17},{17,1},{2,18},{18,2},{3,19},{19,3},{4,20},{20... | collective-permute-start | bytes 196616 | tf_op jit(solution)/shard_map/ppermute | solution.py:395
  134.9 6.6 %collective-permute-start.10 = (bf16[2,2,128,128]{3,2,1,0:T(8,128)(2,1)S(1)}, bf16[2,2,128,128]{3,2,1,0:T(8,128)(2,1)S(1)}, u32[]{:S(2)}, u32[]{:S(2)}) collective-permute-start(bf16[2,2,128,128]{3,2,1,0:T(8,128)(2,1)S(1)} %pad_maximum_fusion.r0), channel_id=1, source_target_pairs={{0,96},{32,0},{64,32},{96,64},{1,97},{33,1},{65,33},{97,65},{2,98}... | collective-permute-start | bytes 393224 | tf_op jit(solution)/shard_map/ppermute | solution.py:391
  141.5 1.1 collective-permute-start.11
  142.7 0.8 collective-permute-start.9
  143.5 0.8 copy.24
  144.3 2.6 %collective-permute-done.11.rt = bf16[2,2,128,128]{3,2,1,0:T(8,128)(2,1)S(1)} collective-permute-done((bf16[2,2,128,128]{3,2,1,0:T(8,128)(2,1)S(1)}, bf16[2,2,128,128]{3,2,1,0:T(8,128)(2,1)S(1)}, u32[]{:S(2)}, u32[]{:S(2)}) %collective-permute-start.11) | collective-permute-done | bytes 131104 | tf_op jit(solution)/shard_map/ppermute | solution.py:391
  146.9 2.6 %collective-permute-done.9.rp = bf16[2,2,128,128]{3,2,1,0:T(8,128)(2,1)S(1)} collective-permute-done((bf16[2,2,128,128]{3,2,1,0:T(8,128)(2,1)S(1)}, bf16[2,2,128,128]{3,2,1,0:T(8,128)(2,1)S(1)}, u32[]{:S(2)}, u32[]{:S(2)}) %collective-permute-start.9) | collective-permute-done | bytes 131104 | tf_op jit(solution)/shard_map/ppermute | solution.py:391
  149.6 0.8 broadcast_in_dim.30.kj_ref
  150.4 27.0 %outer_update.1 = bf16[192,96,128]{2,1,0:T(8,128)(2,1)} custom-call(s32[4]{0:T(128)} %pad_add_fusion.at_ref, bf16[8,192,128]{2,1,0:T(8,128)(2,1)} %copy-done.2, bf16[8,192,128]{2,1,0:T(8,128)(2,1)} %copy-done.7, bf16[2,2,128,128]{3,2,1,0:T(8,128)(2,1)} %copy-done.6, bf16[2,2,128,128]{3,2,1,0:T(8,128)(2,1)} %copy-done.12, ...), custom_call_target="tpu_custom_call" | custom-call | tf_op jit(solution)/shard_map/outer_update/pallas_call | solution.py:340
  (57 shorter events, 7.0 us)
Async XLA Ops:
  1.9 17.6 %copy-start.15 = (s32[4,192]{1,0:T(4,128)S(1)}, s32[4,192]{1,0:T(4,128)}, u32[]{:S(2)}) copy-start(s32[4,192]{1,0:T(4,128)} %param.19) | copy-start | bytes 9220
  10.1 21.4 %all-to-all-start = ((bf16[32,24,384]{2,1,0:T(8,128)(2,1)}), bf16[32,24,384]{2,1,0:T(8,128)(2,1)S(1)}, u32[]{:S(2)}, u32[]{:S(2)}) async-start(bf16[32,24,384]{2,1,0:T(8,128)(2,1)} %bitcast.39), calls=%async_computation | async-start | bytes 1179648 | tf_op jit(solution)/shard_map/all_to_all | solution.py:443
  31.5 39.6 %copy-start.1 = (bf16[32,24,384]{2,1,0:T(8,128)(2,1)}, bf16[32,24,384]{2,1,0:T(8,128)(2,1)S(1)}, u32[]{:S(2)}) copy-start(bf16[32,24,384]{2,1,0:T(8,128)(2,1)S(1)} %all-to-all-done) | copy-start | bytes 1769476
  51.5 22.8 %copy-start = (bf16[8,592,128]{2,1,0:T(8,128)(2,1)}, bf16[8,592,128]{2,1,0:T(8,128)(2,1)S(1)}, u32[]{:S(2)}) copy-start(bf16[8,592,128]{2,1,0:T(8,128)(2,1)S(1)} %all_to_all.20.own_ref) | copy-start | bytes 3637252
  51.5 22.8 %collective-permute-start = (bf16[8,592,128]{2,1,0:T(8,128)(2,1)S(1)}, bf16[8,592,128]{2,1,0:T(8,128)(2,1)}, u32[]{:S(2)}, u32[]{:S(2)}) collective-permute-start(bf16[8,592,128]{2,1,0:T(8,128)(2,1)S(1)} %all_to_all.20.own_ref), channel_id=1, source_target_pairs={{0,1},{1,0},{2,3},{3,2},{4,5},{5,4},{6,7},{7,6},{8,9},{9,8},{10,11... | collective-permute-start | bytes 3637256 | tf_op jit(solution)/shard_map/ppermute | solution.py:383
  53.1 16.3 %collective-permute-start.1 = (bf16[8,4,24,384]{3,2,1,0:T(8,128)(2,1)S(1)}, bf16[8,4,24,384]{3,2,1,0:T(8,128)(2,1)S(1)}, u32[]{:S(2)}, u32[]{:S(2)}) collective-permute-start(bf16[8,4,24,384]{3,2,1,0:T(8,128)(2,1)S(1)} %bitcast.36), channel_id=1, source_target_pairs={{0,4},{4,8},{8,12},{12,0},{1,5},{5,9},{9,13},{13,1},{2,6},{6,10},{... | collective-permute-start | bytes 1769480 | tf_op jit(solution)/shard_map/ppermute | solution.py:387
  54.4 15.8 %collective-permute-start.2 = (bf16[8,4,24,384]{3,2,1,0:T(8,128)(2,1)S(1)}, bf16[8,4,24,384]{3,2,1,0:T(8,128)(2,1)S(1)}, u32[]{:S(2)}, u32[]{:S(2)}) collective-permute-start(bf16[8,4,24,384]{3,2,1,0:T(8,128)(2,1)S(1)} %bitcast.37), channel_id=1, source_target_pairs={{0,12},{4,0},{8,4},{12,8},{1,13},{5,1},{9,5},{13,9},{2,14},{6,2},{... | collective-permute-start | bytes 1769480 | tf_op jit(solution)/shard_map/ppermute | solution.py:387
  69.4 8.8 %copy-start.4 = (bf16[8,4,24,384]{3,2,1,0:T(8,128)(2,1)}, bf16[8,4,24,384]{3,2,1,0:T(8,128)(2,1)S(1)}, u32[]{:S(2)}) copy-start(bf16[8,4,24,384]{3,2,1,0:T(8,128)(2,1)S(1)} %collective-permute-done.1.bp) | copy-start | bytes 1769476
  70.2 9.3 %collective-permute-start.3 = (bf16[8,2,24,384]{3,2,1,0:T(8,128)(2,1)}, bf16[8,2,24,384]{3,2,1,0:T(8,128)(2,1)S(1)}, u32[]{:S(2)}, u32[]{:S(2)}) collective-permute-start(bf16[8,2,24,384]{3,2,1,0:T(8,128)(2,1)} %slice.18), channel_id=1, source_target_pairs={{0,4},{4,8},{8,12},{12,0},{1,5},{5,9},{9,13},{13,1},{2,6},{6,10},{... | collective-permute-start | bytes 884744 | tf_op jit(solution)/shard_map/ppermute | solution.py:387
  70.2 9.3 %copy-start.5 = (bf16[8,4,24,384]{3,2,1,0:T(8,128)(2,1)}, bf16[8,4,24,384]{3,2,1,0:T(8,128)(2,1)S(1)}, u32[]{:S(2)}) copy-start(bf16[8,4,24,384]{3,2,1,0:T(8,128)(2,1)S(1)} %collective-permute-done.2.bm) | copy-start | bytes 1769476
  71.0 8.4 %collective-permute-start.4 = (bf16[8,2,24,384]{3,2,1,0:T(8,128)(2,1)}, bf16[8,2,24,384]{3,2,1,0:T(8,128)(2,1)}, u32[]{:S(2)}, u32[]{:S(2)}) collective-permute-start(bf16[8,2,24,384]{3,2,1,0:T(8,128)(2,1)} %slice.19), channel_id=1, source_target_pairs={{0,12},{4,0},{8,4},{12,8},{1,13},{5,1},{9,5},{13,9},{2,14},{6,2},{... | collective-permute-start | bytes 884744 | tf_op jit(solution)/shard_map/ppermute | solution.py:387
  79.5 0.7 copy-start.8
  80.2 23.3 %copy-start.13 = (bf16[256,32]{0,1:T(8,128)(2,1)S(1)}, bf16[256,32]{0,1:T(8,128)(2,1)}, u32[]{:S(2)}) copy-start(bf16[256,32]{0,1:T(8,128)(2,1)} %param.27) | copy-start | bytes 49156
  97.8 13.6 %all-to-all-start.2 = ((bf16[16,96,128]{2,1,0:T(8,128)(2,1)}), bf16[16,96,128]{2,1,0:T(8,128)(2,1)S(1)}, u32[]{:S(2)}, u32[]{:S(2)}) async-start(bf16[16,96,128]{2,1,0:T(8,128)(2,1)} %bitcast.40), calls=%async_computation.2 | async-start | bytes 786432 | tf_op jit(solution)/shard_map/all_to_all | solution.py:462
  103.5 29.9 %copy-start.14 = (s32[1536]{0:T(1024)S(1)}, s32[1536]{0:T(1024)}, u32[]{:S(2)}) copy-start(s32[1536]{0:T(1024)} %param.20) | copy-start | bytes 18436
  111.3 0.7 copy-start.3
  112.1 31.4 %copy-start.9 = (bf16[1024,128]{1,0:T(8,128)(2,1)S(1)}, bf16[1024,128]{1,0:T(8,128)(2,1)}, u32[]{:S(2)}) copy-start(bf16[1024,128]{1,0:T(8,128)(2,1)} %param.29) | copy-start | bytes 786436
  116.8 15.9 %all-to-all-start.3 = ((bf16[8,192,128]{2,1,0:T(8,128)(2,1)}), bf16[8,192,128]{2,1,0:T(8,128)(2,1)S(1)}, u32[]{:S(2)}, u32[]{:S(2)}) async-start(bf16[8,192,128]{2,1,0:T(8,128)(2,1)} %get-tuple-element.21), calls=%async_computation.3 | async-start | bytes 786432 | tf_op jit(solution)/shard_map/all_to_all | solution.py:478
  121.7 2.5 %collective-permute-start.6 = (bf16[128,128]{1,0:T(8,128)(2,1)}, bf16[128,128]{1,0:T(8,128)(2,1)S(1)}, u32[]{:S(2)}, u32[]{:S(2)}) collective-permute-start(bf16[128,128]{1,0:T(8,128)(2,1)} %get-tuple-element.22), channel_id=1, source_target_pairs={{0,0},{1,1},{2,16},{3,17},{4,32},{5,33},{6,48},{7,49},{8,64},{9,65... | collective-permute-start | bytes 98312 | tf_op jit(solution)/shard_map/ppermute | solution.py:410
  123.1 2.1 %collective-permute-start.7 = (bf16[128,128]{1,0:T(8,128)(2,1)}, bf16[128,128]{1,0:T(8,128)(2,1)S(1)}, u32[]{:S(2)}, u32[]{:S(2)}) collective-permute-start(bf16[128,128]{1,0:T(8,128)(2,1)} %get-tuple-element.23), channel_id=1, source_target_pairs={{0,1},{1,0},{2,17},{3,16},{4,33},{5,32},{6,49},{7,48},{8,65},{9,64... | collective-permute-start | bytes 98312 | tf_op jit(solution)/shard_map/ppermute | solution.py:410
  125.2 9.7 %collective-permute-start.8 = (bf16[2,128,128]{2,1,0:T(8,128)(2,1)S(1)}, bf16[2,128,128]{2,1,0:T(8,128)(2,1)S(1)}, u32[]{:S(2)}, u32[]{:S(2)}) collective-permute-start(bf16[2,128,128]{2,1,0:T(8,128)(2,1)S(1)} %get-tuple-element.25), channel_id=1, source_target_pairs={{0,16},{16,0},{1,17},{17,1},{2,18},{18,2},{3,19},{19,3},{4,20},{20... | collective-permute-start | bytes 196616 | tf_op jit(solution)/shard_map/ppermute | solution.py:395
  132.7 17.6 %copy-start.2 = (bf16[8,192,128]{2,1,0:T(8,128)(2,1)}, bf16[8,192,128]{2,1,0:T(8,128)(2,1)S(1)}, u32[]{:S(2)}) copy-start(bf16[8,192,128]{2,1,0:T(8,128)(2,1)S(1)} %all-to-all-done.3.lo_ref) | copy-start | bytes 1179652
  132.7 16.8 %collective-permute-start.5 = (bf16[8,192,128]{2,1,0:T(8,128)(2,1)S(1)}, bf16[8,192,128]{2,1,0:T(8,128)(2,1)S(1)}, u32[]{:S(2)}, u32[]{:S(2)}) collective-permute-start(bf16[8,192,128]{2,1,0:T(8,128)(2,1)S(1)} %all-to-all-done.3.lo_ref), channel_id=1, source_target_pairs={{0,1},{1,0},{2,3},{3,2},{4,5},{5,4},{6,7},{7,6},{8,9},{9,8},{10,11... | collective-permute-start | bytes 1179656 | tf_op jit(solution)/shard_map/ppermute | solution.py:383
  134.9 15.5 %copy-start.6 = (bf16[2,2,128,128]{3,2,1,0:T(8,128)(2,1)}, bf16[2,2,128,128]{3,2,1,0:T(8,128)(2,1)S(1)}, u32[]{:S(2)}) copy-start(bf16[2,2,128,128]{3,2,1,0:T(8,128)(2,1)S(1)} %pad_maximum_fusion.r0) | copy-start | bytes 393220
  134.9 9.4 %collective-permute-start.10 = (bf16[2,2,128,128]{3,2,1,0:T(8,128)(2,1)S(1)}, bf16[2,2,128,128]{3,2,1,0:T(8,128)(2,1)S(1)}, u32[]{:S(2)}, u32[]{:S(2)}) collective-permute-start(bf16[2,2,128,128]{3,2,1,0:T(8,128)(2,1)S(1)} %pad_maximum_fusion.r0), channel_id=1, source_target_pairs={{0,96},{32,0},{64,32},{96,64},{1,97},{33,1},{65,33},{97,65},{2,98}... | collective-permute-start | bytes 393224 | tf_op jit(solution)/shard_map/ppermute | solution.py:391
  141.5 5.4 %collective-permute-start.11 = (bf16[2,2,128,128]{3,2,1,0:T(8,128)(2,1)S(1)}, bf16[2,2,128,128]{3,2,1,0:T(8,128)(2,1)S(1)}, u32[]{:S(2)}, u32[]{:S(2)}) collective-permute-start(bf16[2,2,128,128]{3,2,1,0:T(8,128)(2,1)S(1)} %pad_maximum_fusion.r0), channel_id=1, source_target_pairs={{0,64},{32,96},{64,0},{96,32},{1,65},{33,97},{65,1},{97,33},{2,66}... | collective-permute-start | bytes 393224 | tf_op jit(solution)/shard_map/ppermute | solution.py:391
  142.7 6.9 %collective-permute-start.9 = (bf16[2,2,128,128]{3,2,1,0:T(8,128)(2,1)S(1)}, bf16[2,2,128,128]{3,2,1,0:T(8,128)(2,1)S(1)}, u32[]{:S(2)}, u32[]{:S(2)}) collective-permute-start(bf16[2,2,128,128]{3,2,1,0:T(8,128)(2,1)S(1)} %pad_maximum_fusion.r0), channel_id=1, source_target_pairs={{0,32},{32,64},{64,96},{96,0},{1,33},{33,65},{65,97},{97,1},{2,34}... | collective-permute-start | bytes 393224 | tf_op jit(solution)/shard_map/ppermute | solution.py:391
  144.3 6.1 %copy-start.10 = (bf16[2,2,128,128]{3,2,1,0:T(8,128)(2,1)}, bf16[2,2,128,128]{3,2,1,0:T(8,128)(2,1)S(1)}, u32[]{:S(2)}) copy-start(bf16[2,2,128,128]{3,2,1,0:T(8,128)(2,1)S(1)} %collective-permute-done.10.rm) | copy-start | bytes 393220
  146.9 3.5 %copy-start.11 = (bf16[2,2,128,128]{3,2,1,0:T(8,128)(2,1)}, bf16[2,2,128,128]{3,2,1,0:T(8,128)(2,1)S(1)}, u32[]{:S(2)}) copy-start(bf16[2,2,128,128]{3,2,1,0:T(8,128)(2,1)S(1)} %collective-permute-done.11.rt) | copy-start | bytes 393220
  149.6 0.8 copy-start.12
  149.6 0.8 copy-start.7

commit v4 on v3

--- a/solution.py
+++ b/solution.py
@@ -19,21 +19,21 @@
 PAIR = 128
 PEERS_COL = 16
 TOTAL = 1536
-CHUNK = 4
+CHUNK = 2
+BIAS_AT = 48
 Q_ROWS, K_ROWS, V_ROWS, M_ROWS = 0, 192, 384, 576
 SENT_ROWS = 592
 LOG2E = 1.4426950408889634
 ROW = ("x", "zl")
 COL = ("y", "zh", "core")
-VMEM_LIMIT = 56 * 1024 * 1024
 
 
 def mm(a, b):
     return jnp.dot(a, b, preferred_element_type=F32)
 
 
-def mm_nt(a, b):
-    return lax.dot_general(a, b, (((1,), (1,)), ((), ())), preferred_element_type=F32)
+def mm_tn(a, b):
+    return lax.dot_general(a, b, (((0,), (0,)), ((), ())), preferred_element_type=F32)
 
 
 def normalised(x, gain):
@@ -47,8 +47,8 @@
     return (lax.broadcasted_iota(jnp.int32, shape, len(shape) - 1) // HEAD) % 4
 
 
-def params():
-    return pltpu.CompilerParams(vmem_limit_bytes=VMEM_LIMIT)
+def params(mib):
+    return pltpu.CompilerParams(vmem_limit_bytes=mib * 1024 * 1024)
 
 
 def vmem():
@@ -92,21 +92,23 @@
             jax.ShapeDtypeStruct((HEADS, SENT_ROWS, 128), BF16),
             jax.ShapeDtypeStruct((HEADS, ROWS, 128), F32),
         ),
-        compiler_params=params(),
+        compiler_params=params(24),
         name="project",
     )(x, gain, w, expand, perm, present)
 
 
 def bias_kernel(z_ref, g_ref, w_ref, o_ref):
-    acc = jnp.zeros((128, 4 * COLS), F32)
-    group = lax.broadcasted_iota(jnp.int32, (128, PAIR), 0) % 16
-    w = w_ref[...].astype(F32)
+    acc = jnp.zeros((4 * COLS, 128), F32)
+    head = lax.broadcasted_iota(jnp.int32, (HEADS, 128), 0)
+    lane = lax.broadcasted_iota(jnp.int32, (HEADS, 128), 1)
+    w = mm_tn(w_ref[...], jnp.where(lane // 16 == head, 1.0, 0.0).astype(BF16))
+    group = lax.broadcasted_iota(jnp.int32, (PAIR, 128), 1) % 16
     for k in range(8):
         n = normalised(z_ref[768 * k : 768 * (k + 1)].astype(F32), g_ref[...])
         both = jnp.concatenate([n[:384], n[384:]], axis=1)
         spread = [jnp.where(group == 2 * k + e, w, 0.0).astype(BF16) for e in range(2)]
-        acc += mm_nt(jnp.concatenate(spread, axis=1), both)
-    out = acc.astype(BF16).reshape(HEADS, 16, 4 * COLS)
+        acc += mm(both, jnp.concatenate(spread, axis=0))
+    out = jnp.transpose(acc).astype(BF16).reshape(HEADS, 16, 4 * COLS)
     for copy in range(2):
         o_ref[:, copy] = out
 
@@ -119,10 +121,10 @@
         in_specs=[
             pl.BlockSpec((6144, PAIR), lambda t: (t, 0)),
             pl.BlockSpec((1, PAIR), lambda t: (0, 0)),
-            pl.BlockSpec((128, PAIR), lambda t: (0, 0)),
+            pl.BlockSpec((HEADS, PAIR), lambda t: (0, 0)),
         ],
         out_specs=pl.BlockSpec((HEADS, 2, 16, 4 * COLS), lambda t: (0, 0, t, 0)),
-        compiler_params=params(),
+        compiler_params=params(60),
         name="pair_bias",
     )(z, gain, w)
 
@@ -144,7 +146,10 @@
             masks = [ref[first + e, M_ROWS:].astype(F32) for e in range(2)]
             line = jnp.concatenate([masks[0][:8], masks[0][8:, :64], masks[1][:8], masks[1][8:, :64]], axis=1)
             absent = (line - 1.0) * 1000000000.0
-            k_ref[side, 128:, span] = jnp.concatenate([absent, jnp.zeros((120, 384), F32)], axis=0).astype(BF16)
+            rows = []
+            for s in range(SEQS):
+                rows += [absent[s : s + 1], jnp.zeros((15, 384), F32)]
+            k_ref[side, 128:192, span] = jnp.concatenate(rows, axis=0).astype(BF16)
         v_ref[side, :, 128:] = jnp.ones((TOTAL, 128), BF16)
         for r in range(8):
             q_ref[side, r] = ref[r, pl.ds(pl.multiple_of(core * HALF, HALF), HALF)]
@@ -154,60 +159,64 @@
     return pl.pallas_call(
         prepare_kernel,
         out_shape=(
-            jax.ShapeDtypeStruct((2, EMB, TOTAL), BF16),
+            jax.ShapeDtypeStruct((2, 192, TOTAL), BF16),
             jax.ShapeDtypeStruct((2, TOTAL, EMB), BF16),
             jax.ShapeDtypeStruct((2, 8, HALF, 128), BF16),
         ),
         in_specs=[smem(), vmem(), vmem()],
         out_specs=(vmem(), vmem(), vmem()),
-        compiler_params=params(),
+        compiler_params=params(24),
         name="prepare",
     )(at, own, par)
 
 
-def attend_kernel(at_ref, k_ref, v_ref, q_ref, b0, bp, bm, f1, f2, o_ref, bias, even, odd):
+def attend_kernel(at_ref, k_ref, v_ref, q_ref, b0, bp, bm, f1, f2, o_ref, rhs_even, rhs_odd, even, odd):
     core = at_ref[1]
     count = CHUNK * HALF
     for d, refs in enumerate(((b0,), (bp,), (bm,), (f1, f2))):
         for r in range(CHUNK):
-            got = [ref[r, k].astype(F32) * LOG2E for ref in refs for k in range(4 // len(refs))]
-            for u in range(4):
-                line = jnp.concatenate([g[:, COLS * u : COLS * (u + 1)] for g in got], axis=1)
-                top = r * HALF + u * QUADS
-                bias[top : top + QUADS, 384 * d : 384 * (d + 1)] = line
-    slot = slot_of((count, 128))
+            got = [ref[r, k].astype(F32) for ref in refs for k in range(4 // len(refs))]
+            lines = [
+                jnp.concatenate([g[:, COLS * u : COLS * (u + 1)] for g in got], axis=1) for u in range(4)
+            ]
+            block = jnp.concatenate(lines, axis=0).astype(BF16)
+            for rhs in (rhs_even, rhs_odd):
+                rhs[BIAS_AT + HALF * r : BIAS_AT + HALF * (r + 1), 384 * d : 384 * (d + 1)] = block
+    for rhs in (rhs_even, rhs_odd):
+        rhs[BIAS_AT + count :] = jnp.zeros((EMB - BIAS_AT - count, TOTAL), BF16)
     wide = slot_of((count, 256))
-    lane = lax.broadcasted_iota(jnp.int32, (count, 128), 1)
-
-    def scores(out, side, s):
+    lane = lax.broadcasted_iota(jnp.int32, (count, 256), 1)
+    row = lax.broadcasted_iota(jnp.int32, (count, 256), 0)
+    pick = jnp.where((lane == HEAD) | (lane == row + BIAS_AT), 1.0, 0.0)
+    first = lane[:, :128] < HEAD
+    tail = pick[:, 128:].astype(BF16)
+
+    def scores(out, rhs, side, s):
+        rhs[:HEAD] = k_ref[side, HEAD * s : HEAD * (s + 1)]
+        rhs[HEAD:BIAS_AT] = k_ref[side, 128 + 16 * s : 128 + 16 * (s + 1)]
         q = jnp.concatenate([q_ref[side, r] for r in range(CHUNK)], axis=0).astype(F32)
-        lhs = jnp.concatenate(
-            [jnp.where(slot == s, q, 0.0).astype(BF16), jnp.where(lane == s, 1.0, 0.0).astype(BF16)], axis=1
-        )
+        if s:
+            q = pltpu.roll(q, 128 - HEAD * s, 1)
+        lhs = jnp.concatenate([jnp.where(first, q, pick[:, :128]).astype(BF16), tail], axis=1)
         top = None
         for t in range(6):
             span = slice(256 * t, 256 * (t + 1))
-            c = mm(lhs, k_ref[side, :, span]) * LOG2E + bias[:, span]
+            c = mm(lhs, rhs[:, span])
             out[:, span] = c
             both = jnp.maximum(c[:, :128], c[:, 128:])
             top = both if top is None else jnp.maximum(top, both)
         return jnp.max(top, axis=1, keepdims=True)
 
     def values(buf, top, side):
-        acc = None
-        for t in range(6):
-            span = slice(256 * t, 256 * (t + 1))
-            e = jnp.exp2(buf[:, span] - top).astype(BF16)
-            p = mm(e, v_ref[side, span])
-            acc = p if acc is None else acc + p
-        return acc
-
-    top = scores(even, 0, 0)
+        e = jnp.exp(buf[...] - top).astype(BF16)
+        return mm(e, v_ref[side])
+
+    top = scores(even, rhs_even, 0, 0)
     for n in range(2 * SEQS):
         side, s = divmod(n, SEQS)
-        now, later = (even, odd) if n % 2 == 0 else (odd, even)
+        now, later, rhs = (even, odd, rhs_odd) if n % 2 == 0 else (odd, even, rhs_even)
         if n < 2 * SEQS - 1:
-            following = scores(later, *divmod(n + 1, SEQS))
+            following = scores(later, rhs, *divmod(n + 1, SEQS))
         got = values(now, top, side)
         total = got if s == 0 else jnp.where(wide == s, got, total)
         if n < 2 * SEQS - 1:
@@ -229,7 +238,7 @@
         grid=(8 // CHUNK,),
         in_specs=[
             smem(),
-            pl.BlockSpec((2, EMB, TOTAL), lambda t: (0, 0, 0)),
+            pl.BlockSpec((2, 192, TOTAL), lambda t: (0, 0, 0)),
             pl.BlockSpec((2, TOTAL, EMB), lambda t: (0, 0, 0)),
             pl.BlockSpec((2, CHUNK, HALF, 128), lambda t: (0, t, 0, 0)),
             piece(4),
@@ -239,14 +248,14 @@
             piece(2),
         ],
         out_specs=pl.BlockSpec((CHUNK, 2, HALF, 128), lambda t: (t, 0, 0, 0)),
-        scratch_shapes=[pltpu.VMEM((CHUNK * HALF, TOTAL), F32) for _ in range(3)],
-        compiler_params=params(),
+        scratch_shapes=[pltpu.VMEM((EMB, TOTAL), BF16)] * 2 + [pltpu.VMEM((CHUNK * HALF, TOTAL), F32)] * 2,
+        compiler_params=params(28),
         name="attend",
     )(at, k, v, q, *pieces)
 
 
 def finish_kernel(
-    at_ref, att_ref, gate_ref, x_ref, wf_ref, pinv_ref, g_ref, wl_ref, wr_ref, ac_ref, ar_ref, new_ref, left_ref, near_ref, far_ref
+    at_ref, att_ref, gate_ref, x_ref, wf_ref, pinv_ref, g_ref, wl_ref, wr_ref, ac_ref, new_ref, left_ref, near_ref, far_ref
 ):
     gated = jnp.concatenate(
         [(gate_ref[h] * att_ref[h].astype(F32)).astype(BF16) for h in range(HEADS)], axis=1
@@ -256,18 +265,18 @@
     slot = slot_of((ROWS, 4 * EMB))
     slot_one = slot_of((ROWS, 128))
     left = jnp.zeros((ROWS, 128), F32)
+    right = jnp.zeros((ROWS, 128), F32)
     for s in range(SEQS):
         inc = mm(jnp.where(slot == s, gated, 0.0).astype(BF16), w)
         new = (x_ref[s].astype(F32) + inc).astype(BF16)
         new_ref[s] = new
         n = normalised(new.astype(F32), g_ref[...])
         left = jnp.where(slot_one == s, mm(n, wl_ref[...]), left)
-        right = mm_nt(wr_ref[...], n) * ar_ref[s : s + 1]
-        rows = slice(HEAD * s, HEAD * (s + 1))
-        halves = [right[:, :128], jnp.concatenate([right[:, COLS:], right[:, :32]], axis=1)]
-        first = at_ref[1] == 0
-        near_ref[rows] = jnp.where(first, halves[0], halves[1]).astype(BF16)
-        far_ref[rows] = jnp.where(first, halves[1], halves[0]).astype(BF16)
+        right = jnp.where(slot_one == s, mm(n, wr_ref[...]), right)
+    right = right * ac_ref[...]
+    first = at_ref[1] == 0
+    near_ref[...] = jnp.where(first, right[:HALF], right[HALF:]).astype(BF16)
+    far_ref[...] = jnp.where(first, right[HALF:], right[:HALF]).astype(BF16)
     left = (left * ac_ref[...]).astype(BF16)
     for copy in range(PEERS_COL // 2):
         left_ref[copy] = left
@@ -279,11 +288,11 @@
         out_shape=(
             jax.ShapeDtypeStruct((SEQS, ROWS, EMB), BF16),
             jax.ShapeDtypeStruct((PEERS_COL // 2, ROWS, 128), BF16),
-            jax.ShapeDtypeStruct((128, 128), BF16),
-            jax.ShapeDtypeStruct((128, 128), BF16),
+            jax.ShapeDtypeStruct((HALF, 128), BF16),
+            jax.ShapeDtypeStruct((HALF, 128), BF16),
         ),
-        in_specs=[smem()] + [vmem()] * 10,
-        compiler_params=params(),
+        in_specs=[smem()] + [vmem()] * 9,
+        compiler_params=params(24),
         name="finish",
     )(*args)
 
@@ -291,7 +300,35 @@
 STEP = 48
 
 
-def outer_kernel(at_ref, lo_ref, lp_ref, r0, rp, rm, rt, w_ref, off_ref, ki_ref, kj_ref, z_ref, o_ref, l_all, r_all, lhs, rhs, obf):
+def columns_kernel(at_ref, r_ref, o_ref, r_all):
+    core = at_ref[1]
+    pad = jnp.zeros((128 - COLS, 128), F32)
+    for p in range(PEERS_COL // 2):
+        for side in range(2):
+            c = 2 * p + (core if side == 0 else 1 - core)
+            turned = jnp.transpose(jnp.concatenate([r_ref[p, side].astype(F32), pad], axis=0))
+            r_all[pl.ds(pl.multiple_of(c * 128, 128), 128)] = turned
+    for q in range(8):
+        lines = [
+            r_all[pl.ds(HEAD * s + 4 * q + b, PEERS_COL, stride=128), :] for b in range(4) for s in range(SEQS)
+        ]
+        turned = jnp.transpose(jnp.concatenate(lines, axis=0))
+        o_ref[COLS * q : COLS * (q + 1)] = turned[:COLS].astype(BF16)
+
+
+def columns(at, right):
+    return pl.pallas_call(
+        columns_kernel,
+        out_shape=jax.ShapeDtypeStruct((8 * COLS, EMB), BF16),
+        in_specs=[smem(), vmem()],
+        out_specs=vmem(),
+        scratch_shapes=[pltpu.VMEM((PEERS_COL * 128, 128), F32)],
+        compiler_params=params(16),
+        name="columns",
+    )(at, right)
+
+
+def outer_kernel(at_ref, lo_ref, lp_ref, lhs, w_ref, off_ref, ki_ref, kj_ref, z_ref, o_ref, l_all, rhs, obf):
     step = pl.program_id(0)
 
     @pl.when(step == 0)
@@ -301,19 +338,6 @@
             for side, ref in enumerate((lo_ref, lp_ref)):
                 c = 2 * p + (core if side == 0 else 1 - core)
                 l_all[pl.ds(pl.multiple_of(c * ROWS, ROWS), ROWS)] = ref[p].astype(F32)
-        for d, ref in enumerate((r0, rp, rm, rt)):
-            y = lax.rem(at_ref[2] + OFFSETS[d], 4)
-            for e in range(2):
-                zh = at_ref[3] if e == 0 else 1 - at_ref[3]
-                for side in range(2):
-                    c = 4 * y + 2 * zh + (core if side == 0 else 1 - core)
-                    r_all[pl.ds(pl.multiple_of(c * 128, 128), 128)] = ref[e, side].astype(F32)
-        for q in range(8):
-            lines = [
-                r_all[pl.ds(HEAD * s + 4 * q + b, PEERS_COL, stride=128), :] for b in range(4) for s in range(SEQS)
-            ]
-            turned = jnp.transpose(jnp.concatenate(lines, axis=0))
-            lhs[COLS * q : COLS * (q + 1)] = turned[:COLS].astype(BF16)
 
     slot = slot_of((PEERS_COL, 128))
     for k in range(STEP):
@@ -336,7 +360,7 @@
         o_ref[k] = (z_ref[k].astype(F32) + update[COLS * k : COLS * (k + 1)] * keep).astype(BF16)
 
 
-def outer_update(at, left_own, left_par, rights, w, offset, keep_i, keep_j, z):
+def outer_update(at, left_own, left_par, right, w, offset, keep_i, keep_j, z):
     return pl.pallas_call(
         outer_kernel,
         out_shape=jax.ShapeDtypeStruct((ROWS, COLS, PAIR), BF16),
@@ -345,9 +369,7 @@
             smem(),
             pl.BlockSpec((PEERS_COL // 2, ROWS, 128), lambda t: (0, 0, 0)),
             pl.BlockSpec((PEERS_COL // 2, ROWS, 128), lambda t: (0, 0, 0)),
-        ]
-        + [pl.BlockSpec((2, 2, 128, 128), lambda t: (0, 0, 0, 0))] * 4
-        + [
+            pl.BlockSpec((8 * COLS, EMB), lambda t: (0, 0)),
             pl.BlockSpec((1024, PAIR), lambda t: (0, 0)),
             pl.BlockSpec((1, PAIR), lambda t: (0, 0)),
             smem(),
@@ -357,14 +379,12 @@
         out_specs=pl.BlockSpec((STEP, COLS, PAIR), lambda t: (t, 0, 0)),
         scratch_shapes=[
             pltpu.VMEM((PEERS_COL * ROWS, 128), F32),
-            pltpu.VMEM((PEERS_COL * 128, 128), F32),
-            pltpu.VMEM((8 * COLS, 256), BF16),
             pltpu.VMEM((256, 128 * STEP), BF16),
             pltpu.VMEM((STEP * COLS, 1024), BF16),
         ],
-        compiler_params=params(),
+        compiler_params=params(60),
         name="outer_update",
-    )(at, left_own, left_par, *rights, w, offset, keep_i, keep_j, z)
+    )(at, left_own, left_par, right, w, offset, keep_i, keep_j, z)
 
 
 def tables():
@@ -387,14 +407,6 @@
     return lax.ppermute(x, "y", [(a, (a + d) % 4) for a in range(4)])
 
 
-def along_x(x, d):
-    return lax.ppermute(x, "x", [(a, (a + d) % 4) for a in range(4)])
-
-
-def swap_z(x):
-    return lax.ppermute(x, "zl", [(0, 1), (1, 0)])
-
-
 def turn_grid(x, cross):
     def index(a, b, c, d, k):
         return (((a * 2 + b) * 4 + c) * 2 + d) * 2 + k
@@ -410,9 +422,8 @@
     return lax.ppermute(x, ROW + COL, moves)
 
 
-def ring_pieces(block):
-    up, down = along_y(block, 1), along_y(block, 3)
-    return block, up, down, along_y(up[:, :2], 1), along_y(down[:, 2:], 3)
+def to_all(x, axes, n):
+    return lax.all_to_all(jnp.broadcast_to(x[None], (n,) + x.shape), axes, 0, 0, tiled=True)
 
 
 def on_device(
@@ -432,16 +443,20 @@
     tensor_offset_vector,
 ):
     core = lax.axis_index("core")
-    at = jnp.stack([lax.axis_index(name) for name in ("y", "core", "x", "zl")]).astype(jnp.int32)
+    at = jnp.stack([lax.axis_index(name) for name in ("y", "core")]).astype(jnp.int32)
     expand, perm = tables()
 
     bias = pair_bias(
         couplings_embedding.reshape(ROWS * COLS, PAIR),
         coupling_scaling_vector[None],
-        jnp.repeat(coupling_logit_matrix.T, 16, axis=0),
+        coupling_logit_matrix.T,
     ).reshape(4 * HEADS, QUADS, 4 * COLS)
     bias = lax.all_to_all(bias, ROW + ("zh", "core"), 0, 0, tiled=True).reshape(8, 4, QUADS, 4 * COLS)
 
+    keep = amino_availability.astype(F32)
+    keep_i = lax.dynamic_slice_in_dim(keep, lax.axis_index(ROW) * ROWS, ROWS)
+    keep_j = lax.dynamic_slice_in_dim(keep, lax.axis_index(COL) * COLS, COLS)
+    keep_j = jnp.broadcast_to(keep_j[:, None], (COLS, PAIR))
     present = alignment_availability.astype(BF16)
     sent_mask = jnp.pad(
         jnp.stack([present[:, :128], jnp.pad(present[:, 128:], ((0, 0), (0, 64)))]), ((0, 0), (0, 4), (0, 0))
@@ -454,9 +469,11 @@
         jnp.asarray(perm, BF16),
         sent_mask,
     )
-    own, bias = lax.optimization_barrier((own, bias))
+    own, bias, at, keep_i, keep_j = lax.optimization_barrier((own, bias, at, keep_i, keep_j))
+    up, down = along_y(bias, 1), along_y(bias, 3)
     own = lax.all_to_all(own, ROW, 0, 0, tiled=True)
-    pieces = ring_pieces(bias)
+    own = lax.optimization_barrier((own, up, down))[0]
+    pieces = (bias, up, down, along_y(up[:, :2], 1), along_y(down[:, 2:], 3))
     k, v, q = prepare(at, own, swap_cores(own))
     attended = attend(at, k, v, q, pieces).reshape(16, HALF, 128)
     attended = lax.all_to_all(attended, ROW + ("core",), 0, 0, tiled=True).reshape(HEADS, ROWS, 128)
@@ -471,29 +488,24 @@
         jnp.asarray(perm.T, BF16),
         tensor_scaling_vector[None],
         jnp.tile(first_factor_matrix, (1, 4)),
-        second_factor_matrix.T,
+        jnp.tile(second_factor_matrix, (1, 4)),
         jnp.repeat(present.T, HEAD, axis=1),
-        present,
     )
     left = lax.all_to_all(left, ("y", "zh"), 0, 0, tiled=True)
     right = jnp.stack([turn_grid(near, 0), turn_grid(far, 1)])
-    right = jnp.stack([right, swap_z(right)])
-    rights = [right] + [along_x(right, d) for d in (1, 3, 2)]
-
-    keep = amino_availability.astype(F32)
-    keep_i = lax.dynamic_slice_in_dim(keep, lax.axis_index(ROW) * ROWS, ROWS)
-    keep_j = lax.dynamic_slice_in_dim(keep, lax.axis_index(COL) * COLS, COLS)
+    right = columns(at, to_all(right, ROW, 8))
+
     projection = (tensor_projection_matrix.astype(F32) / 64).astype(BF16)
     projection = projection.reshape(HEAD, 8, 4, PAIR).transpose(1, 2, 0, 3).reshape(1024, PAIR)
     couplings_refreshed = outer_update(
         at,
         left,
         swap_cores(left),
-        rights,
+        right,
         projection,
         tensor_offset_vector[None],
         keep_i,
-        jnp.broadcast_to(keep_j[:, None], (COLS, PAIR)),
+        keep_j,
         couplings_embedding,
     )
     return alignment_refreshed, couplings_refreshed

time: 179 us -> 158 us (0.88)
  blocking collectives: 20 us -> 0 us
  waiting for transfers between devices: 33.4 us -> 47.2 us
  Pallas kernels: 67.6 us -> 59.8 us
  starting transfers between devices: 45.4 us -> 41.4 us
  local copies, waits for them, and re-layouts: 8.2 us -> 5.89 us
    all_to_all x1 -> x0, blocking collectives: 20 us -> none  [on_device(): own = lax.all_to_all(own, ROW, 0, 0, tiled=True)]
    ppermute x4 -> x0, starting transfers between devices: 16.1 us -> none  [the longest x3 8.55 us: along_x(): return lax.ppermute(x, 'x', [(a, (a + d) % 4) for a in range(4)])]
    all_to_all x0 -> x2, starting transfers between devices: none -> 11.7 us  [the longest x1 8.15 us: to_all(): lax.all_to_all(jnp.broadcast_to(x[None], (n,) + x.shape), axes, 0, 0, til...]
    all_to_all x0 -> x2, waiting for transfers between devices: none -> 8.44 us  [the longest x1 5.49 us: to_all(): lax.all_to_all(jnp.broadcast_to(x[None], (n,) + x.shape), axes, 0, 0, til...]
    all_to_all x1, waiting for transfers between devices: 0.01 us -> 6.01 us  [on_device(): left = lax.all_to_all(left, ('y', 'zh'), 0, 0, tiled=True)]
    ppermute x4 -> x0, waiting for transfers between devices: 5.96 us -> none  [the longest x3 5.25 us: along_x(): return lax.ppermute(x, 'x', [(a, (a + d) % 4) for a in range(4)])]
    ppermute x4, waiting for transfers between devices: 14.8 us -> 19.1 us  [along_y(): return lax.ppermute(x, 'y', [(a, (a + d) % 4) for a in range(4)])]
    pallas_call x1, Pallas kernels: 17.6 us -> 14.3 us  [attend(): pl.pallas_call(attend_kernel, out_shape=jax.ShapeDtypeStruct((8, 2, HALF,...]
  transfers between devices with their start and end apart: 15 -> 13, of which waited for: 8 -> 7; matrix products, arithmetic and copies ran while one was open for 4% -> 2% of each run, Pallas kernels for 6% -> 5%
where the time goes in v4:
time: 158 us; the launch traced here: 155 us
  Pallas kernels  59.8 us (38%)
  waiting for transfers between devices  47.2 us (30%)
  starting transfers between devices  41.4 us (26%)
  local copies, waits for them, and re-layouts  5.89 us (4%)
    pallas_call x1, Pallas kernels, outer_update(): pl.pallas_call(outer_kernel, out_shape=jax.ShapeDtypeStruct((ROWS, COLS,...  26.1 us
    ppermute x4, waiting for transfers between devices, along_y(): return lax.ppermute(x, 'y', [(a, (a + d) % 4) for a in range(4)])  19.1 us
    pallas_call x1, Pallas kernels, attend(): pl.pallas_call(attend_kernel, out_shape=jax.ShapeDtypeStruct((8, 2, HALF,...  14.3 us
    all_to_all x1, starting transfers between devices, on_device(): lax.all_to_all(bias, ROW + ('zh', 'core'), 0, 0, tiled=True)  9.57 us
    pallas_call x1, Pallas kernels, pair_bias(): pl.pallas_call(bias_kernel, out_shape=jax.ShapeDtypeStruct((HEADS, 2, 2 *...  8.24 us
    all_to_all x1, waiting for transfers between devices, on_device(): lax.all_to_all(attended, ROW + ('core',), 0, 0, tiled=True)  8.24 us
    all_to_all x1, starting transfers between devices, to_all(): lax.all_to_all(jnp.broadcast_to(x[None], (n,) + x.shape), axes, 0, 0, til...  8.15 us
    all_to_all x1, waiting for transfers between devices, on_device(): left = lax.all_to_all(left, ('y', 'zh'), 0, 0, tiled=True)  6.01 us
  transfers between devices with their start and end apart: 13, of which 7 were waited for; matrix products, arithmetic and copies ran while one was open for 2% of the time, Pallas kernels for 5%

profile of v4, /device:TPU:1, one launch (start us, length us, event | category | flops | bytes accessed | tf_op | source)
XLA Modules:
  0.0 155.4 jit_solution(4262524223295748551)
XLA Ops:
  0.6 8.2 %pair_bias.1 = bf16[8,2,48,384]{3,2,1,0:T(8,128)(2,1)} custom-call(bf16[18432,128]{1,0:T(8,128)(2,1)} %bitcast.35, f32[1,128]{1,0:T(1,128)} %bitcast.45, bf16[8,128]{1,0:T(8,128)(2,1)} %bitcast.44), custom_call_target="tpu_custom_call" | custom-call | tf_op jit(solution)/shard_map/pair_bias/pallas_call | solution.py:117
  8.9 9.6 %all-to-all-start = ((bf16[32,24,384]{2,1,0:T(8,128)(2,1)}), bf16[32,24,384]{2,1,0:T(8,128)(2,1)S(1)}, u32[]{:S(2)}, u32[]{:S(2)}) async-start(bf16[32,24,384]{2,1,0:T(8,128)(2,1)} %bitcast.36), calls=%async_computation | async-start | bytes 1179648 | tf_op jit(solution)/shard_map/all_to_all | solution.py:454
  19.4 4.8 %project.1 = (bf16[8,592,128]{2,1,0:T(8,128)(2,1)}, f32[8,192,128]{2,1,0:T(8,128)S(1)}) custom-call(bf16[4,192,256]{2,1,0:T(8,128)(2,1)S(1)} %copy-done.1, f32[1,256]{1,0:T(1,128)S(1)} %bitcast.34, bf16[256,1024]{1,0:T(8,128)(2,1)S(1)} %copy-done.4, bf16[128,512]{1,0:T(8,128)(2,1)S(1)} %copy-done.6, bf16[192,192]{1,0:T(8,128)(2,1)S(1)} %copy-done.8, ...), custom_call_target="tpu_custom_call" | custom-call | tf_op jit(solution)/shard_map/project/pallas_call | solution.py:89
  24.2 0.9 copy-done.2
  25.1 5.4 %all-to-all-done = bf16[32,24,384]{2,1,0:T(8,128)(2,1)S(1)} async-done(((bf16[32,24,384]{2,1,0:T(8,128)(2,1)}), bf16[32,24,384]{2,1,0:T(8,128)(2,1)S(1)}, u32[]{:S(2)}, u32[]{:S(2)}) %all-to-all-start) | async-done | bytes 589856 | tf_op jit(solution)/shard_map/all_to_all | solution.py:454
  30.5 0.7 broadcast_in_dim.29.kj_ref
  31.2 3.6 %all-to-all-start.1 = ((bf16[8,592,128]{2,1,0:T(8,128)(2,1)}), bf16[8,592,128]{2,1,0:T(8,128)(2,1)S(1)}, u32[]{:S(2)}, u32[]{:S(2)}) async-start(bf16[8,592,128]{2,1,0:T(8,128)(2,1)} %get-tuple-element.19), calls=%async_computation.1 | async-start | bytes 2424832 | tf_op jit(solution)/shard_map/all_to_all | solution.py:474
  34.8 1.4 collective-permute-start
  36.1 1.5 collective-permute-start.1
  37.6 13.3 %collective-permute-done.bp = bf16[8,4,24,384]{3,2,1,0:T(8,128)(2,1)S(1)} collective-permute-done((bf16[8,4,24,384]{3,2,1,0:T(8,128)(2,1)S(1)}, bf16[8,4,24,384]{3,2,1,0:T(8,128)(2,1)S(1)}, u32[]{:S(2)}, u32[]{:S(2)}) %collective-permute-start) | collective-permute-done | bytes 589856 | tf_op jit(solution)/shard_map/ppermute | solution.py:407
  50.9 2.9 %all-to-all-done.1.own_ref = bf16[8,592,128]{2,1,0:T(8,128)(2,1)S(1)} async-done(((bf16[8,592,128]{2,1,0:T(8,128)(2,1)}), bf16[8,592,128]{2,1,0:T(8,128)(2,1)S(1)}, u32[]{:S(2)}, u32[]{:S(2)}) %all-to-all-start.1) | async-done | bytes 1212448 | tf_op jit(solution)/shard_map/all_to_all | solution.py:474
  53.8 1.0 collective-permute-start.2
  54.9 1.4 collective-permute-start.3
  56.3 1.7 %collective-permute-start.4 = (bf16[8,2,24,384]{3,2,1,0:T(8,128)(2,1)S(1)}, bf16[8,2,24,384]{3,2,1,0:T(8,128)(2,1)S(1)}, u32[]{:S(2)}, u32[]{:S(2)}) collective-permute-start(bf16[8,2,24,384]{3,2,1,0:T(8,128)(2,1)S(1)} %slice.19), channel_id=1, source_target_pairs={{0,12},{4,0},{8,4},{12,8},{1,13},{5,1},{9,5},{13,9},{2,14},{6,2},{... | collective-permute-start | bytes 884744 | tf_op jit(solution)/shard_map/ppermute | solution.py:407
  58.0 1.1 prepare.1
  59.1 5.9 %collective-permute-done.3.f1 = bf16[8,2,24,384]{3,2,1,0:T(8,128)(2,1)S(1)} collective-permute-done((bf16[8,2,24,384]{3,2,1,0:T(8,128)(2,1)S(1)}, bf16[8,2,24,384]{3,2,1,0:T(8,128)(2,1)S(1)}, u32[]{:S(2)}, u32[]{:S(2)}) %collective-permute-start.3) | collective-permute-done | bytes 294944 | tf_op jit(solution)/shard_map/ppermute | solution.py:407
  65.0 14.3 %attend.1 = bf16[8,2,96,128]{3,2,1,0:T(8,128)(2,1)} custom-call(s32[2]{0:T(128)S(1)} %pad_add_fusion.at_ref, bf16[2,192,1536]{2,1,0:T(8,128)(2,1)S(1)} %get-tuple-element.22.k_ref, bf16[2,1536,256]{2,1,0:T(8,128)(2,1)S(1)} %get-tuple-element.23.v_ref, bf16[2,8,96,128]{3,2,1,0:T(8,128)(2,1)S(1)} %get-tuple-element.24.q_ref, ...), custom_call_target="tpu_custom_call" | custom-call | tf_op jit(solution)/shard_map/attend/pallas_call | solution.py:235
  79.3 4.5 %all-to-all-start.2 = ((bf16[16,96,128]{2,1,0:T(8,128)(2,1)}), bf16[16,96,128]{2,1,0:T(8,128)(2,1)S(1)}, u32[]{:S(2)}, u32[]{:S(2)}) async-start(bf16[16,96,128]{2,1,0:T(8,128)(2,1)} %bitcast.11), calls=%async_computation.2 | async-start | bytes 786432 | tf_op jit(solution)/shard_map/all_to_all | solution.py:479
  84.2 8.2 %all-to-all-done.2 = bf16[16,96,128]{2,1,0:T(8,128)(2,1)S(1)} async-done(((bf16[16,96,128]{2,1,0:T(8,128)(2,1)}), bf16[16,96,128]{2,1,0:T(8,128)(2,1)S(1)}, u32[]{:S(2)}, u32[]{:S(2)}) %all-to-all-start.2) | async-done | bytes 393248 | tf_op jit(solution)/shard_map/all_to_all | solution.py:479
  92.5 3.8 %finish.1 = (bf16[4,192,256]{2,1,0:T(8,128)(2,1)}, bf16[8,192,128]{2,1,0:T(8,128)(2,1)}, bf16[96,128]{1,0:T(8,128)(2,1)S(1)}, bf16[96,128]{1,0:T(8,128)(2,1)S(1)}) custom-call(s32[2]{0:T(128)S(1)} %pad_add_fusion.at_ref, bf16[8,192,128]{2,1,0:T(8,128)(2,1)S(1)} %bitcast.32, f32[8,192,128]{2,1,0:T(8,128)S(1)} %copy-done.3, ...), custom_call_target="tpu_custom_call" | custom-call | tf_op jit(solution)/shard_map/finish/pallas_call | solution.py:286
  96.3 4.1 %all-to-all-start.3 = ((bf16[8,192,128]{2,1,0:T(8,128)(2,1)}), bf16[8,192,128]{2,1,0:T(8,128)(2,1)S(1)}, u32[]{:S(2)}, u32[]{:S(2)}) async-start(bf16[8,192,128]{2,1,0:T(8,128)(2,1)} %get-tuple-element.27), calls=%async_computation.3 | async-start | bytes 786432 | tf_op jit(solution)/shard_map/all_to_all | solution.py:494
  101.0 1.1 collective-permute-start.7
  102.2 6.0 %all-to-all-done.3.lo_ref = bf16[8,192,128]{2,1,0:T(8,128)(2,1)S(1)} async-done(((bf16[8,192,128]{2,1,0:T(8,128)(2,1)}), bf16[8,192,128]{2,1,0:T(8,128)(2,1)S(1)}, u32[]{:S(2)}, u32[]{:S(2)}) %all-to-all-start.3) | async-done | bytes 393248 | tf_op jit(solution)/shard_map/all_to_all | solution.py:494
  108.2 2.8 %collective-permute-start.5 = (bf16[8,192,128]{2,1,0:T(8,128)(2,1)S(1)}, bf16[8,192,128]{2,1,0:T(8,128)(2,1)S(1)}, u32[]{:S(2)}, u32[]{:S(2)}) collective-permute-start(bf16[8,192,128]{2,1,0:T(8,128)(2,1)S(1)} %all-to-all-done.3.lo_ref), channel_id=1, source_target_pairs={{0,1},{1,0},{2,3},{3,2},{4,5},{5,4},{6,7},{7,6},{8,9},{9,8},{10,11... | collective-permute-start | bytes 1179656 | tf_op jit(solution)/shard_map/ppermute | solution.py:403
  111.0 0.8 broadcast_in_dim.32
  111.8 8.1 %all-to-all-start.4 = ((bf16[8,2,96,128]{3,2,1,0:T(8,128)(2,1)}), bf16[8,2,96,128]{3,2,1,0:T(8,128)(2,1)S(1)}, u32[]{:S(2)}, u32[]{:S(2)}) async-start(bf16[8,2,96,128]{3,2,1,0:T(8,128)(2,1)} %broadcast_in_dim.32), calls=%async_computation.4 | async-start | bytes 786432 | tf_op jit(solution)/shard_map/all_to_all | solution.py:426
  120.0 0.8 copy.26
  120.8 5.5 %all-to-all-done.4.r_ref = bf16[8,2,96,128]{3,2,1,0:T(8,128)(2,1)S(1)} async-done(((bf16[8,2,96,128]{3,2,1,0:T(8,128)(2,1)}), bf16[8,2,96,128]{3,2,1,0:T(8,128)(2,1)S(1)}, u32[]{:S(2)}, u32[]{:S(2)}) %all-to-all-start.4) | async-done | bytes 393248 | tf_op jit(solution)/shard_map/all_to_all | solution.py:426
  126.3 1.4 columns.1.lhs
  127.8 0.7 copy-done
  128.5 0.8 copy-done.13
  129.3 26.1 %outer_update.1 = bf16[192,96,128]{2,1,0:T(8,128)(2,1)} custom-call(s32[2]{0:T(128)} %copy-done.9, bf16[8,192,128]{2,1,0:T(8,128)(2,1)} %copy-done.12, bf16[8,192,128]{2,1,0:T(8,128)(2,1)} %copy-done.13, bf16[768,256]{1,0:T(8,128)(2,1)} %copy-done, bf16[1024,128]{1,0:T(8,128)(2,1)} %bitcast.37, f32[1,128]{1,0:T(1,128)} %bitcast.46, f32[192]{0:T(256)} %dynamic_slice.6.ki_ref, ...), custom_call_target="tpu_custom_call" | custom-call | tf_op jit(solution)/shard_map/outer_update/pallas_call | solution.py:364
  (60 shorter events, 2.0 us)
Async XLA Ops:
  8.9 9.7 %copy-start.17 = (s32[1536]{0:T(1024)S(1)}, s32[1536]{0:T(1024)}, u32[]{:S(2)}) copy-start(s32[1536]{0:T(1024)} %param.20) | copy-start | bytes 18436
  8.9 10.4 %copy-start.18 = (s32[4,192]{1,0:T(4,128)S(1)}, s32[4,192]{1,0:T(4,128)}, u32[]{:S(2)}) copy-start(s32[4,192]{1,0:T(4,128)} %param.19) | copy-start | bytes 9220
  8.9 10.4 %copy-start.1 = (bf16[4,192,256]{2,1,0:T(8,128)(2,1)S(1)}, bf16[4,192,256]{2,1,0:T(8,128)(2,1)}, u32[]{:S(2)}) copy-start(bf16[4,192,256]{2,1,0:T(8,128)(2,1)} %x_ref.3) | copy-start | bytes 1179652
  8.9 10.4 %copy-start.4 = (bf16[256,1024]{1,0:T(8,128)(2,1)S(1)}, bf16[256,1024]{1,0:T(8,128)(2,1)}, u32[]{:S(2)}) copy-start(bf16[256,1024]{1,0:T(8,128)(2,1)} %w_ref.1) | copy-start | bytes 1572868
  8.9 10.4 %copy-start.6 = (bf16[128,512]{1,0:T(8,128)(2,1)S(1)}, bf16[128,512]{1,0:T(8,128)(2,1)}, u32[]{:S(2)}) copy-start(bf16[128,512]{1,0:T(8,128)(2,1)} %constant.42.clone.e_ref) | copy-start | bytes 393220
  8.9 10.4 %copy-start.8 = (bf16[192,192]{1,0:T(8,128)(2,1)S(1)}, bf16[192,192]{1,0:T(8,128)(2,1)}, u32[]{:S(2)}) copy-start(bf16[192,192]{1,0:T(8,128)(2,1)} %constant.43.clone.p_ref) | copy-start | bytes 221188
  8.9 10.4 %copy-start.11 = (f32[256]{0:T(256)S(1)}, f32[256]{0:T(256)}, u32[]{:S(2)}) copy-start(f32[256]{0:T(256)} %param.21) | copy-start | bytes 3076
  8.9 21.5 %all-to-all-start = ((bf16[32,24,384]{2,1,0:T(8,128)(2,1)}), bf16[32,24,384]{2,1,0:T(8,128)(2,1)S(1)}, u32[]{:S(2)}, u32[]{:S(2)}) async-start(bf16[32,24,384]{2,1,0:T(8,128)(2,1)} %bitcast.36), calls=%async_computation | async-start | bytes 1179648 | tf_op jit(solution)/shard_map/all_to_all | solution.py:454
  24.2 0.9 copy-start.2
  25.1 101.2 %copy-start.9 = (s32[2]{0:T(128)}, s32[2]{0:T(128)S(1)}, u32[]{:S(2)}) copy-start(s32[2]{0:T(128)S(1)} %pad_add_fusion.at_ref) | copy-start | bytes 28
  31.2 22.7 %all-to-all-start.1 = ((bf16[8,592,128]{2,1,0:T(8,128)(2,1)}), bf16[8,592,128]{2,1,0:T(8,128)(2,1)S(1)}, u32[]{:S(2)}, u32[]{:S(2)}) async-start(bf16[8,592,128]{2,1,0:T(8,128)(2,1)} %get-tuple-element.19), calls=%async_computation.1 | async-start | bytes 2424832 | tf_op jit(solution)/shard_map/all_to_all | solution.py:474
  34.8 16.1 %collective-permute-start = (bf16[8,4,24,384]{3,2,1,0:T(8,128)(2,1)S(1)}, bf16[8,4,24,384]{3,2,1,0:T(8,128)(2,1)S(1)}, u32[]{:S(2)}, u32[]{:S(2)}) collective-permute-start(bf16[8,4,24,384]{3,2,1,0:T(8,128)(2,1)S(1)} %bitcast.29), channel_id=1, source_target_pairs={{0,4},{4,8},{8,12},{12,0},{1,5},{5,9},{9,13},{13,1},{2,6},{6,10},{... | collective-permute-start | bytes 1769480 | tf_op jit(solution)/shard_map/ppermute | solution.py:407
  36.1 14.8 %collective-permute-start.1 = (bf16[8,4,24,384]{3,2,1,0:T(8,128)(2,1)S(1)}, bf16[8,4,24,384]{3,2,1,0:T(8,128)(2,1)S(1)}, u32[]{:S(2)}, u32[]{:S(2)}) collective-permute-start(bf16[8,4,24,384]{3,2,1,0:T(8,128)(2,1)S(1)} %bitcast.30), channel_id=1, source_target_pairs={{0,12},{4,0},{8,4},{12,8},{1,13},{5,1},{9,5},{13,9},{2,14},{6,2},{... | collective-permute-start | bytes 1769480 | tf_op jit(solution)/shard_map/ppermute | solution.py:407
  53.8 4.2 %collective-permute-start.2 = (bf16[8,592,128]{2,1,0:T(8,128)(2,1)S(1)}, bf16[8,592,128]{2,1,0:T(8,128)(2,1)S(1)}, u32[]{:S(2)}, u32[]{:S(2)}) collective-permute-start(bf16[8,592,128]{2,1,0:T(8,128)(2,1)S(1)} %all-to-all-done.1.own_ref), channel_id=1, source_target_pairs={{0,1},{1,0},{2,3},{3,2},{4,5},{5,4},{6,7},{7,6},{8,9},{9,8},{10,11... | collective-permute-start | bytes 3637256 | tf_op jit(solution)/shard_map/ppermute | solution.py:403
  54.9 10.1 %collective-permute-start.3 = (bf16[8,2,24,384]{3,2,1,0:T(8,128)(2,1)S(1)}, bf16[8,2,24,384]{3,2,1,0:T(8,128)(2,1)S(1)}, u32[]{:S(2)}, u32[]{:S(2)}) collective-permute-start(bf16[8,2,24,384]{3,2,1,0:T(8,128)(2,1)S(1)} %slice.18), channel_id=1, source_target_pairs={{0,4},{4,8},{8,12},{12,0},{1,5},{5,9},{9,13},{13,1},{2,6},{6,10},{... | collective-permute-start | bytes 884744 | tf_op jit(solution)/shard_map/ppermute | solution.py:407
  56.3 8.7 %collective-permute-start.4 = (bf16[8,2,24,384]{3,2,1,0:T(8,128)(2,1)S(1)}, bf16[8,2,24,384]{3,2,1,0:T(8,128)(2,1)S(1)}, u32[]{:S(2)}, u32[]{:S(2)}) collective-permute-start(bf16[8,2,24,384]{3,2,1,0:T(8,128)(2,1)S(1)} %slice.19), channel_id=1, source_target_pairs={{0,12},{4,0},{8,4},{12,8},{1,13},{5,1},{9,5},{13,9},{2,14},{6,2},{... | collective-permute-start | bytes 884744 | tf_op jit(solution)/shard_map/ppermute | solution.py:407
  65.0 19.0 %copy-start.15 = (bf16[256,32]{0,1:T(8,128)(2,1)S(1)}, bf16[256,32]{0,1:T(8,128)(2,1)}, u32[]{:S(2)}) copy-start(bf16[256,32]{0,1:T(8,128)(2,1)} %param.27) | copy-start | bytes 49156
  79.3 4.8 %copy-start.16 = (bf16[256,32]{0,1:T(8,128)(2,1)S(1)}, bf16[256,32]{0,1:T(8,128)(2,1)}, u32[]{:S(2)}) copy-start(bf16[256,32]{0,1:T(8,128)(2,1)} %param.28) | copy-start | bytes 49156
  79.3 13.2 %copy-start.3 = (f32[8,192,128]{2,1,0:T(8,128)S(1)}, f32[8,192,128]{2,1,0:T(8,128)}, u32[]{:S(2)}) copy-start(f32[8,192,128]{2,1,0:T(8,128)} %copy-done.2) | copy-start | bytes 2359300
  79.3 13.2 %copy-start.5 = (bf16[256,256]{1,0:T(8,128)(2,1)S(1)}, bf16[256,256]{1,0:T(8,128)(2,1)}, u32[]{:S(2)}) copy-start(bf16[256,256]{1,0:T(8,128)(2,1)} %wf_ref.1) | copy-start | bytes 393220
  79.3 13.2 %copy-start.7 = (bf16[192,192]{1,0:T(8,128)(2,1)S(1)}, bf16[192,192]{1,0:T(8,128)(2,1)}, u32[]{:S(2)}) copy-start(bf16[192,192]{1,0:T(8,128)(2,1)} %constant.44.clone.pinv_ref) | copy-start | bytes 221188
  79.3 13.2 %copy-start.10 = (f32[256]{0:T(256)S(1)}, f32[256]{0:T(256)}, u32[]{:S(2)}) copy-start(f32[256]{0:T(256)} %param.26) | copy-start | bytes 3076
  79.3 13.1 %all-to-all-start.2 = ((bf16[16,96,128]{2,1,0:T(8,128)(2,1)}), bf16[16,96,128]{2,1,0:T(8,128)(2,1)S(1)}, u32[]{:S(2)}, u32[]{:S(2)}) async-start(bf16[16,96,128]{2,1,0:T(8,128)(2,1)} %bitcast.11), calls=%async_computation.2 | async-start | bytes 786432 | tf_op jit(solution)/shard_map/all_to_all | solution.py:479
  96.3 23.7 %copy-start.14 = (bf16[1024,128]{1,0:T(8,128)(2,1)S(1)}, bf16[1024,128]{1,0:T(8,128)(2,1)}, u32[]{:S(2)}) copy-start(bf16[1024,128]{1,0:T(8,128)(2,1)} %param.29) | copy-start | bytes 786436
  96.3 11.9 %all-to-all-start.3 = ((bf16[8,192,128]{2,1,0:T(8,128)(2,1)}), bf16[8,192,128]{2,1,0:T(8,128)(2,1)S(1)}, u32[]{:S(2)}, u32[]{:S(2)}) async-start(bf16[8,192,128]{2,1,0:T(8,128)(2,1)} %get-tuple-element.27), calls=%async_computation.3 | async-start | bytes 786432 | tf_op jit(solution)/shard_map/all_to_all | solution.py:494
  100.4 10.6 %collective-permute-start.6 = (bf16[96,128]{1,0:T(8,128)(2,1)S(1)}, bf16[96,128]{1,0:T(8,128)(2,1)S(1)}, u32[]{:S(2)}, u32[]{:S(2)}) collective-permute-start(bf16[96,128]{1,0:T(8,128)(2,1)S(1)} %get-tuple-element.28), channel_id=1, source_target_pairs={{0,0},{1,1},{2,16},{3,17},{4,32},{5,33},{6,48},{7,49},{8,64},{9,65... | collective-permute-start | bytes 73736 | tf_op jit(solution)/shard_map/ppermute | solution.py:422
  101.0 10.0 %collective-permute-start.7 = (bf16[96,128]{1,0:T(8,128)(2,1)S(1)}, bf16[96,128]{1,0:T(8,128)(2,1)S(1)}, u32[]{:S(2)}, u32[]{:S(2)}) collective-permute-start(bf16[96,128]{1,0:T(8,128)(2,1)S(1)} %get-tuple-element.29), channel_id=1, source_target_pairs={{0,1},{1,0},{2,17},{3,16},{4,33},{5,32},{6,49},{7,48},{8,65},{9,64... | collective-permute-start | bytes 73736 | tf_op jit(solution)/shard_map/ppermute | solution.py:422
  108.2 19.5 %copy-start.12 = (bf16[8,192,128]{2,1,0:T(8,128)(2,1)}, bf16[8,192,128]{2,1,0:T(8,128)(2,1)S(1)}, u32[]{:S(2)}) copy-start(bf16[8,192,128]{2,1,0:T(8,128)(2,1)S(1)} %all-to-all-done.3.lo_ref) | copy-start | bytes 1179652
  108.2 20.3 %collective-permute-start.5 = (bf16[8,192,128]{2,1,0:T(8,128)(2,1)S(1)}, bf16[8,192,128]{2,1,0:T(8,128)(2,1)S(1)}, u32[]{:S(2)}, u32[]{:S(2)}) collective-permute-start(bf16[8,192,128]{2,1,0:T(8,128)(2,1)S(1)} %all-to-all-done.3.lo_ref), channel_id=1, source_target_pairs={{0,1},{1,0},{2,3},{3,2},{4,5},{5,4},{6,7},{7,6},{8,9},{9,8},{10,11... | collective-permute-start | bytes 1179656 | tf_op jit(solution)/shard_map/ppermute | solution.py:403
  111.8 14.5 %all-to-all-start.4 = ((bf16[8,2,96,128]{3,2,1,0:T(8,128)(2,1)}), bf16[8,2,96,128]{3,2,1,0:T(8,128)(2,1)S(1)}, u32[]{:S(2)}, u32[]{:S(2)}) async-start(bf16[8,2,96,128]{3,2,1,0:T(8,128)(2,1)} %broadcast_in_dim.32), calls=%async_computation.4 | async-start | bytes 786432 | tf_op jit(solution)/shard_map/all_to_all | solution.py:426
  127.8 0.7 copy-start
  128.5 0.8 copy-start.13

commit v5 on v4

--- a/solution.py
+++ b/solution.py
@@ -21,6 +21,7 @@
 TOTAL = 1536
 CHUNK = 2
 BIAS_AT = 48
+EARLY = 1152
 Q_ROWS, K_ROWS, V_ROWS, M_ROWS = 0, 192, 384, 576
 SENT_ROWS = 592
 LOG2E = 1.4426950408889634
@@ -59,7 +60,7 @@
     return pl.BlockSpec(memory_space=pltpu.SMEM)
 
 
-def project_kernel(x_ref, g_ref, w_ref, e_ref, p_ref, m_ref, qkv_ref, gate_ref):
+def project_kernel(x_ref, g_ref, w_ref, e_ref, p_ref, m_ref, keep_ref, qkv_ref, gate_ref, column_ref):
     slot = slot_of((ROWS, 4 * 128))
     plain = [normalised(x_ref[s].astype(F32), g_ref[...]) for s in range(SEQS)]
     moved = [mm(p_ref[...], n).astype(BF16) for n in plain]
@@ -83,18 +84,20 @@
                     gate_ref[h] = jax.nn.sigmoid(t)
     for h in range(HEADS):
         qkv_ref[h, M_ROWS:] = m_ref[...]
-
-
-def project(x, gain, w, expand, perm, present):
+    column_ref[...] = jnp.transpose(jnp.broadcast_to(keep_ref[...], (128, 128)))[:COLS]
+
+
+def project(x, gain, w, expand, perm, present, keep):
     return pl.pallas_call(
         project_kernel,
         out_shape=(
             jax.ShapeDtypeStruct((HEADS, SENT_ROWS, 128), BF16),
             jax.ShapeDtypeStruct((HEADS, ROWS, 128), F32),
+            jax.ShapeDtypeStruct((COLS, 128), F32),
         ),
         compiler_params=params(24),
         name="project",
-    )(x, gain, w, expand, perm, present)
+    )(x, gain, w, expand, perm, present, keep)
 
 
 def bias_kernel(z_ref, g_ref, w_ref, o_ref):
@@ -170,21 +173,23 @@
     )(at, own, par)
 
 
-def attend_kernel(at_ref, k_ref, v_ref, q_ref, b0, bp, bm, f1, f2, o_ref, rhs_even, rhs_odd, even, odd):
-    core = at_ref[1]
+def attend_setup(pieces, rhs_pair, width):
     count = CHUNK * HALF
-    for d, refs in enumerate(((b0,), (bp,), (bm,), (f1, f2))):
+    for d, refs in enumerate(pieces):
         for r in range(CHUNK):
             got = [ref[r, k].astype(F32) for ref in refs for k in range(4 // len(refs))]
             lines = [
                 jnp.concatenate([g[:, COLS * u : COLS * (u + 1)] for g in got], axis=1) for u in range(4)
             ]
             block = jnp.concatenate(lines, axis=0).astype(BF16)
-            for rhs in (rhs_even, rhs_odd):
+            for rhs in rhs_pair:
                 rhs[BIAS_AT + HALF * r : BIAS_AT + HALF * (r + 1), 384 * d : 384 * (d + 1)] = block
-    for rhs in (rhs_even, rhs_odd):
-        rhs[BIAS_AT + count :] = jnp.zeros((EMB - BIAS_AT - count, TOTAL), BF16)
-    wide = slot_of((count, 256))
+    for rhs in rhs_pair:
+        rhs[BIAS_AT + count :] = jnp.zeros((EMB - BIAS_AT - count, width), BF16)
+
+
+def attend_scores(k_ref, q_ref, width):
+    count = CHUNK * HALF
     lane = lax.broadcasted_iota(jnp.int32, (count, 256), 1)
     row = lax.broadcasted_iota(jnp.int32, (count, 256), 0)
     pick = jnp.where((lane == HEAD) | (lane == row + BIAS_AT), 1.0, 0.0)
@@ -199,28 +204,54 @@
             q = pltpu.roll(q, 128 - HEAD * s, 1)
         lhs = jnp.concatenate([jnp.where(first, q, pick[:, :128]).astype(BF16), tail], axis=1)
         top = None
-        for t in range(6):
-            span = slice(256 * t, 256 * (t + 1))
+        for at in range(0, width, 256):
+            span = slice(at, min(at + 256, width))
             c = mm(lhs, rhs[:, span])
             out[:, span] = c
-            both = jnp.maximum(c[:, :128], c[:, 128:])
-            top = both if top is None else jnp.maximum(top, both)
+            for half in range(0, c.shape[1], 128):
+                part = c[:, half : half + 128]
+                top = part if top is None else jnp.maximum(top, part)
         return jnp.max(top, axis=1, keepdims=True)
 
-    def values(buf, top, side):
-        e = jnp.exp(buf[...] - top).astype(BF16)
-        return mm(e, v_ref[side])
-
+    return scores
+
+
+def attend_first_kernel(k_ref, v_ref, q_ref, b0, bp, bm, sum_ref, top_ref, rhs_even, rhs_odd, even, odd):
+    count = CHUNK * HALF
+    attend_setup(((b0,), (bp,), (bm,)), (rhs_even, rhs_odd), EARLY)
+    scores = attend_scores(k_ref, q_ref, EARLY)
+    wide = slot_of((count, 256))
     top = scores(even, rhs_even, 0, 0)
     for n in range(2 * SEQS):
         side, s = divmod(n, SEQS)
         now, later, rhs = (even, odd, rhs_odd) if n % 2 == 0 else (odd, even, rhs_even)
         if n < 2 * SEQS - 1:
             following = scores(later, rhs, *divmod(n + 1, SEQS))
-        got = values(now, top, side)
+        got = mm(jnp.exp(now[...] - top).astype(BF16), v_ref[side])
         total = got if s == 0 else jnp.where(wide == s, got, total)
+        top_ref[side, s] = jnp.broadcast_to(top, (count, 128))
         if n < 2 * SEQS - 1:
             top = following
+        if s == SEQS - 1:
+            sum_ref[side] = total
+
+
+def attend_last_kernel(at_ref, k_ref, v_ref, q_ref, f1, f2, sum_ref, top_ref, o_ref, rhs_all, buf_all):
+    core = at_ref[1]
+    count = CHUNK * HALF
+    late = TOTAL - EARLY
+    attend_setup(((f1, f2),), [rhs_all.at[n] for n in range(2 * SEQS)], late)
+    scores = attend_scores(k_ref, q_ref, late)
+    wide = slot_of((count, 256))
+    peaks = [scores(buf_all.at[n], rhs_all.at[n], *divmod(n, SEQS)) for n in range(2 * SEQS)]
+    for n in range(2 * SEQS):
+        side, s = divmod(n, SEQS)
+        before = top_ref[side, s]
+        peak = jnp.maximum(peaks[n], before)
+        e = jnp.exp(buf_all[n] - jnp.concatenate([peak] * (late // 128), axis=1)).astype(BF16)
+        shrink = jnp.exp(before - peak)
+        got = mm(e, v_ref[side]) + sum_ref[side] * jnp.concatenate([shrink, shrink], axis=1)
+        total = got if s == 0 else jnp.where(wide == s, got, total)
         if s == SEQS - 1:
             out = (total[:, :128] / total[:, 128:]).astype(BF16)
             quad = core if side == 0 else 1 - core
@@ -229,29 +260,57 @@
 
 
 def attend(at, k, v, q, pieces):
+    count = CHUNK * HALF
+    late = TOTAL - EARLY
+
     def piece(parts):
         return pl.BlockSpec((CHUNK, parts, QUADS, 4 * COLS), lambda t: (t, 0, 0, 0))
 
+    def scratch(width):
+        return [pltpu.VMEM((EMB, width), BF16)] * 2 + [pltpu.VMEM((count, width), F32)] * 2
+
+    queries = pl.BlockSpec((2, CHUNK, HALF, 128), lambda t: (0, t, 0, 0))
+    sums = pl.BlockSpec((2, count, 256), lambda t: (0, t, 0))
+    tops = pl.BlockSpec((2, SEQS, count, 128), lambda t: (0, 0, t, 0))
+    total, top = pl.pallas_call(
+        attend_first_kernel,
+        out_shape=(
+            jax.ShapeDtypeStruct((2, 8 * HALF, 256), F32),
+            jax.ShapeDtypeStruct((2, SEQS, 8 * HALF, 128), F32),
+        ),
+        grid=(8 // CHUNK,),
+        in_specs=[
+            pl.BlockSpec((2, 192, EARLY), lambda t: (0, 0, 0)),
+            pl.BlockSpec((2, EARLY, EMB), lambda t: (0, 0, 0)),
+            queries,
+            piece(4),
+            piece(4),
+            piece(4),
+        ],
+        out_specs=(sums, tops),
+        scratch_shapes=scratch(EARLY),
+        compiler_params=params(28),
+        name="attend_first",
+    )(k, v, q, *pieces[:3])
     return pl.pallas_call(
-        attend_kernel,
+        attend_last_kernel,
         out_shape=jax.ShapeDtypeStruct((8, 2, HALF, 128), BF16),
         grid=(8 // CHUNK,),
         in_specs=[
             smem(),
-            pl.BlockSpec((2, 192, TOTAL), lambda t: (0, 0, 0)),
-            pl.BlockSpec((2, TOTAL, EMB), lambda t: (0, 0, 0)),
-            pl.BlockSpec((2, CHUNK, HALF, 128), lambda t: (0, t, 0, 0)),
-            piece(4),
-            piece(4),
-            piece(4),
+            pl.BlockSpec((2, 192, late), lambda t: (0, 0, EARLY // late)),
+            pl.BlockSpec((2, late, EMB), lambda t: (0, EARLY // late, 0)),
+            queries,
             piece(2),
             piece(2),
+            sums,
+            tops,
         ],
         out_specs=pl.BlockSpec((CHUNK, 2, HALF, 128), lambda t: (t, 0, 0, 0)),
-        scratch_shapes=[pltpu.VMEM((EMB, TOTAL), BF16)] * 2 + [pltpu.VMEM((CHUNK * HALF, TOTAL), F32)] * 2,
+        scratch_shapes=[pltpu.VMEM((2 * SEQS, EMB, late), BF16), pltpu.VMEM((2 * SEQS, count, late), F32)],
         compiler_params=params(28),
-        name="attend",
-    )(at, k, v, q, *pieces)
+        name="attend_last",
+    )(at, k, v, q, *pieces[3:], total, top)
 
 
 def finish_kernel(
@@ -297,47 +356,29 @@
     )(*args)
 
 
-STEP = 48
-
-
-def columns_kernel(at_ref, r_ref, o_ref, r_all):
-    core = at_ref[1]
-    pad = jnp.zeros((128 - COLS, 128), F32)
-    for p in range(PEERS_COL // 2):
-        for side in range(2):
-            c = 2 * p + (core if side == 0 else 1 - core)
-            turned = jnp.transpose(jnp.concatenate([r_ref[p, side].astype(F32), pad], axis=0))
-            r_all[pl.ds(pl.multiple_of(c * 128, 128), 128)] = turned
-    for q in range(8):
-        lines = [
-            r_all[pl.ds(HEAD * s + 4 * q + b, PEERS_COL, stride=128), :] for b in range(4) for s in range(SEQS)
-        ]
-        turned = jnp.transpose(jnp.concatenate(lines, axis=0))
-        o_ref[COLS * q : COLS * (q + 1)] = turned[:COLS].astype(BF16)
-
-
-def columns(at, right):
-    return pl.pallas_call(
-        columns_kernel,
-        out_shape=jax.ShapeDtypeStruct((8 * COLS, EMB), BF16),
-        in_specs=[smem(), vmem()],
-        out_specs=vmem(),
-        scratch_shapes=[pltpu.VMEM((PEERS_COL * 128, 128), F32)],
-        compiler_params=params(16),
-        name="columns",
-    )(at, right)
-
-
-def outer_kernel(at_ref, lo_ref, lp_ref, lhs, w_ref, off_ref, ki_ref, kj_ref, z_ref, o_ref, l_all, rhs, obf):
+STEP = 64
+PART = 16
+
+
+def outer_kernel(at_ref, lo_ref, lp_ref, r_ref, w_ref, off_ref, ki_ref, kj_ref, z_ref, o_ref, l_all, r_all, lhs, rhs, *obf):
     step = pl.program_id(0)
 
     @pl.when(step == 0)
     def _():
         core = at_ref[1]
+        pad = jnp.zeros((128 - COLS, 128), F32)
         for p in range(PEERS_COL // 2):
             for side, ref in enumerate((lo_ref, lp_ref)):
                 c = 2 * p + (core if side == 0 else 1 - core)
                 l_all[pl.ds(pl.multiple_of(c * ROWS, ROWS), ROWS)] = ref[p].astype(F32)
+                turned = jnp.transpose(jnp.concatenate([r_ref[p, side].astype(F32), pad], axis=0))
+                r_all[pl.ds(pl.multiple_of(c * 128, 128), 128)] = turned
+        for q in range(8):
+            lines = [
+                r_all[pl.ds(HEAD * s + 4 * q + b, PEERS_COL, stride=128), :] for b in range(4) for s in range(SEQS)
+            ]
+            turned = jnp.transpose(jnp.concatenate(lines, axis=0))
+            lhs[COLS * q : COLS * (q + 1)] = turned[:COLS].astype(BF16)
 
     slot = slot_of((PEERS_COL, 128))
     for k in range(STEP):
@@ -347,17 +388,29 @@
             for s in range(SEQS):
                 at = 64 * b + 16 * s
                 rhs[at : at + 16, 128 * k : 128 * (k + 1)] = jnp.where(slot == b, rolled[(b - s) % 4], 0.0).astype(BF16)
-    for k in range(0, STEP, 2):
-        outer = mm(lhs[...], rhs[:, 128 * k : 128 * (k + 2)]).astype(BF16)
-        for e in range(2):
-            for q in range(8):
-                obf[COLS * (k + e) : COLS * (k + e + 1), 128 * q : 128 * (q + 1)] = outer[
-                    COLS * q : COLS * (q + 1), 128 * e : 128 * (e + 1)
-                ]
-    update = mm(obf[...], w_ref[...]) + off_ref[...]
-    for k in range(STEP):
-        keep = kj_ref[...] * ki_ref[step * STEP + k]
-        o_ref[k] = (z_ref[k].astype(F32) + update[COLS * k : COLS * (k + 1)] * keep).astype(BF16)
+
+    def products(part):
+        for k in range(0, PART, 2):
+            at = 128 * (PART * part + k)
+            outer = mm(lhs[...], rhs[:, at : at + 256]).astype(BF16)
+            for e in range(2):
+                for q in range(8):
+                    obf[part % 2][COLS * (k + e) : COLS * (k + e + 1), 128 * q : 128 * (q + 1)] = outer[
+                        COLS * q : COLS * (q + 1), 128 * e : 128 * (e + 1)
+                    ]
+
+    def project_part(part):
+        update = mm(obf[part % 2][...], w_ref[...]) + off_ref[...]
+        for k in range(PART):
+            i = PART * part + k
+            keep = kj_ref[...] * ki_ref[step * STEP + i]
+            o_ref[i] = (z_ref[i].astype(F32) + update[COLS * k : COLS * (k + 1)] * keep).astype(BF16)
+
+    products(0)
+    for part in range(1, STEP // PART):
+        products(part)
+        project_part(part - 1)
+    project_part(STEP // PART - 1)
 
 
 def outer_update(at, left_own, left_par, right, w, offset, keep_i, keep_j, z):
@@ -369,7 +422,7 @@
             smem(),
             pl.BlockSpec((PEERS_COL // 2, ROWS, 128), lambda t: (0, 0, 0)),
             pl.BlockSpec((PEERS_COL // 2, ROWS, 128), lambda t: (0, 0, 0)),
-            pl.BlockSpec((8 * COLS, EMB), lambda t: (0, 0)),
+            pl.BlockSpec((PEERS_COL // 2, 2, COLS, 128), lambda t: (0, 0, 0, 0)),
             pl.BlockSpec((1024, PAIR), lambda t: (0, 0)),
             pl.BlockSpec((1, PAIR), lambda t: (0, 0)),
             smem(),
@@ -379,10 +432,13 @@
         out_specs=pl.BlockSpec((STEP, COLS, PAIR), lambda t: (t, 0, 0)),
         scratch_shapes=[
             pltpu.VMEM((PEERS_COL * ROWS, 128), F32),
+            pltpu.VMEM((PEERS_COL * 128, 128), F32),
+            pltpu.VMEM((8 * COLS, EMB), BF16),
             pltpu.VMEM((256, 128 * STEP), BF16),
-            pltpu.VMEM((STEP * COLS, 1024), BF16),
+            pltpu.VMEM((PART * COLS, 1024), BF16),
+            pltpu.VMEM((PART * COLS, 1024), BF16),
         ],
-        compiler_params=params(60),
+        compiler_params=params(63),
         name="outer_update",
     )(at, left_own, left_par, right, w, offset, keep_i, keep_j, z)
 
@@ -456,20 +512,21 @@
     keep = amino_availability.astype(F32)
     keep_i = lax.dynamic_slice_in_dim(keep, lax.axis_index(ROW) * ROWS, ROWS)
     keep_j = lax.dynamic_slice_in_dim(keep, lax.axis_index(COL) * COLS, COLS)
-    keep_j = jnp.broadcast_to(keep_j[:, None], (COLS, PAIR))
+    keep_j = jnp.pad(keep_j, (0, 128 - COLS))[None]
     present = alignment_availability.astype(BF16)
     sent_mask = jnp.pad(
         jnp.stack([present[:, :128], jnp.pad(present[:, 128:], ((0, 0), (0, 64)))]), ((0, 0), (0, 4), (0, 0))
     ).reshape(16, 128)
-    own, gate = project(
+    own, gate, keep_j = project(
         alignment_embedding,
         alignment_scaling_vector[None],
         attention_joint_matrix,
         jnp.asarray(expand, BF16),
         jnp.asarray(perm, BF16),
         sent_mask,
+        keep_j,
     )
-    own, bias, at, keep_i, keep_j = lax.optimization_barrier((own, bias, at, keep_i, keep_j))
+    own, bias, at, keep_i = lax.optimization_barrier((own, bias, at, keep_i))
     up, down = along_y(bias, 1), along_y(bias, 3)
     own = lax.all_to_all(own, ROW, 0, 0, tiled=True)
     own = lax.optimization_barrier((own, up, down))[0]
@@ -493,7 +550,7 @@
     )
     left = lax.all_to_all(left, ("y", "zh"), 0, 0, tiled=True)
     right = jnp.stack([turn_grid(near, 0), turn_grid(far, 1)])
-    right = columns(at, to_all(right, ROW, 8))
+    right = to_all(right, ROW, 8)
 
     projection = (tensor_projection_matrix.astype(F32) / 64).astype(BF16)
     projection = projection.reshape(HEAD, 8, 4, PAIR).transpose(1, 2, 0, 3).reshape(1024, PAIR)

time: 158 us -> 153 us (0.968)
  waiting for transfers between devices: 47.2 us -> 40.6 us
  Pallas kernels: 59.8 us -> 63.3 us
    ppermute x4, waiting for transfers between devices: 19.1 us -> 13.3 us  [along_y(): return lax.ppermute(x, 'y', [(a, (a + d) % 4) for a in range(4)])]
    pallas_call x2, Pallas kernels: 15.7 us -> 19 us  [the longest x1 11.8 us: attend(): pl.pallas_call(attend_first_kernel, out_shape=(jax.ShapeDtypeStruct((2, 8...]
  transfers between devices with their start and end apart: 13 -> 13, of which waited for: 7 -> 6; matrix products, arithmetic and copies ran while one was open for 2% -> 2% of each run, Pallas kernels for 5% -> 12%
where the time goes in v5:
time: 153 us; the launch traced here: 151 us
  Pallas kernels  63.3 us (41%)
  waiting for transfers between devices  40.6 us (27%)
  starting transfers between devices  40.3 us (26%)
  local copies, waits for them, and re-layouts  5.23 us (3%)
    pallas_call x1, Pallas kernels, outer_update(): pl.pallas_call(outer_kernel, out_shape=jax.ShapeDtypeStruct((ROWS, COLS,...  26.2 us
    ppermute x4, waiting for transfers between devices, along_y(): return lax.ppermute(x, 'y', [(a, (a + d) % 4) for a in range(4)])  13.3 us
    pallas_call x1, Pallas kernels, attend(): pl.pallas_call(attend_first_kernel, out_shape=(jax.ShapeDtypeStruct((2, 8...  11.8 us
    all_to_all x1, starting transfers between devices, on_device(): lax.all_to_all(bias, ROW + ('zh', 'core'), 0, 0, tiled=True)  9.56 us
    pallas_call x1, Pallas kernels, pair_bias(): pl.pallas_call(bias_kernel, out_shape=jax.ShapeDtypeStruct((HEADS, 2, 2 *...  8.29 us
    all_to_all x1, waiting for transfers between devices, on_device(): lax.all_to_all(attended, ROW + ('core',), 0, 0, tiled=True)  8.24 us
    all_to_all x1, starting transfers between devices, to_all(): lax.all_to_all(jnp.broadcast_to(x[None], (n,) + x.shape), axes, 0, 0, til...  8.15 us
    pallas_call x1, Pallas kernels, attend(): pl.pallas_call(attend_last_kernel, out_shape=jax.ShapeDtypeStruct((8, 2,...  7.21 us
  transfers between devices with their start and end apart: 13, of which 6 were waited for; matrix products, arithmetic and copies ran while one was open for 2% of the time, Pallas kernels for 12%

profile of v5, /device:TPU:1, one launch (start us, length us, event | category | flops | bytes accessed | tf_op | source)
XLA Modules:
  0.0 150.5 jit_solution(3407376332014232618)
XLA Ops:
  0.7 8.3 %pair_bias.1 = bf16[8,2,48,384]{3,2,1,0:T(8,128)(2,1)} custom-call(bf16[18432,128]{1,0:T(8,128)(2,1)} %bitcast.37, f32[1,128]{1,0:T(1,128)} %bitcast.47, bf16[8,128]{1,0:T(8,128)(2,1)} %bitcast.46), custom_call_target="tpu_custom_call" | custom-call | tf_op jit(solution)/shard_map/pair_bias/pallas_call | solution.py:120
  9.0 9.6 %all-to-all-start = ((bf16[32,24,384]{2,1,0:T(8,128)(2,1)}), bf16[32,24,384]{2,1,0:T(8,128)(2,1)S(1)}, u32[]{:S(2)}, u32[]{:S(2)}) async-start(bf16[32,24,384]{2,1,0:T(8,128)(2,1)} %bitcast.38), calls=%async_computation | async-start | bytes 1179648 | tf_op jit(solution)/shard_map/all_to_all | solution.py:510
  18.7 0.7 dynamic_slice.7.ki_ref
  19.4 4.8 %project.1 = (bf16[8,592,128]{2,1,0:T(8,128)(2,1)}, f32[8,192,128]{2,1,0:T(8,128)S(1)}, f32[96,128]{1,0:T(8,128)S(1)}) custom-call(bf16[4,192,256]{2,1,0:T(8,128)(2,1)S(1)} %copy-done, f32[1,256]{1,0:T(1,128)S(1)} %bitcast.35, bf16[256,1024]{1,0:T(8,128)(2,1)S(1)} %copy-done.3, bf16[128,512]{1,0:T(8,128)(2,1)S(1)} %copy-done.5, ...), custom_call_target="tpu_custom_call" | custom-call | tf_op jit(solution)/shard_map/project/pallas_call | solution.py:91
  24.3 0.9 copy-done.1
  25.2 0.6 copy-done.8
  25.9 4.6 %all-to-all-done = bf16[32,24,384]{2,1,0:T(8,128)(2,1)S(1)} async-done(((bf16[32,24,384]{2,1,0:T(8,128)(2,1)}), bf16[32,24,384]{2,1,0:T(8,128)(2,1)S(1)}, u32[]{:S(2)}, u32[]{:S(2)}) %all-to-all-start) | async-done | bytes 589856 | tf_op jit(solution)/shard_map/all_to_all | solution.py:510
  30.5 3.6 %all-to-all-start.1 = ((bf16[8,592,128]{2,1,0:T(8,128)(2,1)}), bf16[8,592,128]{2,1,0:T(8,128)(2,1)S(1)}, u32[]{:S(2)}, u32[]{:S(2)}) async-start(bf16[8,592,128]{2,1,0:T(8,128)(2,1)} %get-tuple-element.21), calls=%async_computation.1 | async-start | bytes 2424832 | tf_op jit(solution)/shard_map/all_to_all | solution.py:531
  34.1 1.4 collective-permute-start
  35.5 1.5 %collective-permute-start.1 = (bf16[8,4,24,384]{3,2,1,0:T(8,128)(2,1)S(1)}, bf16[8,4,24,384]{3,2,1,0:T(8,128)(2,1)S(1)}, u32[]{:S(2)}, u32[]{:S(2)}) collective-permute-start(bf16[8,4,24,384]{3,2,1,0:T(8,128)(2,1)S(1)} %bitcast.32), channel_id=1, source_target_pairs={{0,12},{4,0},{8,4},{12,8},{1,13},{5,1},{9,5},{13,9},{2,14},{6,2},{... | collective-permute-start | bytes 1769480 | tf_op jit(solution)/shard_map/ppermute | solution.py:463
  37.0 13.2 %collective-permute-done.bp = bf16[8,4,24,384]{3,2,1,0:T(8,128)(2,1)S(1)} collective-permute-done((bf16[8,4,24,384]{3,2,1,0:T(8,128)(2,1)S(1)}, bf16[8,4,24,384]{3,2,1,0:T(8,128)(2,1)S(1)}, u32[]{:S(2)}, u32[]{:S(2)}) %collective-permute-start) | collective-permute-done | bytes 589856 | tf_op jit(solution)/shard_map/ppermute | solution.py:463
  50.2 3.0 %all-to-all-done.1.own_ref = bf16[8,592,128]{2,1,0:T(8,128)(2,1)S(1)} async-done(((bf16[8,592,128]{2,1,0:T(8,128)(2,1)}), bf16[8,592,128]{2,1,0:T(8,128)(2,1)S(1)}, u32[]{:S(2)}, u32[]{:S(2)}) %all-to-all-start.1) | async-done | bytes 1212448 | tf_op jit(solution)/shard_map/all_to_all | solution.py:531
  53.2 1.0 collective-permute-start.2
  54.2 1.4 collective-permute-start.3
  55.6 1.7 %collective-permute-start.4 = (bf16[8,2,24,384]{3,2,1,0:T(8,128)(2,1)S(1)}, bf16[8,2,24,384]{3,2,1,0:T(8,128)(2,1)S(1)}, u32[]{:S(2)}, u32[]{:S(2)}) collective-permute-start(bf16[8,2,24,384]{3,2,1,0:T(8,128)(2,1)S(1)} %slice.19), channel_id=1, source_target_pairs={{0,12},{4,0},{8,4},{12,8},{1,13},{5,1},{9,5},{13,9},{2,14},{6,2},{... | collective-permute-start | bytes 884744 | tf_op jit(solution)/shard_map/ppermute | solution.py:463
  57.3 1.1 prepare.1
  58.4 11.8 %attend_first.1 = (f32[2,768,256]{2,1,0:T(8,128)S(1)}, f32[2,4,768,128]{3,2,1,0:T(8,128)S(1)}) custom-call(bf16[2,192,1536]{2,1,0:T(8,128)(2,1)S(1)} %get-tuple-element.24.k_ref, bf16[2,1536,256]{2,1,0:T(8,128)(2,1)S(1)} %get-tuple-element.25.v_ref, bf16[2,8,96,128]{3,2,1,0:T(8,128)(2,1)S(1)} %get-tuple-element.26.q_ref, ...), custom_call_target="tpu_custom_call" | custom-call | tf_op jit(solution)/shard_map/attend_first/pallas_call | solution.py:275
  70.3 7.2 %attend_last.1 = bf16[8,2,96,128]{3,2,1,0:T(8,128)(2,1)} custom-call(s32[2]{0:T(128)S(1)} %pad_add_fusion.at_ref, bf16[2,192,1536]{2,1,0:T(8,128)(2,1)S(1)} %get-tuple-element.24.k_ref, bf16[2,1536,256]{2,1,0:T(8,128)(2,1)S(1)} %get-tuple-element.25.v_ref, bf16[2,8,96,128]{3,2,1,0:T(8,128)(2,1)S(1)} %get-tuple-element.26.q_ref, ...), custom_call_target="tpu_custom_call" | custom-call | tf_op jit(solution)/shard_map/attend_last/pallas_call | solution.py:295
  77.5 4.0 %all-to-all-start.2 = ((bf16[16,96,128]{2,1,0:T(8,128)(2,1)}), bf16[16,96,128]{2,1,0:T(8,128)(2,1)S(1)}, u32[]{:S(2)}, u32[]{:S(2)}) async-start(bf16[16,96,128]{2,1,0:T(8,128)(2,1)} %bitcast.12), calls=%async_computation.2 | async-start | bytes 786432 | tf_op jit(solution)/shard_map/all_to_all | solution.py:536
  81.9 8.2 %all-to-all-done.2 = bf16[16,96,128]{2,1,0:T(8,128)(2,1)S(1)} async-done(((bf16[16,96,128]{2,1,0:T(8,128)(2,1)}), bf16[16,96,128]{2,1,0:T(8,128)(2,1)S(1)}, u32[]{:S(2)}, u32[]{:S(2)}) %all-to-all-start.2) | async-done | bytes 393248 | tf_op jit(solution)/shard_map/all_to_all | solution.py:536
  90.2 3.8 %finish.1 = (bf16[4,192,256]{2,1,0:T(8,128)(2,1)}, bf16[8,192,128]{2,1,0:T(8,128)(2,1)}, bf16[96,128]{1,0:T(8,128)(2,1)S(1)}, bf16[96,128]{1,0:T(8,128)(2,1)S(1)}) custom-call(s32[2]{0:T(128)S(1)} %pad_add_fusion.at_ref, bf16[8,192,128]{2,1,0:T(8,128)(2,1)S(1)} %bitcast.34, f32[8,192,128]{2,1,0:T(8,128)S(1)} %copy-done.2, bf16[4,192,256]{2,1,0:T(8,128)(2,1)S(1)} %copy-done, ...), custom_call_target="tpu_custom_call" | custom-call | tf_op jit(solution)/shard_map/finish/pallas_call | solution.py:345
  94.0 3.5 %all-to-all-start.3 = ((bf16[8,192,128]{2,1,0:T(8,128)(2,1)}), bf16[8,192,128]{2,1,0:T(8,128)(2,1)S(1)}, u32[]{:S(2)}, u32[]{:S(2)}) async-start(bf16[8,192,128]{2,1,0:T(8,128)(2,1)} %get-tuple-element.31), calls=%async_computation.3 | async-start | bytes 786432 | tf_op jit(solution)/shard_map/all_to_all | solution.py:551
  97.5 0.7 collective-permute-start.6
  98.1 1.1 collective-permute-start.7
  99.3 6.0 %all-to-all-done.3.lo_ref = bf16[8,192,128]{2,1,0:T(8,128)(2,1)S(1)} async-done(((bf16[8,192,128]{2,1,0:T(8,128)(2,1)}), bf16[8,192,128]{2,1,0:T(8,128)(2,1)S(1)}, u32[]{:S(2)}, u32[]{:S(2)}) %all-to-all-start.3) | async-done | bytes 393248 | tf_op jit(solution)/shard_map/all_to_all | solution.py:551
  105.3 2.8 %collective-permute-start.5 = (bf16[8,192,128]{2,1,0:T(8,128)(2,1)S(1)}, bf16[8,192,128]{2,1,0:T(8,128)(2,1)S(1)}, u32[]{:S(2)}, u32[]{:S(2)}) collective-permute-start(bf16[8,192,128]{2,1,0:T(8,128)(2,1)S(1)} %all-to-all-done.3.lo_ref), channel_id=1, source_target_pairs={{0,1},{1,0},{2,3},{3,2},{4,5},{5,4},{6,7},{7,6},{8,9},{9,8},{10,11... | collective-permute-start | bytes 1179656 | tf_op jit(solution)/shard_map/ppermute | solution.py:459
  108.1 0.8 broadcast_in_dim.29
  108.9 8.1 %all-to-all-start.4 = ((bf16[8,2,96,128]{3,2,1,0:T(8,128)(2,1)}), bf16[8,2,96,128]{3,2,1,0:T(8,128)(2,1)S(1)}, u32[]{:S(2)}, u32[]{:S(2)}) async-start(bf16[8,2,96,128]{3,2,1,0:T(8,128)(2,1)} %broadcast_in_dim.29), calls=%async_computation.4 | async-start | bytes 786432 | tf_op jit(solution)/shard_map/all_to_all | solution.py:482
  117.1 0.8 copy.26
  117.9 5.5 %all-to-all-done.4.r_ref = bf16[8,2,96,128]{3,2,1,0:T(8,128)(2,1)S(1)} async-done(((bf16[8,2,96,128]{3,2,1,0:T(8,128)(2,1)}), bf16[8,2,96,128]{3,2,1,0:T(8,128)(2,1)S(1)}, u32[]{:S(2)}, u32[]{:S(2)}) %all-to-all-start.4) | async-done | bytes 393248 | tf_op jit(solution)/shard_map/all_to_all | solution.py:482
  123.4 0.8 copy-done.14
  124.3 26.2 %outer_update.1 = bf16[192,96,128]{2,1,0:T(8,128)(2,1)} custom-call(s32[2]{0:T(128)} %copy-done.9, bf16[8,192,128]{2,1,0:T(8,128)(2,1)} %copy-done.12, bf16[8,192,128]{2,1,0:T(8,128)(2,1)} %copy-done.14, bf16[8,2,96,128]{3,2,1,0:T(8,128)(2,1)} %copy-done.13, bf16[1024,128]{1,0:T(8,128)(2,1)} %bitcast.39, f32[1,128]{1,0:T(1,128)} %bitcast.48, ...), custom_call_target="tpu_custom_call" | custom-call | tf_op jit(solution)/shard_map/outer_update/pallas_call | solution.py:417
  (62 shorter events, 0.9 us)
Async XLA Ops:
  0.6 17.9 %copy-start.19 = (s32[4,192]{1,0:T(4,128)S(1)}, s32[4,192]{1,0:T(4,128)}, u32[]{:S(2)}) copy-start(s32[4,192]{1,0:T(4,128)} %param.19) | copy-start | bytes 9220
  0.6 18.0 %copy-start.18 = (s32[1536]{0:T(1024)S(1)}, s32[1536]{0:T(1024)}, u32[]{:S(2)}) copy-start(s32[1536]{0:T(1024)} %param.20) | copy-start | bytes 18436
  0.7 18.7 %copy-start = (bf16[4,192,256]{2,1,0:T(8,128)(2,1)S(1)}, bf16[4,192,256]{2,1,0:T(8,128)(2,1)}, u32[]{:S(2)}) copy-start(bf16[4,192,256]{2,1,0:T(8,128)(2,1)} %x_ref.3) | copy-start | bytes 1179652
  0.7 18.7 %copy-start.5 = (bf16[128,512]{1,0:T(8,128)(2,1)S(1)}, bf16[128,512]{1,0:T(8,128)(2,1)}, u32[]{:S(2)}) copy-start(bf16[128,512]{1,0:T(8,128)(2,1)} %constant.44.clone.e_ref) | copy-start | bytes 393220
  0.7 18.7 %copy-start.7 = (bf16[192,192]{1,0:T(8,128)(2,1)S(1)}, bf16[192,192]{1,0:T(8,128)(2,1)}, u32[]{:S(2)}) copy-start(bf16[192,192]{1,0:T(8,128)(2,1)} %constant.45.clone.p_ref) | copy-start | bytes 221188
  0.7 18.7 %copy-start.10 = (f32[256]{0:T(256)S(1)}, f32[256]{0:T(256)}, u32[]{:S(2)}) copy-start(f32[256]{0:T(256)} %param.21) | copy-start | bytes 3076
  9.0 10.4 %copy-start.3 = (bf16[256,1024]{1,0:T(8,128)(2,1)S(1)}, bf16[256,1024]{1,0:T(8,128)(2,1)}, u32[]{:S(2)}) copy-start(bf16[256,1024]{1,0:T(8,128)(2,1)} %w_ref.1) | copy-start | bytes 1572868
  9.0 21.5 %all-to-all-start = ((bf16[32,24,384]{2,1,0:T(8,128)(2,1)}), bf16[32,24,384]{2,1,0:T(8,128)(2,1)S(1)}, u32[]{:S(2)}, u32[]{:S(2)}) async-start(bf16[32,24,384]{2,1,0:T(8,128)(2,1)} %bitcast.38), calls=%async_computation | async-start | bytes 1179648 | tf_op jit(solution)/shard_map/all_to_all | solution.py:510
  24.3 0.9 copy-start.1
  25.9 64.3 %copy-start.9 = (s32[2]{0:T(128)}, s32[2]{0:T(128)S(1)}, u32[]{:S(2)}) copy-start(s32[2]{0:T(128)S(1)} %pad_add_fusion.at_ref) | copy-start | bytes 28
  30.5 22.7 %all-to-all-start.1 = ((bf16[8,592,128]{2,1,0:T(8,128)(2,1)}), bf16[8,592,128]{2,1,0:T(8,128)(2,1)S(1)}, u32[]{:S(2)}, u32[]{:S(2)}) async-start(bf16[8,592,128]{2,1,0:T(8,128)(2,1)} %get-tuple-element.21), calls=%async_computation.1 | async-start | bytes 2424832 | tf_op jit(solution)/shard_map/all_to_all | solution.py:531
  34.1 16.1 %collective-permute-start = (bf16[8,4,24,384]{3,2,1,0:T(8,128)(2,1)S(1)}, bf16[8,4,24,384]{3,2,1,0:T(8,128)(2,1)S(1)}, u32[]{:S(2)}, u32[]{:S(2)}) collective-permute-start(bf16[8,4,24,384]{3,2,1,0:T(8,128)(2,1)S(1)} %bitcast.31), channel_id=1, source_target_pairs={{0,4},{4,8},{8,12},{12,0},{1,5},{5,9},{9,13},{13,1},{2,6},{6,10},{... | collective-permute-start | bytes 1769480 | tf_op jit(solution)/shard_map/ppermute | solution.py:463
  35.5 14.8 %collective-permute-start.1 = (bf16[8,4,24,384]{3,2,1,0:T(8,128)(2,1)S(1)}, bf16[8,4,24,384]{3,2,1,0:T(8,128)(2,1)S(1)}, u32[]{:S(2)}, u32[]{:S(2)}) collective-permute-start(bf16[8,4,24,384]{3,2,1,0:T(8,128)(2,1)S(1)} %bitcast.32), channel_id=1, source_target_pairs={{0,12},{4,0},{8,4},{12,8},{1,13},{5,1},{9,5},{13,9},{2,14},{6,2},{... | collective-permute-start | bytes 1769480 | tf_op jit(solution)/shard_map/ppermute | solution.py:463
  53.2 4.2 %collective-permute-start.2 = (bf16[8,592,128]{2,1,0:T(8,128)(2,1)S(1)}, bf16[8,592,128]{2,1,0:T(8,128)(2,1)S(1)}, u32[]{:S(2)}, u32[]{:S(2)}) collective-permute-start(bf16[8,592,128]{2,1,0:T(8,128)(2,1)S(1)} %all-to-all-done.1.own_ref), channel_id=1, source_target_pairs={{0,1},{1,0},{2,3},{3,2},{4,5},{5,4},{6,7},{7,6},{8,9},{9,8},{10,11... | collective-permute-start | bytes 3637256 | tf_op jit(solution)/shard_map/ppermute | solution.py:459
  54.2 16.0 %collective-permute-start.3 = (bf16[8,2,24,384]{3,2,1,0:T(8,128)(2,1)S(1)}, bf16[8,2,24,384]{3,2,1,0:T(8,128)(2,1)S(1)}, u32[]{:S(2)}, u32[]{:S(2)}) collective-permute-start(bf16[8,2,24,384]{3,2,1,0:T(8,128)(2,1)S(1)} %slice.18), channel_id=1, source_target_pairs={{0,4},{4,8},{8,12},{12,0},{1,5},{5,9},{9,13},{13,1},{2,6},{6,10},{... | collective-permute-start | bytes 884744 | tf_op jit(solution)/shard_map/ppermute | solution.py:463
  55.6 14.6 %collective-permute-start.4 = (bf16[8,2,24,384]{3,2,1,0:T(8,128)(2,1)S(1)}, bf16[8,2,24,384]{3,2,1,0:T(8,128)(2,1)S(1)}, u32[]{:S(2)}, u32[]{:S(2)}) collective-permute-start(bf16[8,2,24,384]{3,2,1,0:T(8,128)(2,1)S(1)} %slice.19), channel_id=1, source_target_pairs={{0,12},{4,0},{8,4},{12,8},{1,13},{5,1},{9,5},{13,9},{2,14},{6,2},{... | collective-permute-start | bytes 884744 | tf_op jit(solution)/shard_map/ppermute | solution.py:463
  70.3 11.3 %copy-start.16 = (bf16[256,32]{0,1:T(8,128)(2,1)S(1)}, bf16[256,32]{0,1:T(8,128)(2,1)}, u32[]{:S(2)}) copy-start(bf16[256,32]{0,1:T(8,128)(2,1)} %param.27) | copy-start | bytes 49156
  70.3 11.5 %copy-start.17 = (bf16[256,32]{0,1:T(8,128)(2,1)S(1)}, bf16[256,32]{0,1:T(8,128)(2,1)}, u32[]{:S(2)}) copy-start(bf16[256,32]{0,1:T(8,128)(2,1)} %param.28) | copy-start | bytes 49156
  77.5 12.6 %copy-start.2 = (f32[8,192,128]{2,1,0:T(8,128)S(1)}, f32[8,192,128]{2,1,0:T(8,128)}, u32[]{:S(2)}) copy-start(f32[8,192,128]{2,1,0:T(8,128)} %copy-done.1) | copy-start | bytes 2359300
  77.5 12.6 %copy-start.4 = (bf16[256,256]{1,0:T(8,128)(2,1)S(1)}, bf16[256,256]{1,0:T(8,128)(2,1)}, u32[]{:S(2)}) copy-start(bf16[256,256]{1,0:T(8,128)(2,1)} %wf_ref.1) | copy-start | bytes 393220
  77.5 12.6 %copy-start.6 = (bf16[192,192]{1,0:T(8,128)(2,1)S(1)}, bf16[192,192]{1,0:T(8,128)(2,1)}, u32[]{:S(2)}) copy-start(bf16[192,192]{1,0:T(8,128)(2,1)} %constant.46.clone.pinv_ref) | copy-start | bytes 221188
  77.5 12.6 %copy-start.11 = (f32[256]{0:T(256)S(1)}, f32[256]{0:T(256)}, u32[]{:S(2)}) copy-start(f32[256]{0:T(256)} %param.26) | copy-start | bytes 3076
  77.5 12.6 %all-to-all-start.2 = ((bf16[16,96,128]{2,1,0:T(8,128)(2,1)}), bf16[16,96,128]{2,1,0:T(8,128)(2,1)S(1)}, u32[]{:S(2)}, u32[]{:S(2)}) async-start(bf16[16,96,128]{2,1,0:T(8,128)(2,1)} %bitcast.12), calls=%async_computation.2 | async-start | bytes 786432 | tf_op jit(solution)/shard_map/all_to_all | solution.py:536
  90.2 26.9 %copy-start.15 = (bf16[1024,128]{1,0:T(8,128)(2,1)S(1)}, bf16[1024,128]{1,0:T(8,128)(2,1)}, u32[]{:S(2)}) copy-start(bf16[1024,128]{1,0:T(8,128)(2,1)} %param.29) | copy-start | bytes 786436
  94.0 11.3 %all-to-all-start.3 = ((bf16[8,192,128]{2,1,0:T(8,128)(2,1)}), bf16[8,192,128]{2,1,0:T(8,128)(2,1)S(1)}, u32[]{:S(2)}, u32[]{:S(2)}) async-start(bf16[8,192,128]{2,1,0:T(8,128)(2,1)} %get-tuple-element.31), calls=%async_computation.3 | async-start | bytes 786432 | tf_op jit(solution)/shard_map/all_to_all | solution.py:551
  97.5 10.6 %collective-permute-start.6 = (bf16[96,128]{1,0:T(8,128)(2,1)S(1)}, bf16[96,128]{1,0:T(8,128)(2,1)S(1)}, u32[]{:S(2)}, u32[]{:S(2)}) collective-permute-start(bf16[96,128]{1,0:T(8,128)(2,1)S(1)} %get-tuple-element.32), channel_id=1, source_target_pairs={{0,0},{1,1},{2,16},{3,17},{4,32},{5,33},{6,48},{7,49},{8,64},{9,65... | collective-permute-start | bytes 73736 | tf_op jit(solution)/shard_map/ppermute | solution.py:478
  98.1 9.9 %collective-permute-start.7 = (bf16[96,128]{1,0:T(8,128)(2,1)S(1)}, bf16[96,128]{1,0:T(8,128)(2,1)S(1)}, u32[]{:S(2)}, u32[]{:S(2)}) collective-permute-start(bf16[96,128]{1,0:T(8,128)(2,1)S(1)} %get-tuple-element.33), channel_id=1, source_target_pairs={{0,1},{1,0},{2,17},{3,16},{4,33},{5,32},{6,49},{7,48},{8,65},{9,64... | collective-permute-start | bytes 73736 | tf_op jit(solution)/shard_map/ppermute | solution.py:478
  105.3 18.9 %copy-start.12 = (bf16[8,192,128]{2,1,0:T(8,128)(2,1)}, bf16[8,192,128]{2,1,0:T(8,128)(2,1)S(1)}, u32[]{:S(2)}) copy-start(bf16[8,192,128]{2,1,0:T(8,128)(2,1)S(1)} %all-to-all-done.3.lo_ref) | copy-start | bytes 1179652
  105.3 18.1 %collective-permute-start.5 = (bf16[8,192,128]{2,1,0:T(8,128)(2,1)S(1)}, bf16[8,192,128]{2,1,0:T(8,128)(2,1)S(1)}, u32[]{:S(2)}, u32[]{:S(2)}) collective-permute-start(bf16[8,192,128]{2,1,0:T(8,128)(2,1)S(1)} %all-to-all-done.3.lo_ref), channel_id=1, source_target_pairs={{0,1},{1,0},{2,3},{3,2},{4,5},{5,4},{6,7},{7,6},{8,9},{9,8},{10,11... | collective-permute-start | bytes 1179656 | tf_op jit(solution)/shard_map/ppermute | solution.py:459
  108.9 14.5 %all-to-all-start.4 = ((bf16[8,2,96,128]{3,2,1,0:T(8,128)(2,1)}), bf16[8,2,96,128]{3,2,1,0:T(8,128)(2,1)S(1)}, u32[]{:S(2)}, u32[]{:S(2)}) async-start(bf16[8,2,96,128]{3,2,1,0:T(8,128)(2,1)} %broadcast_in_dim.29), calls=%async_computation.4 | async-start | bytes 786432 | tf_op jit(solution)/shard_map/all_to_all | solution.py:482
  123.4 0.9 copy-start.13
  123.4 0.8 copy-start.14
  (1 other events, 0.6 us)

commit v6 on v5

--- a/solution.py
+++ b/solution.py
@@ -314,7 +314,7 @@
 
 
 def finish_kernel(
-    at_ref, att_ref, gate_ref, x_ref, wf_ref, pinv_ref, g_ref, wl_ref, wr_ref, ac_ref, new_ref, left_ref, near_ref, far_ref
+    att_ref, gate_ref, x_ref, wf_ref, pinv_ref, g_ref, wl_ref, wr_ref, ac_ref, new_ref, left_ref, right_ref
 ):
     gated = jnp.concatenate(
         [(gate_ref[h] * att_ref[h].astype(F32)).astype(BF16) for h in range(HEADS)], axis=1
@@ -332,10 +332,7 @@
         n = normalised(new.astype(F32), g_ref[...])
         left = jnp.where(slot_one == s, mm(n, wl_ref[...]), left)
         right = jnp.where(slot_one == s, mm(n, wr_ref[...]), right)
-    right = right * ac_ref[...]
-    first = at_ref[1] == 0
-    near_ref[...] = jnp.where(first, right[:HALF], right[HALF:]).astype(BF16)
-    far_ref[...] = jnp.where(first, right[HALF:], right[:HALF]).astype(BF16)
+    right_ref[...] = (right * ac_ref[...]).astype(BF16)
     left = (left * ac_ref[...]).astype(BF16)
     for copy in range(PEERS_COL // 2):
         left_ref[copy] = left
@@ -347,10 +344,8 @@
         out_shape=(
             jax.ShapeDtypeStruct((SEQS, ROWS, EMB), BF16),
             jax.ShapeDtypeStruct((PEERS_COL // 2, ROWS, 128), BF16),
-            jax.ShapeDtypeStruct((HALF, 128), BF16),
-            jax.ShapeDtypeStruct((HALF, 128), BF16),
+            jax.ShapeDtypeStruct((ROWS, 128), BF16),
         ),
-        in_specs=[smem()] + [vmem()] * 9,
         compiler_params=params(24),
         name="finish",
     )(*args)
@@ -371,8 +366,8 @@
             for side, ref in enumerate((lo_ref, lp_ref)):
                 c = 2 * p + (core if side == 0 else 1 - core)
                 l_all[pl.ds(pl.multiple_of(c * ROWS, ROWS), ROWS)] = ref[p].astype(F32)
-                turned = jnp.transpose(jnp.concatenate([r_ref[p, side].astype(F32), pad], axis=0))
-                r_all[pl.ds(pl.multiple_of(c * 128, 128), 128)] = turned
+        for c in range(PEERS_COL):
+            r_all[128 * c : 128 * (c + 1)] = jnp.transpose(jnp.concatenate([r_ref[c].astype(F32), pad], axis=0))
         for q in range(8):
             lines = [
                 r_all[pl.ds(HEAD * s + 4 * q + b, PEERS_COL, stride=128), :] for b in range(4) for s in range(SEQS)
@@ -422,7 +417,7 @@
             smem(),
             pl.BlockSpec((PEERS_COL // 2, ROWS, 128), lambda t: (0, 0, 0)),
             pl.BlockSpec((PEERS_COL // 2, ROWS, 128), lambda t: (0, 0, 0)),
-            pl.BlockSpec((PEERS_COL // 2, 2, COLS, 128), lambda t: (0, 0, 0, 0)),
+            pl.BlockSpec((PEERS_COL, COLS, 128), lambda t: (0, 0, 0)),
             pl.BlockSpec((1024, PAIR), lambda t: (0, 0)),
             pl.BlockSpec((1, PAIR), lambda t: (0, 0)),
             smem(),
@@ -463,23 +458,14 @@
     return lax.ppermute(x, "y", [(a, (a + d) % 4) for a in range(4)])
 
 
-def turn_grid(x, cross):
-    def index(a, b, c, d, k):
-        return (((a * 2 + b) * 4 + c) * 2 + d) * 2 + k
+def turn_grid(x):
+    def index(a, b, c, d):
+        return ((a * 2 + b) * 4 + c) * 2 + d
 
     moves = [
-        (index(a, b, c, d, k), index(c, d, a, b, k ^ cross))
-        for a in range(4)
-        for b in range(2)
-        for c in range(4)
-        for d in range(2)
-        for k in range(2)
+        (index(a, b, c, d), index(c, d, a, b)) for a in range(4) for b in range(2) for c in range(4) for d in range(2)
     ]
-    return lax.ppermute(x, ROW + COL, moves)
-
-
-def to_all(x, axes, n):
-    return lax.all_to_all(jnp.broadcast_to(x[None], (n,) + x.shape), axes, 0, 0, tiled=True)
+    return lax.ppermute(x, ("x", "zl", "y", "zh"), moves)
 
 
 def on_device(
@@ -536,8 +522,7 @@
     attended = lax.all_to_all(attended, ROW + ("core",), 0, 0, tiled=True).reshape(HEADS, ROWS, 128)
 
     present = alignment_availability.astype(F32)
-    alignment_refreshed, left, near, far = finish(
-        at,
+    alignment_refreshed, left, right = finish(
         attended,
         gate,
         alignment_embedding,
@@ -549,8 +534,8 @@
         jnp.repeat(present.T, HEAD, axis=1),
     )
     left = lax.all_to_all(left, ("y", "zh"), 0, 0, tiled=True)
-    right = jnp.stack([turn_grid(near, 0), turn_grid(far, 1)])
-    right = to_all(right, ROW, 8)
+    right = jnp.broadcast_to(turn_grid(right)[None], (8, ROWS, 128)).reshape(PEERS_COL, COLS, 128)
+    right = lax.all_to_all(right, ROW + ("core",), 0, 0, tiled=True)
 
     projection = (tensor_projection_matrix.astype(F32) / 64).astype(BF16)
     projection = projection.reshape(HEAD, 8, 4, PAIR).transpose(1, 2, 0, 3).reshape(1024, PAIR)

time: 153 us -> 149 us (0.974)
  starting transfers between devices: 40.3 us -> 35.1 us
  waiting for transfers between devices: 40.6 us -> 44 us
    all_to_all x1, starting transfers between devices: 8.15 us -> 3.99 us  [on_device(): right = lax.all_to_all(right, ROW + ('core',), 0, 0, tiled=True)]
    all_to_all x1, waiting for transfers between devices: 5.49 us -> 7.71 us  [on_device(): right = lax.all_to_all(right, ROW + ('core',), 0, 0, tiled=True)]
  transfers between devices with their start and end apart: 13 -> 12, of which waited for: 6 -> 6; matrix products, arithmetic and copies ran while one was open for 2% -> 2% of each run, Pallas kernels for 12% -> 12%
where the time goes in v6:
time: 149 us; the launch traced here: 148 us
  Pallas kernels  62.6 us (42%)
  waiting for transfers between devices  44 us (30%)
  starting transfers between devices  35.1 us (24%)
  local copies, waits for them, and re-layouts  5.22 us (4%)
    pallas_call x1, Pallas kernels, outer_update(): pl.pallas_call(outer_kernel, out_shape=jax.ShapeDtypeStruct((ROWS, COLS,...  26.1 us
    ppermute x4, waiting for transfers between devices, along_y(): return lax.ppermute(x, 'y', [(a, (a + d) % 4) for a in range(4)])  13.3 us
    pallas_call x1, Pallas kernels, attend(): pl.pallas_call(attend_first_kernel, out_shape=(jax.ShapeDtypeStruct((2, 8...  11.8 us
    all_to_all x1, starting transfers between devices, on_device(): lax.all_to_all(bias, ROW + ('zh', 'core'), 0, 0, tiled=True)  9.56 us
    pallas_call x1, Pallas kernels, pair_bias(): pl.pallas_call(bias_kernel, out_shape=jax.ShapeDtypeStruct((HEADS, 2, 2 *...  8.29 us
    all_to_all x1, waiting for transfers between devices, on_device(): lax.all_to_all(attended, ROW + ('core',), 0, 0, tiled=True)  8.24 us
    all_to_all x1, waiting for transfers between devices, on_device(): right = lax.all_to_all(right, ROW + ('core',), 0, 0, tiled=True)  7.71 us
    pallas_call x1, Pallas kernels, attend(): pl.pallas_call(attend_last_kernel, out_shape=jax.ShapeDtypeStruct((8, 2,...  7.22 us
  transfers between devices with their start and end apart: 12, of which 6 were waited for; matrix products, arithmetic and copies ran while one was open for 2% of the time, Pallas kernels for 12%

profile of v6, /device:TPU:1, one launch (start us, length us, event | category | flops | bytes accessed | tf_op | source)
XLA Modules:
  0.0 148.0 jit_solution(5732386071910663270)
XLA Ops:
  0.7 8.3 %pair_bias.1 = bf16[8,2,48,384]{3,2,1,0:T(8,128)(2,1)} custom-call(bf16[18432,128]{1,0:T(8,128)(2,1)} %bitcast.36, f32[1,128]{1,0:T(1,128)} %bitcast.44, bf16[8,128]{1,0:T(8,128)(2,1)} %bitcast.43), custom_call_target="tpu_custom_call" | custom-call | tf_op jit(solution)/shard_map/pair_bias/pallas_call | solution.py:120
  9.0 9.6 %all-to-all-start = ((bf16[32,24,384]{2,1,0:T(8,128)(2,1)}), bf16[32,24,384]{2,1,0:T(8,128)(2,1)S(1)}, u32[]{:S(2)}, u32[]{:S(2)}) async-start(bf16[32,24,384]{2,1,0:T(8,128)(2,1)} %bitcast.37), calls=%async_computation | async-start | bytes 1179648 | tf_op jit(solution)/shard_map/all_to_all | solution.py:496
  18.7 0.7 dynamic_slice.7.ki_ref
  19.4 4.8 %project.1 = (bf16[8,592,128]{2,1,0:T(8,128)(2,1)}, f32[8,192,128]{2,1,0:T(8,128)S(1)}, f32[96,128]{1,0:T(8,128)S(1)}) custom-call(bf16[4,192,256]{2,1,0:T(8,128)(2,1)S(1)} %copy-done, f32[1,256]{1,0:T(1,128)S(1)} %bitcast.35, bf16[256,1024]{1,0:T(8,128)(2,1)S(1)} %copy-done.3, bf16[128,512]{1,0:T(8,128)(2,1)S(1)} %copy-done.5, ...), custom_call_target="tpu_custom_call" | custom-call | tf_op jit(solution)/shard_map/project/pallas_call | solution.py:91
  24.3 0.9 copy-done.1
  25.2 0.6 copy-done.8
  25.9 4.7 %all-to-all-done = bf16[32,24,384]{2,1,0:T(8,128)(2,1)S(1)} async-done(((bf16[32,24,384]{2,1,0:T(8,128)(2,1)}), bf16[32,24,384]{2,1,0:T(8,128)(2,1)S(1)}, u32[]{:S(2)}, u32[]{:S(2)}) %all-to-all-start) | async-done | bytes 589856 | tf_op jit(solution)/shard_map/all_to_all | solution.py:496
  30.5 3.6 %all-to-all-start.1 = ((bf16[8,592,128]{2,1,0:T(8,128)(2,1)}), bf16[8,592,128]{2,1,0:T(8,128)(2,1)S(1)}, u32[]{:S(2)}, u32[]{:S(2)}) async-start(bf16[8,592,128]{2,1,0:T(8,128)(2,1)} %get-tuple-element.20), calls=%async_computation.1 | async-start | bytes 2424832 | tf_op jit(solution)/shard_map/all_to_all | solution.py:517
  34.1 1.4 collective-permute-start
  35.5 1.5 %collective-permute-start.1 = (bf16[8,4,24,384]{3,2,1,0:T(8,128)(2,1)S(1)}, bf16[8,4,24,384]{3,2,1,0:T(8,128)(2,1)S(1)}, u32[]{:S(2)}, u32[]{:S(2)}) collective-permute-start(bf16[8,4,24,384]{3,2,1,0:T(8,128)(2,1)S(1)} %bitcast.31), channel_id=1, source_target_pairs={{0,12},{4,0},{8,4},{12,8},{1,13},{5,1},{9,5},{13,9},{2,14},{6,2},{... | collective-permute-start | bytes 1769480 | tf_op jit(solution)/shard_map/ppermute | solution.py:458
  37.0 13.2 %collective-permute-done.bp = bf16[8,4,24,384]{3,2,1,0:T(8,128)(2,1)S(1)} collective-permute-done((bf16[8,4,24,384]{3,2,1,0:T(8,128)(2,1)S(1)}, bf16[8,4,24,384]{3,2,1,0:T(8,128)(2,1)S(1)}, u32[]{:S(2)}, u32[]{:S(2)}) %collective-permute-start) | collective-permute-done | bytes 589856 | tf_op jit(solution)/shard_map/ppermute | solution.py:458
  50.2 3.0 %all-to-all-done.1.own_ref = bf16[8,592,128]{2,1,0:T(8,128)(2,1)S(1)} async-done(((bf16[8,592,128]{2,1,0:T(8,128)(2,1)}), bf16[8,592,128]{2,1,0:T(8,128)(2,1)S(1)}, u32[]{:S(2)}, u32[]{:S(2)}) %all-to-all-start.1) | async-done | bytes 1212448 | tf_op jit(solution)/shard_map/all_to_all | solution.py:517
  53.2 1.0 collective-permute-start.2
  54.2 1.4 collective-permute-start.3
  55.6 1.7 %collective-permute-start.4 = (bf16[8,2,24,384]{3,2,1,0:T(8,128)(2,1)S(1)}, bf16[8,2,24,384]{3,2,1,0:T(8,128)(2,1)S(1)}, u32[]{:S(2)}, u32[]{:S(2)}) collective-permute-start(bf16[8,2,24,384]{3,2,1,0:T(8,128)(2,1)S(1)} %slice.19), channel_id=1, source_target_pairs={{0,12},{4,0},{8,4},{12,8},{1,13},{5,1},{9,5},{13,9},{2,14},{6,2},{... | collective-permute-start | bytes 884744 | tf_op jit(solution)/shard_map/ppermute | solution.py:458
  57.3 1.1 prepare.1
  58.4 11.8 %attend_first.1 = (f32[2,768,256]{2,1,0:T(8,128)S(1)}, f32[2,4,768,128]{3,2,1,0:T(8,128)S(1)}) custom-call(bf16[2,192,1536]{2,1,0:T(8,128)(2,1)S(1)} %get-tuple-element.23.k_ref, bf16[2,1536,256]{2,1,0:T(8,128)(2,1)S(1)} %get-tuple-element.24.v_ref, bf16[2,8,96,128]{3,2,1,0:T(8,128)(2,1)S(1)} %get-tuple-element.25.q_ref, ...), custom_call_target="tpu_custom_call" | custom-call | tf_op jit(solution)/shard_map/attend_first/pallas_call | solution.py:275
  70.3 7.2 %attend_last.1 = bf16[8,2,96,128]{3,2,1,0:T(8,128)(2,1)} custom-call(s32[2]{0:T(128)S(1)} %pad_add_fusion.at_ref, bf16[2,192,1536]{2,1,0:T(8,128)(2,1)S(1)} %get-tuple-element.23.k_ref, bf16[2,1536,256]{2,1,0:T(8,128)(2,1)S(1)} %get-tuple-element.24.v_ref, bf16[2,8,96,128]{3,2,1,0:T(8,128)(2,1)S(1)} %get-tuple-element.25.q_ref, ...), custom_call_target="tpu_custom_call" | custom-call | tf_op jit(solution)/shard_map/attend_last/pallas_call | solution.py:295
  77.5 4.0 %all-to-all-start.2 = ((bf16[16,96,128]{2,1,0:T(8,128)(2,1)}), bf16[16,96,128]{2,1,0:T(8,128)(2,1)S(1)}, u32[]{:S(2)}, u32[]{:S(2)}) async-start(bf16[16,96,128]{2,1,0:T(8,128)(2,1)} %bitcast.12), calls=%async_computation.2 | async-start | bytes 786432 | tf_op jit(solution)/shard_map/all_to_all | solution.py:522
  81.6 0.1 copy.23.wl_ref
  81.9 8.2 %all-to-all-done.2 = bf16[16,96,128]{2,1,0:T(8,128)(2,1)S(1)} async-done(((bf16[16,96,128]{2,1,0:T(8,128)(2,1)}), bf16[16,96,128]{2,1,0:T(8,128)(2,1)S(1)}, u32[]{:S(2)}, u32[]{:S(2)}) %all-to-all-start.2) | async-done | bytes 393248 | tf_op jit(solution)/shard_map/all_to_all | solution.py:522
  90.2 3.3 %finish.1 = (bf16[4,192,256]{2,1,0:T(8,128)(2,1)}, bf16[8,192,128]{2,1,0:T(8,128)(2,1)}, bf16[192,128]{1,0:T(8,128)(2,1)S(1)}) custom-call(bf16[8,192,128]{2,1,0:T(8,128)(2,1)S(1)} %bitcast.33, f32[8,192,128]{2,1,0:T(8,128)S(1)} %copy-done.2, bf16[4,192,256]{2,1,0:T(8,128)(2,1)S(1)} %copy-done, bf16[256,256]{1,0:T(8,128)(2,1)S(1)} %copy-done.4, ...), custom_call_target="tpu_custom_call" | custom-call | tf_op jit(solution)/shard_map/finish/pallas_call | solution.py:342
  93.5 3.6 %all-to-all-start.3 = ((bf16[8,192,128]{2,1,0:T(8,128)(2,1)}), bf16[8,192,128]{2,1,0:T(8,128)(2,1)S(1)}, u32[]{:S(2)}, u32[]{:S(2)}) async-start(bf16[8,192,128]{2,1,0:T(8,128)(2,1)} %get-tuple-element.30), calls=%async_computation.3 | async-start | bytes 786432 | tf_op jit(solution)/shard_map/all_to_all | solution.py:536
  97.1 0.7 collective-permute-start.6
  97.7 7.1 %all-to-all-done.3.lo_ref = bf16[8,192,128]{2,1,0:T(8,128)(2,1)S(1)} async-done(((bf16[8,192,128]{2,1,0:T(8,128)(2,1)}), bf16[8,192,128]{2,1,0:T(8,128)(2,1)S(1)}, u32[]{:S(2)}, u32[]{:S(2)}) %all-to-all-start.3) | async-done | bytes 393248 | tf_op jit(solution)/shard_map/all_to_all | solution.py:536
  104.9 2.8 %collective-permute-start.5 = (bf16[8,192,128]{2,1,0:T(8,128)(2,1)S(1)}, bf16[8,192,128]{2,1,0:T(8,128)(2,1)S(1)}, u32[]{:S(2)}, u32[]{:S(2)}) collective-permute-start(bf16[8,192,128]{2,1,0:T(8,128)(2,1)S(1)} %all-to-all-done.3.lo_ref), channel_id=1, source_target_pairs={{0,1},{1,0},{2,3},{3,2},{4,5},{5,4},{6,7},{7,6},{8,9},{9,8},{10,11... | collective-permute-start | bytes 1179656 | tf_op jit(solution)/shard_map/ppermute | solution.py:454
  107.7 0.8 broadcast_in_dim.29
  108.5 4.0 %all-to-all-start.4 = ((bf16[16,96,128]{2,1,0:T(8,128)(2,1)}), bf16[16,96,128]{2,1,0:T(8,128)(2,1)S(1)}, u32[]{:S(2)}, u32[]{:S(2)}) async-start(bf16[16,96,128]{2,1,0:T(8,128)(2,1)} %bitcast.19), calls=%async_computation.4 | async-start | bytes 786432 | tf_op jit(solution)/shard_map/all_to_all | solution.py:538
  112.5 0.8 copy.26
  113.3 7.7 %all-to-all-done.4.r_ref = bf16[16,96,128]{2,1,0:T(8,128)(2,1)S(1)} async-done(((bf16[16,96,128]{2,1,0:T(8,128)(2,1)}), bf16[16,96,128]{2,1,0:T(8,128)(2,1)S(1)}, u32[]{:S(2)}, u32[]{:S(2)}) %all-to-all-start.4) | async-done | bytes 393248 | tf_op jit(solution)/shard_map/all_to_all | solution.py:538
  121.0 0.8 copy-done.14
  121.9 26.1 %outer_update.1 = bf16[192,96,128]{2,1,0:T(8,128)(2,1)} custom-call(s32[2]{0:T(128)} %copy-done.9, bf16[8,192,128]{2,1,0:T(8,128)(2,1)} %copy-done.12, bf16[8,192,128]{2,1,0:T(8,128)(2,1)} %copy-done.14, bf16[16,96,128]{2,1,0:T(8,128)(2,1)} %copy-done.13, bf16[1024,128]{1,0:T(8,128)(2,1)} %bitcast.38, f32[1,128]{1,0:T(1,128)} %bitcast.45, ...), custom_call_target="tpu_custom_call" | custom-call | tf_op jit(solution)/shard_map/outer_update/pallas_call | solution.py:412
  (59 shorter events, 0.7 us)
Async XLA Ops:
  0.6 17.9 %copy-start.19 = (s32[4,192]{1,0:T(4,128)S(1)}, s32[4,192]{1,0:T(4,128)}, u32[]{:S(2)}) copy-start(s32[4,192]{1,0:T(4,128)} %param.19) | copy-start | bytes 9220
  0.6 18.0 %copy-start.18 = (s32[1536]{0:T(1024)S(1)}, s32[1536]{0:T(1024)}, u32[]{:S(2)}) copy-start(s32[1536]{0:T(1024)} %param.20) | copy-start | bytes 18436
  0.7 18.7 %copy-start = (bf16[4,192,256]{2,1,0:T(8,128)(2,1)S(1)}, bf16[4,192,256]{2,1,0:T(8,128)(2,1)}, u32[]{:S(2)}) copy-start(bf16[4,192,256]{2,1,0:T(8,128)(2,1)} %x_ref.3) | copy-start | bytes 1179652
  0.7 18.7 %copy-start.5 = (bf16[128,512]{1,0:T(8,128)(2,1)S(1)}, bf16[128,512]{1,0:T(8,128)(2,1)}, u32[]{:S(2)}) copy-start(bf16[128,512]{1,0:T(8,128)(2,1)} %constant.44.clone.e_ref) | copy-start | bytes 393220
  0.7 18.7 %copy-start.7 = (bf16[192,192]{1,0:T(8,128)(2,1)S(1)}, bf16[192,192]{1,0:T(8,128)(2,1)}, u32[]{:S(2)}) copy-start(bf16[192,192]{1,0:T(8,128)(2,1)} %constant.45.clone.p_ref) | copy-start | bytes 221188
  0.7 18.7 %copy-start.11 = (f32[256]{0:T(256)S(1)}, f32[256]{0:T(256)}, u32[]{:S(2)}) copy-start(f32[256]{0:T(256)} %param.21) | copy-start | bytes 3076
  9.0 10.5 %copy-start.3 = (bf16[256,1024]{1,0:T(8,128)(2,1)S(1)}, bf16[256,1024]{1,0:T(8,128)(2,1)}, u32[]{:S(2)}) copy-start(bf16[256,1024]{1,0:T(8,128)(2,1)} %w_ref.1) | copy-start | bytes 1572868
  9.0 21.5 %all-to-all-start = ((bf16[32,24,384]{2,1,0:T(8,128)(2,1)}), bf16[32,24,384]{2,1,0:T(8,128)(2,1)S(1)}, u32[]{:S(2)}, u32[]{:S(2)}) async-start(bf16[32,24,384]{2,1,0:T(8,128)(2,1)} %bitcast.37), calls=%async_computation | async-start | bytes 1179648 | tf_op jit(solution)/shard_map/all_to_all | solution.py:496
  24.3 0.9 copy-start.1
  25.2 0.6 copy-start.8
  25.9 44.4 %copy-start.9 = (s32[2]{0:T(128)}, s32[2]{0:T(128)S(1)}, u32[]{:S(2)}) copy-start(s32[2]{0:T(128)S(1)} %pad_add_fusion.at_ref) | copy-start | bytes 28
  30.5 22.7 %all-to-all-start.1 = ((bf16[8,592,128]{2,1,0:T(8,128)(2,1)}), bf16[8,592,128]{2,1,0:T(8,128)(2,1)S(1)}, u32[]{:S(2)}, u32[]{:S(2)}) async-start(bf16[8,592,128]{2,1,0:T(8,128)(2,1)} %get-tuple-element.20), calls=%async_computation.1 | async-start | bytes 2424832 | tf_op jit(solution)/shard_map/all_to_all | solution.py:517
  34.1 16.1 %collective-permute-start = (bf16[8,4,24,384]{3,2,1,0:T(8,128)(2,1)S(1)}, bf16[8,4,24,384]{3,2,1,0:T(8,128)(2,1)S(1)}, u32[]{:S(2)}, u32[]{:S(2)}) collective-permute-start(bf16[8,4,24,384]{3,2,1,0:T(8,128)(2,1)S(1)} %bitcast.30), channel_id=1, source_target_pairs={{0,4},{4,8},{8,12},{12,0},{1,5},{5,9},{9,13},{13,1},{2,6},{6,10},{... | collective-permute-start | bytes 1769480 | tf_op jit(solution)/shard_map/ppermute | solution.py:458
  35.5 14.8 %collective-permute-start.1 = (bf16[8,4,24,384]{3,2,1,0:T(8,128)(2,1)S(1)}, bf16[8,4,24,384]{3,2,1,0:T(8,128)(2,1)S(1)}, u32[]{:S(2)}, u32[]{:S(2)}) collective-permute-start(bf16[8,4,24,384]{3,2,1,0:T(8,128)(2,1)S(1)} %bitcast.31), channel_id=1, source_target_pairs={{0,12},{4,0},{8,4},{12,8},{1,13},{5,1},{9,5},{13,9},{2,14},{6,2},{... | collective-permute-start | bytes 1769480 | tf_op jit(solution)/shard_map/ppermute | solution.py:458
  53.2 4.2 %collective-permute-start.2 = (bf16[8,592,128]{2,1,0:T(8,128)(2,1)S(1)}, bf16[8,592,128]{2,1,0:T(8,128)(2,1)S(1)}, u32[]{:S(2)}, u32[]{:S(2)}) collective-permute-start(bf16[8,592,128]{2,1,0:T(8,128)(2,1)S(1)} %all-to-all-done.1.own_ref), channel_id=1, source_target_pairs={{0,1},{1,0},{2,3},{3,2},{4,5},{5,4},{6,7},{7,6},{8,9},{9,8},{10,11... | collective-permute-start | bytes 3637256 | tf_op jit(solution)/shard_map/ppermute | solution.py:454
  54.2 16.0 %collective-permute-start.3 = (bf16[8,2,24,384]{3,2,1,0:T(8,128)(2,1)S(1)}, bf16[8,2,24,384]{3,2,1,0:T(8,128)(2,1)S(1)}, u32[]{:S(2)}, u32[]{:S(2)}) collective-permute-start(bf16[8,2,24,384]{3,2,1,0:T(8,128)(2,1)S(1)} %slice.18), channel_id=1, source_target_pairs={{0,4},{4,8},{8,12},{12,0},{1,5},{5,9},{9,13},{13,1},{2,6},{6,10},{... | collective-permute-start | bytes 884744 | tf_op jit(solution)/shard_map/ppermute | solution.py:458
  55.6 14.6 %collective-permute-start.4 = (bf16[8,2,24,384]{3,2,1,0:T(8,128)(2,1)S(1)}, bf16[8,2,24,384]{3,2,1,0:T(8,128)(2,1)S(1)}, u32[]{:S(2)}, u32[]{:S(2)}) collective-permute-start(bf16[8,2,24,384]{3,2,1,0:T(8,128)(2,1)S(1)} %slice.19), channel_id=1, source_target_pairs={{0,12},{4,0},{8,4},{12,8},{1,13},{5,1},{9,5},{13,9},{2,14},{6,2},{... | collective-permute-start | bytes 884744 | tf_op jit(solution)/shard_map/ppermute | solution.py:458
  70.3 11.3 %copy-start.16 = (bf16[256,32]{0,1:T(8,128)(2,1)S(1)}, bf16[256,32]{0,1:T(8,128)(2,1)}, u32[]{:S(2)}) copy-start(bf16[256,32]{0,1:T(8,128)(2,1)} %param.27) | copy-start | bytes 49156
  70.3 11.5 %copy-start.17 = (bf16[256,32]{0,1:T(8,128)(2,1)S(1)}, bf16[256,32]{0,1:T(8,128)(2,1)}, u32[]{:S(2)}) copy-start(bf16[256,32]{0,1:T(8,128)(2,1)} %param.28) | copy-start | bytes 49156
  77.5 12.6 %copy-start.2 = (f32[8,192,128]{2,1,0:T(8,128)S(1)}, f32[8,192,128]{2,1,0:T(8,128)}, u32[]{:S(2)}) copy-start(f32[8,192,128]{2,1,0:T(8,128)} %copy-done.1) | copy-start | bytes 2359300
  77.5 12.6 %copy-start.4 = (bf16[256,256]{1,0:T(8,128)(2,1)S(1)}, bf16[256,256]{1,0:T(8,128)(2,1)}, u32[]{:S(2)}) copy-start(bf16[256,256]{1,0:T(8,128)(2,1)} %wf_ref.1) | copy-start | bytes 393220
  77.5 12.6 %copy-start.6 = (bf16[192,192]{1,0:T(8,128)(2,1)S(1)}, bf16[192,192]{1,0:T(8,128)(2,1)}, u32[]{:S(2)}) copy-start(bf16[192,192]{1,0:T(8,128)(2,1)} %constant.46.clone.pinv_ref) | copy-start | bytes 221188
  77.5 12.6 %copy-start.10 = (f32[256]{0:T(256)S(1)}, f32[256]{0:T(256)}, u32[]{:S(2)}) copy-start(f32[256]{0:T(256)} %param.26) | copy-start | bytes 3076
  77.5 12.6 %all-to-all-start.2 = ((bf16[16,96,128]{2,1,0:T(8,128)(2,1)}), bf16[16,96,128]{2,1,0:T(8,128)(2,1)S(1)}, u32[]{:S(2)}, u32[]{:S(2)}) async-start(bf16[16,96,128]{2,1,0:T(8,128)(2,1)} %bitcast.12), calls=%async_computation.2 | async-start | bytes 786432 | tf_op jit(solution)/shard_map/all_to_all | solution.py:522
  93.5 19.0 %copy-start.15 = (bf16[1024,128]{1,0:T(8,128)(2,1)S(1)}, bf16[1024,128]{1,0:T(8,128)(2,1)}, u32[]{:S(2)}) copy-start(bf16[1024,128]{1,0:T(8,128)(2,1)} %param.29) | copy-start | bytes 786436
  93.5 11.4 %all-to-all-start.3 = ((bf16[8,192,128]{2,1,0:T(8,128)(2,1)}), bf16[8,192,128]{2,1,0:T(8,128)(2,1)S(1)}, u32[]{:S(2)}, u32[]{:S(2)}) async-start(bf16[8,192,128]{2,1,0:T(8,128)(2,1)} %get-tuple-element.30), calls=%async_computation.3 | async-start | bytes 786432 | tf_op jit(solution)/shard_map/all_to_all | solution.py:536
  97.1 10.6 %collective-permute-start.6 = (bf16[192,128]{1,0:T(8,128)(2,1)S(1)}, bf16[192,128]{1,0:T(8,128)(2,1)S(1)}, u32[]{:S(2)}, u32[]{:S(2)}) collective-permute-start(bf16[192,128]{1,0:T(8,128)(2,1)S(1)} %get-tuple-element.31), channel_id=1, source_target_pairs={{0,0},{2,16},{4,32},{6,48},{8,64},{10,80},{12,96},{14,112},{16,2},... | collective-permute-start | bytes 147464 | tf_op jit(solution)/shard_map/ppermute | solution.py:468
  104.9 17.0 %copy-start.12 = (bf16[8,192,128]{2,1,0:T(8,128)(2,1)}, bf16[8,192,128]{2,1,0:T(8,128)(2,1)S(1)}, u32[]{:S(2)}) copy-start(bf16[8,192,128]{2,1,0:T(8,128)(2,1)S(1)} %all-to-all-done.3.lo_ref) | copy-start | bytes 1179652
  104.9 16.2 %collective-permute-start.5 = (bf16[8,192,128]{2,1,0:T(8,128)(2,1)S(1)}, bf16[8,192,128]{2,1,0:T(8,128)(2,1)S(1)}, u32[]{:S(2)}, u32[]{:S(2)}) collective-permute-start(bf16[8,192,128]{2,1,0:T(8,128)(2,1)S(1)} %all-to-all-done.3.lo_ref), channel_id=1, source_target_pairs={{0,1},{1,0},{2,3},{3,2},{4,5},{5,4},{6,7},{7,6},{8,9},{9,8},{10,11... | collective-permute-start | bytes 1179656 | tf_op jit(solution)/shard_map/ppermute | solution.py:454
  108.5 12.6 %all-to-all-start.4 = ((bf16[16,96,128]{2,1,0:T(8,128)(2,1)}), bf16[16,96,128]{2,1,0:T(8,128)(2,1)S(1)}, u32[]{:S(2)}, u32[]{:S(2)}) async-start(bf16[16,96,128]{2,1,0:T(8,128)(2,1)} %bitcast.19), calls=%async_computation.4 | async-start | bytes 786432 | tf_op jit(solution)/shard_map/all_to_all | solution.py:538
  121.0 0.9 copy-start.13
  121.0 0.8 copy-start.14

commit v7 on v6

--- a/solution.py
+++ b/solution.py
@@ -355,17 +355,31 @@
 PART = 16
 
 
-def outer_kernel(at_ref, lo_ref, lp_ref, r_ref, w_ref, off_ref, ki_ref, kj_ref, z_ref, o_ref, l_all, r_all, lhs, rhs, *obf):
+def lines_kernel(at_ref, lo_ref, lp_ref, o_ref):
+    core = at_ref[1]
+    for p in range(PEERS_COL // 2):
+        for side, ref in enumerate((lo_ref, lp_ref)):
+            c = 2 * p + (core if side == 0 else 1 - core)
+            o_ref[pl.ds(pl.multiple_of(c * ROWS, ROWS), ROWS)] = ref[p].astype(F32)
+
+
+def lines(at, left_own, left_par):
+    return pl.pallas_call(
+        lines_kernel,
+        out_shape=jax.ShapeDtypeStruct((PEERS_COL * ROWS, 128), F32),
+        in_specs=[smem(), vmem(), vmem()],
+        out_specs=vmem(),
+        compiler_params=params(16),
+        name="lines",
+    )(at, left_own, left_par)
+
+
+def outer_kernel(l_all, r_ref, w_ref, off_ref, ki_ref, kj_ref, z_ref, o_ref, r_all, lhs, rhs, *obf):
     step = pl.program_id(0)
 
     @pl.when(step == 0)
     def _():
-        core = at_ref[1]
         pad = jnp.zeros((128 - COLS, 128), F32)
-        for p in range(PEERS_COL // 2):
-            for side, ref in enumerate((lo_ref, lp_ref)):
-                c = 2 * p + (core if side == 0 else 1 - core)
-                l_all[pl.ds(pl.multiple_of(c * ROWS, ROWS), ROWS)] = ref[p].astype(F32)
         for c in range(PEERS_COL):
             r_all[128 * c : 128 * (c + 1)] = jnp.transpose(jnp.concatenate([r_ref[c].astype(F32), pad], axis=0))
         for q in range(8):
@@ -408,15 +422,13 @@
     project_part(STEP // PART - 1)
 
 
-def outer_update(at, left_own, left_par, right, w, offset, keep_i, keep_j, z):
+def outer_update(left, right, w, offset, keep_i, keep_j, z):
     return pl.pallas_call(
         outer_kernel,
         out_shape=jax.ShapeDtypeStruct((ROWS, COLS, PAIR), BF16),
         grid=(ROWS // STEP,),
         in_specs=[
-            smem(),
-            pl.BlockSpec((PEERS_COL // 2, ROWS, 128), lambda t: (0, 0, 0)),
-            pl.BlockSpec((PEERS_COL // 2, ROWS, 128), lambda t: (0, 0, 0)),
+            pl.BlockSpec((PEERS_COL * ROWS, 128), lambda t: (0, 0)),
             pl.BlockSpec((PEERS_COL, COLS, 128), lambda t: (0, 0, 0)),
             pl.BlockSpec((1024, PAIR), lambda t: (0, 0)),
             pl.BlockSpec((1, PAIR), lambda t: (0, 0)),
@@ -426,7 +438,6 @@
         ],
         out_specs=pl.BlockSpec((STEP, COLS, PAIR), lambda t: (t, 0, 0)),
         scratch_shapes=[
-            pltpu.VMEM((PEERS_COL * ROWS, 128), F32),
             pltpu.VMEM((PEERS_COL * 128, 128), F32),
             pltpu.VMEM((8 * COLS, EMB), BF16),
             pltpu.VMEM((256, 128 * STEP), BF16),
@@ -435,7 +446,7 @@
         ],
         compiler_params=params(63),
         name="outer_update",
-    )(at, left_own, left_par, right, w, offset, keep_i, keep_j, z)
+    )(left, right, w, offset, keep_i, keep_j, z)
 
 
 def tables():
@@ -540,9 +551,7 @@
     projection = (tensor_projection_matrix.astype(F32) / 64).astype(BF16)
     projection = projection.reshape(HEAD, 8, 4, PAIR).transpose(1, 2, 0, 3).reshape(1024, PAIR)
     couplings_refreshed = outer_update(
-        at,
-        left,
-        swap_cores(left),
+        lines(at, left, swap_cores(left)),
         right,
         projection,
         tensor_offset_vector[None],

time: 149 us -> 148 us (level)
  waiting for transfers between devices: 44 us -> 42.2 us
    all_to_all x1, waiting for transfers between devices: 7.71 us -> 5.85 us  [on_device(): right = lax.all_to_all(right, ROW + ('core',), 0, 0, tiled=True)]
    unnamed x40 -> x36, local copies, waits for them, and re-layouts: 2.48 us -> 3.5 us
where the time goes in v7:
time: 148 us
  Pallas kernels  63.4 us (43%)
  waiting for transfers between devices  42.2 us (29%)
  starting transfers between devices  35 us (24%)
  local copies, waits for them, and re-layouts  6.2 us (4%)
    pallas_call x1, Pallas kernels, outer_update(): pl.pallas_call(outer_kernel, out_shape=jax.ShapeDtypeStruct((ROWS, COLS,...  26.3 us
    ppermute x4, waiting for transfers between devices, along_y(): return lax.ppermute(x, 'y', [(a, (a + d) % 4) for a in range(4)])  13.3 us
    pallas_call x1, Pallas kernels, attend(): pl.pallas_call(attend_first_kernel, out_shape=(jax.ShapeDtypeStruct((2, 8...  11.8 us
    all_to_all x1, starting transfers between devices, on_device(): lax.all_to_all(bias, ROW + ('zh', 'core'), 0, 0, tiled=True)  9.56 us
    pallas_call x1, Pallas kernels, pair_bias(): pl.pallas_call(bias_kernel, out_shape=jax.ShapeDtypeStruct((HEADS, 2, 2 *...  8.27 us
    all_to_all x1, waiting for transfers between devices, on_device(): lax.all_to_all(attended, ROW + ('core',), 0, 0, tiled=True)  8.24 us
    pallas_call x1, Pallas kernels, attend(): pl.pallas_call(attend_last_kernel, out_shape=jax.ShapeDtypeStruct((8, 2,...  7.21 us
    all_to_all x1, waiting for transfers between devices, on_device(): left = lax.all_to_all(left, ('y', 'zh'), 0, 0, tiled=True)  7.14 us
  transfers between devices with their start and end apart: 12, of which 6 were waited for; matrix products, arithmetic and copies ran while one was open for 2% of the time, Pallas kernels for 12%

profile of v7, /device:TPU:1, one launch (start us, length us, event | category | flops | bytes accessed | tf_op | source)
XLA Modules:
  0.0 147.9 jit_solution(4783853511381275122)
XLA Ops:
  0.7 8.3 %pair_bias.1 = bf16[8,2,48,384]{3,2,1,0:T(8,128)(2,1)} custom-call(bf16[18432,128]{1,0:T(8,128)(2,1)} %bitcast.36, f32[1,128]{1,0:T(1,128)} %bitcast.44, bf16[8,128]{1,0:T(8,128)(2,1)} %bitcast.43), custom_call_target="tpu_custom_call" | custom-call | tf_op jit(solution)/shard_map/pair_bias/pallas_call | solution.py:120
  9.0 9.6 %all-to-all-start = ((bf16[32,24,384]{2,1,0:T(8,128)(2,1)}), bf16[32,24,384]{2,1,0:T(8,128)(2,1)S(1)}, u32[]{:S(2)}, u32[]{:S(2)}) async-start(bf16[32,24,384]{2,1,0:T(8,128)(2,1)} %bitcast.37), calls=%async_computation | async-start | bytes 1179648 | tf_op jit(solution)/shard_map/all_to_all | solution.py:507
  19.4 4.8 %project.1 = (bf16[8,592,128]{2,1,0:T(8,128)(2,1)}, f32[8,192,128]{2,1,0:T(8,128)S(1)}, f32[96,128]{1,0:T(8,128)S(1)}) custom-call(bf16[4,192,256]{2,1,0:T(8,128)(2,1)S(1)} %copy-done.1, f32[1,256]{1,0:T(1,128)S(1)} %bitcast.35, bf16[256,1024]{1,0:T(8,128)(2,1)S(1)} %copy-done.4, bf16[128,512]{1,0:T(8,128)(2,1)S(1)} %copy-done.6, ...), custom_call_target="tpu_custom_call" | custom-call | tf_op jit(solution)/shard_map/project/pallas_call | solution.py:91
  24.2 0.9 copy-done.2
  25.1 0.6 copy-done.9
  25.8 4.7 %all-to-all-done = bf16[32,24,384]{2,1,0:T(8,128)(2,1)S(1)} async-done(((bf16[32,24,384]{2,1,0:T(8,128)(2,1)}), bf16[32,24,384]{2,1,0:T(8,128)(2,1)S(1)}, u32[]{:S(2)}, u32[]{:S(2)}) %all-to-all-start) | async-done | bytes 589856 | tf_op jit(solution)/shard_map/all_to_all | solution.py:507
  30.5 3.6 %all-to-all-start.1 = ((bf16[8,592,128]{2,1,0:T(8,128)(2,1)}), bf16[8,592,128]{2,1,0:T(8,128)(2,1)S(1)}, u32[]{:S(2)}, u32[]{:S(2)}) async-start(bf16[8,592,128]{2,1,0:T(8,128)(2,1)} %get-tuple-element.20), calls=%async_computation.1 | async-start | bytes 2424832 | tf_op jit(solution)/shard_map/all_to_all | solution.py:528
  34.1 1.4 collective-permute-start
  35.4 1.5 %collective-permute-start.1 = (bf16[8,4,24,384]{3,2,1,0:T(8,128)(2,1)S(1)}, bf16[8,4,24,384]{3,2,1,0:T(8,128)(2,1)S(1)}, u32[]{:S(2)}, u32[]{:S(2)}) collective-permute-start(bf16[8,4,24,384]{3,2,1,0:T(8,128)(2,1)S(1)} %bitcast.31), channel_id=1, source_target_pairs={{0,12},{4,0},{8,4},{12,8},{1,13},{5,1},{9,5},{13,9},{2,14},{6,2},{... | collective-permute-start | bytes 1769480 | tf_op jit(solution)/shard_map/ppermute | solution.py:469
  37.0 13.2 %collective-permute-done.bp = bf16[8,4,24,384]{3,2,1,0:T(8,128)(2,1)S(1)} collective-permute-done((bf16[8,4,24,384]{3,2,1,0:T(8,128)(2,1)S(1)}, bf16[8,4,24,384]{3,2,1,0:T(8,128)(2,1)S(1)}, u32[]{:S(2)}, u32[]{:S(2)}) %collective-permute-start) | collective-permute-done | bytes 589856 | tf_op jit(solution)/shard_map/ppermute | solution.py:469
  50.2 3.0 %all-to-all-done.1.own_ref = bf16[8,592,128]{2,1,0:T(8,128)(2,1)S(1)} async-done(((bf16[8,592,128]{2,1,0:T(8,128)(2,1)}), bf16[8,592,128]{2,1,0:T(8,128)(2,1)S(1)}, u32[]{:S(2)}, u32[]{:S(2)}) %all-to-all-start.1) | async-done | bytes 1212448 | tf_op jit(solution)/shard_map/all_to_all | solution.py:528
  53.2 1.0 collective-permute-start.2
  54.2 1.4 collective-permute-start.3
  55.6 1.7 %collective-permute-start.4 = (bf16[8,2,24,384]{3,2,1,0:T(8,128)(2,1)S(1)}, bf16[8,2,24,384]{3,2,1,0:T(8,128)(2,1)S(1)}, u32[]{:S(2)}, u32[]{:S(2)}) collective-permute-start(bf16[8,2,24,384]{3,2,1,0:T(8,128)(2,1)S(1)} %slice.19), channel_id=1, source_target_pairs={{0,12},{4,0},{8,4},{12,8},{1,13},{5,1},{9,5},{13,9},{2,14},{6,2},{... | collective-permute-start | bytes 884744 | tf_op jit(solution)/shard_map/ppermute | solution.py:469
  57.3 1.1 prepare.1
  58.4 11.8 %attend_first.1 = (f32[2,768,256]{2,1,0:T(8,128)S(1)}, f32[2,4,768,128]{3,2,1,0:T(8,128)S(1)}) custom-call(bf16[2,192,1536]{2,1,0:T(8,128)(2,1)S(1)} %get-tuple-element.23.k_ref, bf16[2,1536,256]{2,1,0:T(8,128)(2,1)S(1)} %get-tuple-element.24.v_ref, bf16[2,8,96,128]{3,2,1,0:T(8,128)(2,1)S(1)} %get-tuple-element.25.q_ref, ...), custom_call_target="tpu_custom_call" | custom-call | tf_op jit(solution)/shard_map/attend_first/pallas_call | solution.py:275
  70.3 7.2 %attend_last.1 = bf16[8,2,96,128]{3,2,1,0:T(8,128)(2,1)} custom-call(s32[2]{0:T(128)S(1)} %pad_add_fusion.at_ref, bf16[2,192,1536]{2,1,0:T(8,128)(2,1)S(1)} %get-tuple-element.23.k_ref, bf16[2,1536,256]{2,1,0:T(8,128)(2,1)S(1)} %get-tuple-element.24.v_ref, bf16[2,8,96,128]{3,2,1,0:T(8,128)(2,1)S(1)} %get-tuple-element.25.q_ref, ...), custom_call_target="tpu_custom_call" | custom-call | tf_op jit(solution)/shard_map/attend_last/pallas_call | solution.py:295
  77.5 4.0 %all-to-all-start.2 = ((bf16[16,96,128]{2,1,0:T(8,128)(2,1)}), bf16[16,96,128]{2,1,0:T(8,128)(2,1)S(1)}, u32[]{:S(2)}, u32[]{:S(2)}) async-start(bf16[16,96,128]{2,1,0:T(8,128)(2,1)} %bitcast.12), calls=%async_computation.2 | async-start | bytes 786432 | tf_op jit(solution)/shard_map/all_to_all | solution.py:533
  81.9 8.2 %all-to-all-done.2 = bf16[16,96,128]{2,1,0:T(8,128)(2,1)S(1)} async-done(((bf16[16,96,128]{2,1,0:T(8,128)(2,1)}), bf16[16,96,128]{2,1,0:T(8,128)(2,1)S(1)}, u32[]{:S(2)}, u32[]{:S(2)}) %all-to-all-start.2) | async-done | bytes 393248 | tf_op jit(solution)/shard_map/all_to_all | solution.py:533
  90.1 3.3 %finish.1 = (bf16[4,192,256]{2,1,0:T(8,128)(2,1)}, bf16[8,192,128]{2,1,0:T(8,128)(2,1)}, bf16[192,128]{1,0:T(8,128)(2,1)S(1)}) custom-call(bf16[8,192,128]{2,1,0:T(8,128)(2,1)S(1)} %bitcast.33, f32[8,192,128]{2,1,0:T(8,128)S(1)} %copy-done.3, bf16[4,192,256]{2,1,0:T(8,128)(2,1)S(1)} %copy-done.1, bf16[256,256]{1,0:T(8,128)(2,1)S(1)} %copy-done.5, ...), custom_call_target="tpu_custom_call" | custom-call | tf_op jit(solution)/shard_map/finish/pallas_call | solution.py:342
  93.4 3.5 %all-to-all-start.3 = ((bf16[8,192,128]{2,1,0:T(8,128)(2,1)}), bf16[8,192,128]{2,1,0:T(8,128)(2,1)S(1)}, u32[]{:S(2)}, u32[]{:S(2)}) async-start(bf16[8,192,128]{2,1,0:T(8,128)(2,1)} %get-tuple-element.30), calls=%async_computation.3 | async-start | bytes 786432 | tf_op jit(solution)/shard_map/all_to_all | solution.py:547
  96.9 0.7 collective-permute-start.6
  97.6 7.1 %all-to-all-done.3.lo_ref = bf16[8,192,128]{2,1,0:T(8,128)(2,1)S(1)} async-done(((bf16[8,192,128]{2,1,0:T(8,128)(2,1)}), bf16[8,192,128]{2,1,0:T(8,128)(2,1)S(1)}, u32[]{:S(2)}, u32[]{:S(2)}) %all-to-all-start.3) | async-done | bytes 393248 | tf_op jit(solution)/shard_map/all_to_all | solution.py:547
  104.7 2.8 %collective-permute-start.5 = (bf16[8,192,128]{2,1,0:T(8,128)(2,1)S(1)}, bf16[8,192,128]{2,1,0:T(8,128)(2,1)S(1)}, u32[]{:S(2)}, u32[]{:S(2)}) collective-permute-start(bf16[8,192,128]{2,1,0:T(8,128)(2,1)S(1)} %all-to-all-done.3.lo_ref), channel_id=1, source_target_pairs={{0,1},{1,0},{2,3},{3,2},{4,5},{5,4},{6,7},{7,6},{8,9},{9,8},{10,11... | collective-permute-start | bytes 1179656 | tf_op jit(solution)/shard_map/ppermute | solution.py:465
  107.5 0.8 broadcast_in_dim.29
  108.3 4.0 %all-to-all-start.4 = ((bf16[16,96,128]{2,1,0:T(8,128)(2,1)}), bf16[16,96,128]{2,1,0:T(8,128)(2,1)S(1)}, u32[]{:S(2)}, u32[]{:S(2)}) async-start(bf16[16,96,128]{2,1,0:T(8,128)(2,1)} %bitcast.19), calls=%async_computation.4 | async-start | bytes 786432 | tf_op jit(solution)/shard_map/all_to_all | solution.py:549
  112.4 0.8 copy.26
  113.2 0.6 lines.1.l_all
  113.9 1.2 copy-done
  115.0 5.8 %all-to-all-done.4.r_ref = bf16[16,96,128]{2,1,0:T(8,128)(2,1)S(1)} async-done(((bf16[16,96,128]{2,1,0:T(8,128)(2,1)}), bf16[16,96,128]{2,1,0:T(8,128)(2,1)S(1)}, u32[]{:S(2)}, u32[]{:S(2)}) %all-to-all-start.4) | async-done | bytes 393248 | tf_op jit(solution)/shard_map/all_to_all | solution.py:549
  120.9 0.8 copy-done.12
  121.6 26.3 %outer_update.1 = bf16[192,96,128]{2,1,0:T(8,128)(2,1)} custom-call(f32[3072,128]{1,0:T(8,128)} %copy-done, bf16[16,96,128]{2,1,0:T(8,128)(2,1)} %copy-done.12, bf16[1024,128]{1,0:T(8,128)(2,1)} %bitcast.38, f32[1,128]{1,0:T(1,128)} %bitcast.45, f32[192]{0:T(256)} %dynamic_slice.7.ki_ref, f32[96,128]{1,0:T(8,128)} %copy-done.9, bf16[192,96,128]{2,1,0:T(8,128)(2,1)} %z_ref.1), custom_call_target="tpu_custom_call" | custom-call | tf_op jit(solution)/shard_map/outer_update/pallas_call | solution.py:426
  (56 shorter events, 1.3 us)
Async XLA Ops:
  0.6 17.9 %copy-start.17 = (s32[4,192]{1,0:T(4,128)S(1)}, s32[4,192]{1,0:T(4,128)}, u32[]{:S(2)}) copy-start(s32[4,192]{1,0:T(4,128)} %param.19) | copy-start | bytes 9220
  0.6 17.9 %copy-start.16 = (s32[1536]{0:T(1024)S(1)}, s32[1536]{0:T(1024)}, u32[]{:S(2)}) copy-start(s32[1536]{0:T(1024)} %param.20) | copy-start | bytes 18436
  0.7 18.7 %copy-start.1 = (bf16[4,192,256]{2,1,0:T(8,128)(2,1)S(1)}, bf16[4,192,256]{2,1,0:T(8,128)(2,1)}, u32[]{:S(2)}) copy-start(bf16[4,192,256]{2,1,0:T(8,128)(2,1)} %x_ref.3) | copy-start | bytes 1179652
  0.7 18.7 %copy-start.6 = (bf16[128,512]{1,0:T(8,128)(2,1)S(1)}, bf16[128,512]{1,0:T(8,128)(2,1)}, u32[]{:S(2)}) copy-start(bf16[128,512]{1,0:T(8,128)(2,1)} %constant.44.clone.e_ref) | copy-start | bytes 393220
  0.7 18.7 %copy-start.8 = (bf16[192,192]{1,0:T(8,128)(2,1)S(1)}, bf16[192,192]{1,0:T(8,128)(2,1)}, u32[]{:S(2)}) copy-start(bf16[192,192]{1,0:T(8,128)(2,1)} %constant.45.clone.p_ref) | copy-start | bytes 221188
  0.7 18.7 %copy-start.11 = (f32[256]{0:T(256)S(1)}, f32[256]{0:T(256)}, u32[]{:S(2)}) copy-start(f32[256]{0:T(256)} %param.21) | copy-start | bytes 3076
  9.0 10.4 %copy-start.4 = (bf16[256,1024]{1,0:T(8,128)(2,1)S(1)}, bf16[256,1024]{1,0:T(8,128)(2,1)}, u32[]{:S(2)}) copy-start(bf16[256,1024]{1,0:T(8,128)(2,1)} %w_ref.1) | copy-start | bytes 1572868
  9.0 21.5 %all-to-all-start = ((bf16[32,24,384]{2,1,0:T(8,128)(2,1)}), bf16[32,24,384]{2,1,0:T(8,128)(2,1)S(1)}, u32[]{:S(2)}, u32[]{:S(2)}) async-start(bf16[32,24,384]{2,1,0:T(8,128)(2,1)} %bitcast.37), calls=%async_computation | async-start | bytes 1179648 | tf_op jit(solution)/shard_map/all_to_all | solution.py:507
  24.2 0.9 copy-start.2
  25.1 0.6 copy-start.9
  30.5 22.7 %all-to-all-start.1 = ((bf16[8,592,128]{2,1,0:T(8,128)(2,1)}), bf16[8,592,128]{2,1,0:T(8,128)(2,1)S(1)}, u32[]{:S(2)}, u32[]{:S(2)}) async-start(bf16[8,592,128]{2,1,0:T(8,128)(2,1)} %get-tuple-element.20), calls=%async_computation.1 | async-start | bytes 2424832 | tf_op jit(solution)/shard_map/all_to_all | solution.py:528
  34.1 16.1 %collective-permute-start = (bf16[8,4,24,384]{3,2,1,0:T(8,128)(2,1)S(1)}, bf16[8,4,24,384]{3,2,1,0:T(8,128)(2,1)S(1)}, u32[]{:S(2)}, u32[]{:S(2)}) collective-permute-start(bf16[8,4,24,384]{3,2,1,0:T(8,128)(2,1)S(1)} %bitcast.30), channel_id=1, source_target_pairs={{0,4},{4,8},{8,12},{12,0},{1,5},{5,9},{9,13},{13,1},{2,6},{6,10},{... | collective-permute-start | bytes 1769480 | tf_op jit(solution)/shard_map/ppermute | solution.py:469
  35.4 14.8 %collective-permute-start.1 = (bf16[8,4,24,384]{3,2,1,0:T(8,128)(2,1)S(1)}, bf16[8,4,24,384]{3,2,1,0:T(8,128)(2,1)S(1)}, u32[]{:S(2)}, u32[]{:S(2)}) collective-permute-start(bf16[8,4,24,384]{3,2,1,0:T(8,128)(2,1)S(1)} %bitcast.31), channel_id=1, source_target_pairs={{0,12},{4,0},{8,4},{12,8},{1,13},{5,1},{9,5},{13,9},{2,14},{6,2},{... | collective-permute-start | bytes 1769480 | tf_op jit(solution)/shard_map/ppermute | solution.py:469
  53.2 4.2 %collective-permute-start.2 = (bf16[8,592,128]{2,1,0:T(8,128)(2,1)S(1)}, bf16[8,592,128]{2,1,0:T(8,128)(2,1)S(1)}, u32[]{:S(2)}, u32[]{:S(2)}) collective-permute-start(bf16[8,592,128]{2,1,0:T(8,128)(2,1)S(1)} %all-to-all-done.1.own_ref), channel_id=1, source_target_pairs={{0,1},{1,0},{2,3},{3,2},{4,5},{5,4},{6,7},{7,6},{8,9},{9,8},{10,11... | collective-permute-start | bytes 3637256 | tf_op jit(solution)/shard_map/ppermute | solution.py:465
  54.2 16.0 %collective-permute-start.3 = (bf16[8,2,24,384]{3,2,1,0:T(8,128)(2,1)S(1)}, bf16[8,2,24,384]{3,2,1,0:T(8,128)(2,1)S(1)}, u32[]{:S(2)}, u32[]{:S(2)}) collective-permute-start(bf16[8,2,24,384]{3,2,1,0:T(8,128)(2,1)S(1)} %slice.18), channel_id=1, source_target_pairs={{0,4},{4,8},{8,12},{12,0},{1,5},{5,9},{9,13},{13,1},{2,6},{6,10},{... | collective-permute-start | bytes 884744 | tf_op jit(solution)/shard_map/ppermute | solution.py:469
  55.6 14.6 %collective-permute-start.4 = (bf16[8,2,24,384]{3,2,1,0:T(8,128)(2,1)S(1)}, bf16[8,2,24,384]{3,2,1,0:T(8,128)(2,1)S(1)}, u32[]{:S(2)}, u32[]{:S(2)}) collective-permute-start(bf16[8,2,24,384]{3,2,1,0:T(8,128)(2,1)S(1)} %slice.19), channel_id=1, source_target_pairs={{0,12},{4,0},{8,4},{12,8},{1,13},{5,1},{9,5},{13,9},{2,14},{6,2},{... | collective-permute-start | bytes 884744 | tf_op jit(solution)/shard_map/ppermute | solution.py:469
  70.3 11.3 %copy-start.14 = (bf16[256,32]{0,1:T(8,128)(2,1)S(1)}, bf16[256,32]{0,1:T(8,128)(2,1)}, u32[]{:S(2)}) copy-start(bf16[256,32]{0,1:T(8,128)(2,1)} %param.27) | copy-start | bytes 49156
  70.3 11.5 %copy-start.15 = (bf16[256,32]{0,1:T(8,128)(2,1)S(1)}, bf16[256,32]{0,1:T(8,128)(2,1)}, u32[]{:S(2)}) copy-start(bf16[256,32]{0,1:T(8,128)(2,1)} %param.28) | copy-start | bytes 49156
  77.5 12.6 %copy-start.3 = (f32[8,192,128]{2,1,0:T(8,128)S(1)}, f32[8,192,128]{2,1,0:T(8,128)}, u32[]{:S(2)}) copy-start(f32[8,192,128]{2,1,0:T(8,128)} %copy-done.2) | copy-start | bytes 2359300
  77.5 12.6 %copy-start.5 = (bf16[256,256]{1,0:T(8,128)(2,1)S(1)}, bf16[256,256]{1,0:T(8,128)(2,1)}, u32[]{:S(2)}) copy-start(bf16[256,256]{1,0:T(8,128)(2,1)} %wf_ref.1) | copy-start | bytes 393220
  77.5 12.6 %copy-start.7 = (bf16[192,192]{1,0:T(8,128)(2,1)S(1)}, bf16[192,192]{1,0:T(8,128)(2,1)}, u32[]{:S(2)}) copy-start(bf16[192,192]{1,0:T(8,128)(2,1)} %constant.46.clone.pinv_ref) | copy-start | bytes 221188
  77.5 12.6 %copy-start.10 = (f32[256]{0:T(256)S(1)}, f32[256]{0:T(256)}, u32[]{:S(2)}) copy-start(f32[256]{0:T(256)} %param.26) | copy-start | bytes 3076
  77.5 12.6 %all-to-all-start.2 = ((bf16[16,96,128]{2,1,0:T(8,128)(2,1)}), bf16[16,96,128]{2,1,0:T(8,128)(2,1)S(1)}, u32[]{:S(2)}, u32[]{:S(2)}) async-start(bf16[16,96,128]{2,1,0:T(8,128)(2,1)} %bitcast.12), calls=%async_computation.2 | async-start | bytes 786432 | tf_op jit(solution)/shard_map/all_to_all | solution.py:533
  90.1 22.2 %copy-start.13 = (bf16[1024,128]{1,0:T(8,128)(2,1)S(1)}, bf16[1024,128]{1,0:T(8,128)(2,1)}, u32[]{:S(2)}) copy-start(bf16[1024,128]{1,0:T(8,128)(2,1)} %param.29) | copy-start | bytes 786436
  93.4 11.3 %all-to-all-start.3 = ((bf16[8,192,128]{2,1,0:T(8,128)(2,1)}), bf16[8,192,128]{2,1,0:T(8,128)(2,1)S(1)}, u32[]{:S(2)}, u32[]{:S(2)}) async-start(bf16[8,192,128]{2,1,0:T(8,128)(2,1)} %get-tuple-element.30), calls=%async_computation.3 | async-start | bytes 786432 | tf_op jit(solution)/shard_map/all_to_all | solution.py:547
  96.9 10.6 %collective-permute-start.6 = (bf16[192,128]{1,0:T(8,128)(2,1)S(1)}, bf16[192,128]{1,0:T(8,128)(2,1)S(1)}, u32[]{:S(2)}, u32[]{:S(2)}) collective-permute-start(bf16[192,128]{1,0:T(8,128)(2,1)S(1)} %get-tuple-element.31), channel_id=1, source_target_pairs={{0,0},{2,16},{4,32},{6,48},{8,64},{10,80},{12,96},{14,112},{16,2},... | collective-permute-start | bytes 147464 | tf_op jit(solution)/shard_map/ppermute | solution.py:479
  104.7 8.5 %collective-permute-start.5 = (bf16[8,192,128]{2,1,0:T(8,128)(2,1)S(1)}, bf16[8,192,128]{2,1,0:T(8,128)(2,1)S(1)}, u32[]{:S(2)}, u32[]{:S(2)}) collective-permute-start(bf16[8,192,128]{2,1,0:T(8,128)(2,1)S(1)} %all-to-all-done.3.lo_ref), channel_id=1, source_target_pairs={{0,1},{1,0},{2,3},{3,2},{4,5},{5,4},{6,7},{7,6},{8,9},{9,8},{10,11... | collective-permute-start | bytes 1179656 | tf_op jit(solution)/shard_map/ppermute | solution.py:465
  108.3 12.6 %all-to-all-start.4 = ((bf16[16,96,128]{2,1,0:T(8,128)(2,1)}), bf16[16,96,128]{2,1,0:T(8,128)(2,1)S(1)}, u32[]{:S(2)}, u32[]{:S(2)}) async-start(bf16[16,96,128]{2,1,0:T(8,128)(2,1)} %bitcast.19), calls=%async_computation.4 | async-start | bytes 786432 | tf_op jit(solution)/shard_map/all_to_all | solution.py:549
  113.8 1.2 copy-start
  120.9 0.8 copy-start.12
